TPU v7x, 32 devices: a whole 2x2x4 slice. The times are simulated.
32 devices in a mesh: group: 4 (over y, x), shard: 8 (over z, core).
Axes of the slice: x: 2, y: 2, z: 4, core: 2. Of those that a mesh axis runs over, the one named last changes fastest.
Arguments:
- entity_rows: float32 [32768, 200], P(('group', 'shard')), may hold values from -4 to 4
- entity_state: float32 [32768], P(('group', 'shard')), may hold values from 0.5 to 4
- relation_rows: float32 [1387, 200], replicated, may hold values from -6 to 6
- relation_state: float32 [1387], replicated, may hold values from 16 to 160
- conv_weight: bfloat16 [32, 3, 3], replicated, may hold values from -2 to 2
- conv_bias: float32 [32], replicated, may hold values from -3 to 3
- fc_weight: bfloat16 [10368, 200], replicated, may hold values from -0.0625 to 0.0625
- fc_bias: float32 [200], replicated, may hold values from -3 to 3
- head_ids: int32 [2, 4096], P(None, ('group', 'shard')), may hold values from 0 to 1023
- rel_ids: int32 [2, 4096], P(None, ('group', 'shard')), may hold values from 0 to 1386
- tail_ids: int32 [2, 4096], P(None, ('group', 'shard')), may hold values from 0 to 1023
- neg_ids: int32 [2, 1024], P(None, ('group', 'shard')), may hold values from 0 to 1023
Outputs:
- new_entity_rows: float32 [32768, 200], P(('group', 'shard'))
- new_entity_state: float32 [32768], P(('group', 'shard'))
- new_relation_rows: float32 [1387, 200], replicated
- new_relation_state: float32 [1387], replicated
All inputs are finite; a program needn't handle non-finite values.
Results may differ from a plain program's by a relative error of at most 0.002.
Values may be sent and summed in bfloat16 or wider, within the bound.
No kernel may reach another device: no remote copies, remote signals or barrier semaphores. Data moves between devices by JAX's collectives and lax.ppermute only.
A program may use at most 128 MiB of HBM per device.

v0:
```python
import jax
import jax.numpy as jnp
from jax import lax
from jax.sharding import PartitionSpec as P

EMB_H = 10
EMB_W = 20
D = 200
FILTERS = 32
FLAT = 10368
REL = 1387
ROUNDS = 2


negative_weight = 0.03125
learn_rate = 0.5


def from_partner(block, axis, bit):
    count = lax.axis_size(axis)
    route = []
    for low in range(count):
        high = low | 1 << bit
        if high != low and high < count:
            route += [(low, high), (high, low)]
    return lax.ppermute(block, axis, route)


def silu_slope(values):
    sigma = jax.nn.sigmoid(values)
    return sigma * (1.0 + values * (1.0 - sigma))


def adagrad(rows, state, gradient):
    state = state + jnp.mean(gradient * gradient, axis=1)
    rows = rows - learn_rate * gradient / jnp.sqrt(state)[:, None]
    return (rows, state)


def local_pass(head_rows, rel_rows, tail_rows, negset, conv_weight, conv_bias, fc_weight, fc_bias):
    number = head_rows.shape[0]
    picture = jnp.concatenate(
        [head_rows.reshape(number, EMB_H, EMB_W), rel_rows.reshape(number, EMB_H, EMB_W)], axis=1
    )
    picture = jnp.transpose(picture, (1, 2, 0))
    height = picture.shape[0] - 2
    across = picture.shape[1] - 2
    patches = jnp.stack(
        [
            picture[row_off : row_off + height, col_off : col_off + across]
            for row_off in range(3)
            for col_off in range(3)
        ]
    )
    filters = conv_weight.reshape(FILTERS, 9)
    pre1 = (
        jnp.einsum("fk,kijt->fijt", filters, patches, preferred_element_type=jnp.float32)
        + conv_bias[:, None, None, None]
    )
    act = jax.nn.silu(pre1).astype(jnp.bfloat16).reshape(FLAT, number)
    pre2 = (
        lax.dot_general(
            fc_weight, act, (((0,), (0,)), ((), ())), preferred_element_type=jnp.float32
        )
        + fc_bias[:, None]
    )
    query = jax.nn.silu(pre2).astype(jnp.bfloat16)
    tail_cols = tail_rows.T.astype(jnp.float32)
    pos_score = jnp.sum(query.astype(jnp.float32) * tail_cols, axis=0)
    neg_score = jnp.dot(negset, query, preferred_element_type=jnp.float32)
    pos_grad = -jax.nn.sigmoid(-pos_score)
    neg_grad = (negative_weight * jax.nn.sigmoid(neg_score)).astype(jnp.bfloat16)
    query_grad = pos_grad[None, :] * tail_cols + lax.dot_general(
        negset, neg_grad, (((0,), (0,)), ((), ())), preferred_element_type=jnp.float32
    )
    pre2_grad = (query_grad * silu_slope(pre2)).astype(jnp.bfloat16)
    act_grad = jnp.dot(fc_weight, pre2_grad, preferred_element_type=jnp.float32)
    pre1_grad = (act_grad.reshape(pre1.shape) * silu_slope(pre1)).astype(jnp.bfloat16)
    spread = jnp.einsum("fk,fijt->kijt", filters, pre1_grad, preferred_element_type=jnp.float32)
    picture_grad = jnp.zeros((height + 2, across + 2, number), jnp.float32)
    for offset in range(9):
        row_off, col_off = divmod(offset, 3)
        picture_grad = picture_grad + jnp.pad(
            spread[offset], ((row_off, 2 - row_off), (col_off, 2 - col_off), (0, 0))
        )
    head_grad = jnp.transpose(picture_grad[:EMB_H], (2, 0, 1)).reshape(number, D)
    relation_grad = jnp.transpose(picture_grad[EMB_H:], (2, 0, 1)).reshape(number, D)
    tail_grad = (pos_grad[None, :] * query.astype(jnp.float32)).T
    return (head_grad, relation_grad, tail_grad, neg_grad, query)


def shards(
    entity_rows,
    entity_state,
    relation_rows,
    relation_state,
    conv_weight,
    conv_bias,
    fc_weight,
    fc_bias,
    head_ids,
    rel_ids,
    tail_ids,
    neg_ids,
):
    ent_rows_dev = entity_rows.shape[0]
    tri_rows = head_ids.shape[1]
    for round_index in range(ROUNDS):
        ent_bf = entity_rows.astype(jnp.bfloat16)
        rel_bf = relation_rows.astype(jnp.bfloat16)
        heads = head_ids[round_index]
        relations = rel_ids[round_index]
        tails = tail_ids[round_index]
        negatives = neg_ids[round_index]
        wanted = jnp.concatenate([tails, negatives])
        requested = from_partner(wanted, "group", round_index)
        answered = from_partner(ent_bf[requested], "group", round_index)
        tail_rows = answered[:tri_rows]
        own_negative = answered[tri_rows:]
        negset = lax.all_gather(own_negative, "shard", axis=0, tiled=True)
        head_grad, relation_grad, tail_grad, neg_grad, query = local_pass(
            ent_bf[heads],
            rel_bf[relations],
            tail_rows,
            negset,
            conv_weight,
            conv_bias,
            fc_weight,
            fc_bias,
        )
        my_share = lax.psum_scatter(
            lax.dot_general(
                neg_grad, query, (((1,), (1,)), ((), ())), preferred_element_type=jnp.float32
            ),
            "shard",
            scatter_dimension=0,
            tiled=True,
        )
        gradient = jax.ops.segment_sum(head_grad, heads, num_segments=ent_rows_dev)
        returned = from_partner(jnp.concatenate([tail_grad, my_share]), "group", round_index)
        gradient = gradient + jax.ops.segment_sum(returned, requested, num_segments=ent_rows_dev)
        rel_part = jax.ops.segment_sum(relation_grad, relations, num_segments=REL)
        entity_rows, entity_state = adagrad(entity_rows, entity_state, gradient)
        rel_total = lax.psum(rel_part, ("group", "shard"))
        relation_rows, relation_state = adagrad(relation_rows, relation_state, rel_total)
    return (entity_rows, entity_state, relation_rows, relation_state)


def solution(mesh):
    in_specs = (
        P(("group", "shard"), None),
        P(("group", "shard")),
        P(),
        P(),
        P(),
        P(),
        P(),
        P(),
        P(None, ("group", "shard")),
        P(None, ("group", "shard")),
        P(None, ("group", "shard")),
        P(None, ("group", "shard")),
    )
    out_specs = (P(("group", "shard"), None), P(("group", "shard")), P(), P())
    return jax.shard_map(shards, mesh=mesh, in_specs=in_specs, out_specs=out_specs, check_vma=False)
```

profile of v0, /device:TPU:0, one launch (start us, length us, event | category | flops | bytes accessed | tf_op | source)
XLA Modules:
  0.0 489.9 jit_solution(13643787321477718561)
XLA Ops:
  10.1 3.0 collective-permute-start.3
  29.5 4.3 stack.69
  33.8 4.8 fusion.11
  40.2 4.6 copy.703
  44.9 5.5 %reshape.181 = bf16[10368,128]{1,0:T(8,128)(2,1)} reshape(bf16[32,18,18,128]{3,2,1,0:T(8,128)(2,1)} %copy.703) | data formatting | bytes 5308416 | tf_op jit(solution)/shard_map/reshape | solution.py:60
  53.3 2.9 collective-permute-done.1
  56.3 14.3 %all_gather.6 = bf16[256,200]{1,0:T(8,128)(2,1)S(1)} all-gather(bf16[32,200]{1,0:T(8,128)(2,1)S(1)} %copy.705), channel_id=1, replica_groups=mesh['group'=4,'shard'=8] {'shard'}, dimensions={0}, use_global_device_ids=true | all-gather | bytes 115200 | tf_op jit(solution)/shard_map/all_gather | solution.py:120
  70.5 4.3 fusion.54
  76.2 5.6 %convolution_bitcast_fusion.1 = f32[10368,128]{0,1:T(8,128)} fusion(bf16[10368,200]{0,1:T(8,128)(2,1)} %param.18, f32[128,200]{0,1:T(8,128)S(1)} %get-tuple-element.118, f32[128]{0:T(128)S(1)} %divide_negate_fusion.1, bf16[160,200]{0,1:T(8,128)(2,1)S(1)} %collective-permute-done.1, bf16[256,200]{1,0:T(8,128)(2,1)S(1)} %all_gather.6, ...), kind=kOutput, calls=%fused_computation.11 | convolution fusion | flops 544256000 | bytes 9806336 | tf_op jit(solution)/shard_map/dot_general | solution.py:77
  81.9 6.0 %copy.706 = f32[10368,128]{1,0:T(8,128)} copy(f32[10368,128]{0,1:T(8,128)} %convolution_bitcast_fusion.1) | data formatting | bytes 10616832 | tf_op jit(solution)/shard_map/dot_general | solution.py:77
  87.9 6.7 %reshape.182 = f32[32,18,18,128]{3,2,1,0:T(8,128)} reshape(f32[10368,128]{1,0:T(8,128)} %copy.706) | data formatting | bytes 10616832 | tf_op jit(solution)/shard_map/reshape | solution.py:78
  94.6 5.9 %fusion.23 = f32[9,18,18,128]{3,0,2,1:T(8,128)S(1)} fusion(f32[32,18,18,128]{3,2,1,0:T(8,128)} %reshape.182, f32[18,18,128,32]{2,3,1,0:T(8,128)} %get-tuple-element.117, f32[32]{0:T(128)S(1)} %copy-done.17, bf16[32,9,1,1]{0,1,2,3:T(8,128)(2,1)S(1)} %reshape.275), kind=kOutput, calls=%fused_computation.37 | convolution fusion | flops 37158912 | bytes 12110528 | tf_op jit(solution)/shard_map/fk,fijt->kijt/dot_general | solution.py:79
  102.0 3.6 reduce-scatter.7.cloned.1.call-done
  113.2 3.0 scatter_custom_fusion
  121.2 2.6 gather_fusion.5
  129.9 109.6 %all-reduce.21.cloned.1.call-done = f32[1387,200]{1,0:T(8,128)} async-done(((f32[1387,200]{1,0:T(8,128)}), f32[1387,200]{1,0:T(8,128)}) %all-reduce.21.cloned.1.call-update) | async-done | bytes 1109616 | tf_op jit(solution)/shard_map/psum | solution.py:144
  243.6 2.6 gather_fusion.4
  257.3 8.6 %stack.79 = bf16[9,18,18,128]{3,0,2,1:T(8,128)(2,1)} concatenate(bf16[1,18,18,128]{3,0,2,1:T(2,128)(2,1)} %copy.723, bf16[1,18,18,128]{3,0,2,1:T(2,128)(2,1)} %copy.724, bf16[1,18,18,128]{3,0,2,1:T(2,128)(2,1)} %copy.725, bf16[1,18,18,128]{3,0,2,1:T(2,128)(2,1)} %copy.726, bf16[1,18,18,128]{3,0,2,1:T(2,128)(2,1)} %copy.727, bf16[1,18,18,128]{3,0,2,1:T(2,128)(2,1)} %copy.728, ...), dimensions={0} | concatenate | bytes 1492992 | tf_op jit(solution)/shard_map/stack | solution.py:48
  265.9 5.2 %fusion.3 = (bf16[32,18,18,128]{3,0,2,1:T(8,128)(2,1)S(1)}, f32[18,18,128,32]{2,3,1,0:T(8,128)}) fusion(f32[32]{0:T(128)S(1)} %copy-done.18, bf16[9,18,18,128]{3,0,2,1:T(8,128)(2,1)} %stack.79, bf16[32,9,1,1]{0,1,2,3:T(8,128)(2,1)S(1)} %reshape.275), kind=kOutput, calls=%fused_computation.18 | convolution fusion | flops 31850496 | bytes 8709824 | tf_op jit(solution)/shard_map/fk,kijt->fijt/dot_general | solution.py:57
  271.1 2.9 copy.732
  274.0 5.5 %reshape.187 = bf16[10368,128]{1,0:T(8,128)(2,1)} reshape(bf16[32,18,18,128]{3,2,1,0:T(8,128)(2,1)} %copy.732) | data formatting | bytes 5308416 | tf_op jit(solution)/shard_map/reshape | solution.py:60
  281.8 14.0 %all_gather.7 = bf16[256,200]{1,0:T(8,128)(2,1)S(1)} all-gather(bf16[32,200]{1,0:T(8,128)(2,1)S(1)} %copy.734), channel_id=1, replica_groups=mesh['group'=4,'shard'=8] {'shard'}, dimensions={0}, use_global_device_ids=true | all-gather | bytes 115200 | tf_op jit(solution)/shard_map/all_gather | solution.py:120
  295.7 5.0 %fusion.44 = (f32[128]{0:T(128)S(1)}, bf16[200,128]{1,0:T(8,128)(2,1)S(1)}, f32[128,200]{0,1:T(8,128)}) fusion(bf16[160,200]{0,1:T(8,128)(2,1)} %collective-permute-done.4, f32[200]{0:T(256)} %param.19, bf16[10368,128]{1,0:T(8,128)(2,1)} %reshape.187, bf16[10368,200]{0,1:T(8,128)(2,1)} %param.18), kind=kOutput, calls=%fused_computation.118 | convolution fusion | flops 531097472 | bytes 7007520 | tf_op jit(solution)/shard_map/dot_general | solution.py:62
  302.8 5.8 %convolution_bitcast_fusion = f32[10368,128]{0,1:T(8,128)} fusion(bf16[10368,200]{0,1:T(8,128)(2,1)} %param.18, f32[128,200]{0,1:T(8,128)} %get-tuple-element.121, f32[128]{0:T(128)S(1)} %divide_negate_fusion, bf16[160,200]{0,1:T(8,128)(2,1)} %collective-permute-done.4, bf16[256,200]{1,0:T(8,128)(2,1)} %copy-done.3, bf16[256,128]{1,0:T(8,128)(2,1)} %copy-done.4), kind=kOutput, calls=%fused_computation.10 | convolution fusion | flops 544256000 | bytes 9806336 | tf_op jit(solution)/shard_map/dot_general | solution.py:77
  308.6 6.0 %copy.735 = f32[10368,128]{1,0:T(8,128)} copy(f32[10368,128]{0,1:T(8,128)} %convolution_bitcast_fusion) | data formatting | bytes 10616832 | tf_op jit(solution)/shard_map/dot_general | solution.py:77
  314.6 6.7 %reshape.188 = f32[32,18,18,128]{3,2,1,0:T(8,128)} reshape(f32[10368,128]{1,0:T(8,128)} %copy.735) | data formatting | bytes 10616832 | tf_op jit(solution)/shard_map/reshape | solution.py:78
  321.4 5.9 %fusion.20 = f32[9,18,18,128]{3,0,2,1:T(8,128)S(1)} fusion(f32[32,18,18,128]{3,2,1,0:T(8,128)} %reshape.188, f32[18,18,128,32]{2,3,1,0:T(8,128)} %get-tuple-element.120, f32[32]{0:T(128)S(1)} %copy-done.19, bf16[32,9,1,1]{0,1,2,3:T(8,128)(2,1)S(1)} %copy-done.14), kind=kOutput, calls=%fused_computation.36 | convolution fusion | flops 37158912 | bytes 12110528 | tf_op jit(solution)/shard_map/fk,fijt->kijt/dot_general | solution.py:79
  343.0 2.8 scatter_custom_fusion.3
  349.4 3.5 scatter_custom_fusion.2
  360.8 113.7 %all-reduce.23.cloned.1.call-done = f32[1387,200]{1,0:T(8,128)} async-done(((f32[1387,200]{1,0:T(8,128)}), f32[1387,200]{1,0:T(8,128)}) %all-reduce.23.cloned.1.call-update) | async-done | bytes 1109616 | tf_op jit(solution)/shard_map/psum | solution.py:144
  476.8 2.9 divide_subtract_fusion
  479.7 2.8 copy.749
  (181 shorter events, 93.2 us)
Async XLA Ops:
  8.0 14.7 %copy-start.2 = (f32[1024,200]{0,1:T(8,128)S(1)}, f32[1024,200]{0,1:T(8,128)}, u32[]{:S(2)}) copy-start(f32[1024,200]{0,1:T(8,128)} %param.12) | copy-start | bytes 2457604
  8.0 97.6 %reduce-scatter.7.cloned.1.call-start = ((), (), s32[]{:S(2)}) async-start(), calls=%async_computation.4 | async-start | bytes 294912
  10.1 41.9 %collective-permute-start.3 = (s32[160]{0:T(256)}, s32[160]{0:T(256)S(1)}, u32[]{:S(2)}, u32[]{:S(2)}) collective-permute-start(s32[160]{0:T(256)} %pad_add_fusion.3), channel_id=1, source_target_pairs={{0,16},{16,0},{8,24},{24,8},{1,17},{17,1},{9,25},{25,9},{2,18},{18... | collective-permute-start | bytes 1928 | tf_op jit(solution)/shard_map/ppermute | solution.py:26
  13.7 36.7 %collective-permute-start = (s32[160]{0:T(256)}, s32[160]{0:T(256)S(1)}, u32[]{:S(2)}, u32[]{:S(2)}) collective-permute-start(s32[160]{0:T(256)} %pad_add_fusion.2), channel_id=1, source_target_pairs={{0,8},{8,0},{16,24},{24,16},{1,9},{9,1},{17,25},{25,17},{2,10},{10... | collective-permute-start | bytes 1928 | tf_op jit(solution)/shard_map/ppermute | solution.py:26
  20.1 245.8 %copy-start.13 = (bf16[32,9,1,1]{0,1,2,3:T(8,128)(2,1)}, bf16[32,9,1,1]{0,1,2,3:T(8,128)(2,1)S(1)}, u32[]{:S(2)}) copy-start(bf16[32,9,1,1]{0,1,2,3:T(8,128)(2,1)S(1)} %reshape.275) | copy-start | bytes 1732
  23.1 10.6 %copy-start.16 = (f32[32]{0:T(128)S(1)}, f32[32]{0:T(128)}, u32[]{:S(2)}) copy-start(f32[32]{0:T(128)} %param.17) | copy-start | bytes 388
  44.9 7.2 %copy-start.15 = (s32[128,1]{0,1:T(1,128)S(1)}, s32[128,1]{0,1:T(1,128)}, u32[]{:S(2)}) copy-start(s32[128,1]{0,1:T(1,128)} %get-tuple-element.111) | copy-start | bytes 1540
  44.9 25.6 %copy-start.12 = (f32[200]{0:T(256)S(1)}, f32[200]{0:T(256)}, u32[]{:S(2)}) copy-start(f32[200]{0:T(256)} %param.19) | copy-start | bytes 2404
  51.5 4.7 collective-permute-start.1
  76.0 163.5 %all-reduce.21.cloned.1.call-start = ((), (), s32[]{:S(2)}) async-start(), calls=%async_computation.2 | async-start | bytes 2850816 | tf_op jit(solution)/shard_map/psum | solution.py:144
  87.9 6.7 %copy-start.17 = (f32[32]{0:T(128)S(1)}, f32[32]{0:T(128)}, u32[]{:S(2)}) copy-start(f32[32]{0:T(128)} %param.17) | copy-start | bytes 388
  102.0 15.1 %copy-start.11 = (f32[1024]{0:T(1024)S(1)}, f32[1024]{0:T(1024)}, u32[]{:S(2)}) copy-start(f32[1024]{0:T(1024)} %param.13) | copy-start | bytes 12292
  106.5 5.8 %collective-permute-start.2 = (f32[160,200]{0,1:T(8,128)S(1)}, f32[160,200]{0,1:T(8,128)S(1)}, u32[]{:S(2)}, u32[]{:S(2)}) collective-permute-start(f32[160,200]{0,1:T(8,128)S(1)} %pad_maximum_fusion.2), channel_id=1, source_target_pairs={{0,8},{8,0},{16,24},{24,16},{1,9},{9,1},{17,25},{25,17},{2,10},{10... | collective-permute-start | bytes 384008 | tf_op jit(solution)/shard_map/ppermute | solution.py:26
  110.7 221.3 %reduce-scatter.9.cloned.1.call-start = ((), (), s32[]{:S(2)}) async-start(), calls=%async_computation.5 | async-start | bytes 294912
  112.4 128.7 %copy-start.9 = (f32[1387]{0:T(1024)S(1)}, f32[1387]{0:T(1024)}, u32[]{:S(2)}) copy-start(f32[1387]{0:T(1024)} %param.15) | copy-start | bytes 16648
  116.5 0.6 copy-start.5
  117.1 0.6 copy-start.7
  128.4 151.1 %collective-permute-start.4 = (bf16[160,200]{0,1:T(8,128)(2,1)}, bf16[160,200]{0,1:T(8,128)(2,1)}, u32[]{:S(2)}, u32[]{:S(2)}) collective-permute-start(bf16[160,200]{0,1:T(8,128)(2,1)} %copy.733), channel_id=1, source_target_pairs={{0,16},{16,0},{8,24},{24,8},{1,17},{17,1},{9,25},{25,9},{2,18},{18... | collective-permute-start | bytes 192008 | tf_op jit(solution)/shard_map/ppermute | solution.py:26
  243.6 22.3 %copy-start.18 = (f32[32]{0:T(128)S(1)}, f32[32]{0:T(128)}, u32[]{:S(2)}) copy-start(f32[32]{0:T(128)} %param.17) | copy-start | bytes 388
  295.7 5.0 %copy-start.3 = (bf16[256,200]{1,0:T(8,128)(2,1)}, bf16[256,200]{1,0:T(8,128)(2,1)S(1)}, u32[]{:S(2)}) copy-start(bf16[256,200]{1,0:T(8,128)(2,1)S(1)} %all_gather.7) | copy-start | bytes 307204
  300.9 0.6 copy-start.4
  302.5 172.0 %all-reduce.23.cloned.1.call-start = ((), (), s32[]{:S(2)}) async-start(), calls=%async_computation.3 | async-start | bytes 2850816 | tf_op jit(solution)/shard_map/psum | solution.py:144
  314.6 6.7 %copy-start.14 = (bf16[32,9,1,1]{0,1,2,3:T(8,128)(2,1)S(1)}, bf16[32,9,1,1]{0,1,2,3:T(8,128)(2,1)}, u32[]{:S(2)}) copy-start(bf16[32,9,1,1]{0,1,2,3:T(8,128)(2,1)} %copy-done.13) | copy-start | bytes 1732
  314.6 6.7 %copy-start.19 = (f32[32]{0:T(128)S(1)}, f32[32]{0:T(128)}, u32[]{:S(2)}) copy-start(f32[32]{0:T(128)} %param.17) | copy-start | bytes 388
  327.3 2.1 copy-start.1
  329.5 24.9 %copy-start.6 = (f32[1024]{0:T(1024)S(1)}, f32[1024]{0:T(1024)}, u32[]{:S(2)}) copy-start(f32[1024]{0:T(1024)} %copy-done.5) | copy-start | bytes 12292
  329.5 26.2 %copy-start.8 = (f32[1024]{0:T(1024)S(1)}, f32[1024]{0:T(1024)}, u32[]{:S(2)}) copy-start(f32[1024]{0:T(1024)} %copy-done.7) | copy-start | bytes 12292
  335.2 10.7 %collective-permute-start.5 = (f32[160,200]{0,1:T(8,128)}, f32[160,200]{0,1:T(8,128)}, u32[]{:S(2)}, u32[]{:S(2)}) collective-permute-start(f32[160,200]{0,1:T(8,128)} %pad_maximum_fusion.3), channel_id=1, source_target_pairs={{0,16},{16,0},{8,24},{24,8},{1,17},{17,1},{9,25},{25,9},{2,18},{18... | collective-permute-start | bytes 384008 | tf_op jit(solution)/shard_map/ppermute | solution.py:26
  352.9 123.2 %copy-start.10 = (f32[1387]{0:T(1024)S(1)}, f32[1387]{0:T(1024)}, u32[]{:S(2)}) copy-start(f32[1387]{0:T(1024)} %param.15) | copy-start | bytes 16648
  358.2 118.5 %copy-start = (f32[1387,200]{1,0:T(8,128)S(1)}, f32[1387,200]{1,0:T(8,128)}, u32[]{:S(2)}) copy-start(f32[1387,200]{1,0:T(8,128)} %all-reduce.21.cloned.1.call-done) | copy-start | bytes 3328804
Sparse Core Ops, SparseCore 0:
  76.1 29.4 reduce-scatter.6
  302.6 29.3 reduce-scatter.8
Sparse Core Ops, SparseCore 1:
  110.8 128.6 all-reduce.20
  345.9 128.6 all-reduce.22
where the time goes:
time: 493 us; the launch traced here: 490 us
  waiting for transfers between devices  233 us (47%)
  local copies, waits for them, and re-layouts  118 us (24%)
  matrix products  44.8 us (9%)
  other arithmetic  39 us (8%)
  blocking collectives  28.2 us (6%)
  between operations  16.1 us (3%)
  starting transfers between devices  10.2 us (2%)
    psum x2, waiting for transfers between devices, shards(): rel_total = lax.psum(rel_part, ('group', 'shard'))  223 us
    all_gather x2, blocking collectives, shards(): negset = lax.all_gather(own_negative, 'shard', axis=0, tiled=True)  28.2 us
    another operation x22, local copies, waits for them, and re-layouts, local_pass(): jnp.stack([picture[row_off:row_off + height, col_off:col_off + across] fo...  25.4 us
    reshape x2, local copies, waits for them, and re-layouts, local_pass(): act_grad.reshape(pre1.shape) * silu_slope(pre1)  13.5 us
    dot_general x2, local copies, waits for them, and re-layouts, local_pass(): act_grad = jnp.dot(fc_weight, pre2_grad, preferred_element_type=jnp.float32)  12.1 us
    dot_general x2, matrix products, local_pass(): jnp.einsum('fk,fijt->kijt', filters, pre1_grad, preferred_element_type=jn...  11.9 us
    unnamed x64, local copies, waits for them, and re-layouts  11.8 us
    dot_general x2, matrix products, local_pass(): act_grad = jnp.dot(fc_weight, pre2_grad, preferred_element_type=jnp.float32)  11.5 us
  transfers between devices with their start and end apart: 10, of which 6 were waited for; matrix products, arithmetic and copies ran while one was open for 35% of the time, Pallas kernels for 0%

commit v1 on v0

v1 whole, which is shorter than its diff:
```python
import functools

import jax
import jax.numpy as jnp
from jax import lax
from jax.experimental import pallas as pl
from jax.experimental.pallas import tpu as pltpu
from jax.sharding import PartitionSpec as P

EMB_W = 20
D = 200
FILTERS = 32
PIXELS = 400
SIDE = 18
PAIRS = 9
WINDOW = 80
WIDE = 1152
PACK = 208
LANES = 128
ROUNDS = 2
SPLITS = ((0, 256), (256, 512), (512, 768), (768, 1024), (1024, 1152))

negative_weight = 0.03125
learn_rate = 0.5

f32 = jnp.float32
bf16 = jnp.bfloat16
BOTH = ("group", "shard")
PARAMS = pltpu.CompilerParams(vmem_limit_bytes=48 * 1024 * 1024)
VMEM = pl.BlockSpec(memory_space=pltpu.VMEM)
SMEM = pl.BlockSpec(memory_space=pltpu.SMEM)


def sigmoid(values):
    return 0.5 * jnp.tanh(0.5 * values) + 0.5


def rows_nt(left, right):
    return lax.dot_general(left, right, (((1,), (1,)), ((), ())), preferred_element_type=f32)


def rows_tn(left, right):
    return lax.dot_general(left, right, (((0,), (0,)), ((), ())), preferred_element_type=f32)


def as_columns(row):
    return jnp.transpose(jnp.broadcast_to(row.astype(f32), (LANES, LANES)))


def one_hot_rows(ids_row, count):
    wide = as_columns(ids_row)
    lane = lax.broadcasted_iota(jnp.int32, (LANES, LANES), 1)
    parts = [
        jnp.where(wide == (lane + first).astype(f32), 1.0, 0.0).astype(bf16)
        for first in range(0, count, LANES)
    ]
    return jnp.concatenate(parts, axis=1)


def halves(values):
    high = values.astype(bf16)
    return high, (values - high.astype(f32)).astype(bf16)


def prepare_kernel(fc_ref, taps_ref, fc_out, band_out, band_t_out, left, right):
    rows = fc_ref.shape[0]
    step = rows // 16

    def widen(index, carry):
        at = pl.ds(pl.multiple_of(index * step, 8), step)
        block = fc_ref[at, :].astype(f32)
        left[at, :] = block[:, :LANES]
        right[at, : D - LANES] = block[:, LANES:]
        return carry

    lax.fori_loop(0, 16, widen, 0)
    spots = SIDE * SIDE

    def regroup(index, carry):
        low = left[pl.ds(index, FILTERS, stride=spots), :]
        high = right[pl.ds(index, FILTERS, stride=spots), :]
        at = pl.ds(pl.multiple_of(index * FILTERS, FILTERS), FILTERS)
        fc_out[at, :LANES] = low.astype(bf16)
        fc_out[at, LANES:] = high[:, : D - LANES].astype(bf16)
        return carry

    lax.fori_loop(0, spots, regroup, 0, unroll=4)
    group = lax.broadcasted_iota(jnp.int32, (WINDOW, WIDE), 1) >> 5
    lower = jnp.where(group >= SIDE, 1, 0)
    start = group + (EMB_W - SIDE) * lower
    gap = lax.broadcasted_iota(jnp.int32, (WINDOW, WIDE), 0) - start
    band = jnp.zeros((WINDOW, WIDE), f32)
    for row_off in range(3):
        for col_off in range(3):
            tap = row_off * 3 + col_off
            hit = gap == EMB_W * row_off + col_off
            band = jnp.where(hit, taps_ref[tap : tap + 1, :], band)
    band_out[...] = band.astype(bf16)
    band_t_out[...] = jnp.transpose(
        jnp.concatenate([band, jnp.zeros((LANES - WINDOW, WIDE), f32)], axis=0)
    ).astype(bf16)


def prepare(fc_weight, taps):
    rows = fc_weight.shape[0]
    return pl.pallas_call(
        prepare_kernel,
        out_shape=(
            jax.ShapeDtypeStruct((rows, D), bf16),
            jax.ShapeDtypeStruct((WINDOW, WIDE), bf16),
            jax.ShapeDtypeStruct((WIDE, LANES), bf16),
        ),
        in_specs=[VMEM] * 2,
        out_specs=[VMEM] * 3,
        scratch_shapes=[pltpu.VMEM((rows, LANES), f32), pltpu.VMEM((rows, LANES), f32)],
        compiler_params=PARAMS,
        name="prepare",
    )(fc_weight, taps)


def pass_kernel(
    ids_ref, ent_ref, rel_ref, tail_ref, neg_ref, band_ref, band_t_ref, bias_ref, fc_ref, fcb_ref,
    pack_out, head_out, tail_out, neg_out,
    picture, slopes, total,
):
    heads = ids_ref[0:1, :]
    relations = ids_ref[1:2, :]
    ent_bf = ent_ref[...].astype(bf16)
    rel_bf = rel_ref[...].astype(bf16)
    head_rows = jnp.dot(one_hot_rows(heads, ent_bf.shape[0]), ent_bf, preferred_element_type=f32)
    rel_rows = jnp.dot(one_hot_rows(relations, rel_bf.shape[0]), rel_bf, preferred_element_type=f32)
    picture[:D, :] = jnp.transpose(head_rows)
    picture[D:, :] = jnp.transpose(rel_rows)
    number = LANES

    def forward(pair, pre2):
        at = pl.ds(pl.multiple_of(pair * 2 * EMB_W, 8), WINDOW)
        window = jnp.transpose(picture[at, :]).astype(bf16)
        for first, last in SPLITS:
            pre1 = (
                jnp.dot(window, band_ref[:, first:last], preferred_element_type=f32)
                + bias_ref[:, first:last]
            )
            sigma = sigmoid(pre1)
            act = pre1 * sigma
            slopes[pair, :, first:last] = sigma + act * (1.0 - sigma)
            pre2 = pre2 + jnp.dot(
                act.astype(bf16), fc_ref[pair, first:last, :], preferred_element_type=f32
            )
        return pre2

    pre2 = lax.fori_loop(0, PAIRS, forward, jnp.zeros((number, D), f32)) + fcb_ref[...]
    sigma = sigmoid(pre2)
    value = pre2 * sigma
    slope2 = sigma + value * (1.0 - sigma)
    query = value.astype(bf16)
    query32 = query.astype(f32)
    tails = tail_ref[...].astype(f32)
    pos_score = jnp.sum(query32 * tails, axis=1, keepdims=True)
    pos_grad = -sigmoid(-pos_score)
    negset = neg_ref[...]
    neg_grad = (negative_weight * sigmoid(rows_nt(query, negset))).astype(bf16)
    query_grad = pos_grad * tails + jnp.dot(neg_grad, negset, preferred_element_type=f32)
    pre2_grad = (query_grad * slope2).astype(bf16)
    tail_out[...] = pos_grad * query32
    neg_out[...] = rows_tn(neg_grad, query)
    total[...] = jnp.zeros_like(total)

    def backward(pair, carry):
        part = jnp.zeros((number, LANES), f32)
        for first, last in SPLITS:
            act_grad = rows_nt(pre2_grad, fc_ref[pair, first:last, :])
            pre1_grad = (act_grad * slopes[pair, :, first:last]).astype(bf16)
            part = part + jnp.dot(
                pre1_grad, band_t_ref[first:last, :], preferred_element_type=f32
            )
        at = pl.ds(pl.multiple_of(pair * 2 * EMB_W, 8), WINDOW)
        total[at, :] = total[at, :] + jnp.transpose(part)[:WINDOW, :]
        return carry

    lax.fori_loop(0, PAIRS, backward, 0)
    head_out[...] = total[:D, :]
    high = relations >> 6
    low = relations - (high << 6)
    spare = lax.broadcasted_iota(jnp.int32, (PACK - D, number), 0)
    codes = jnp.where(spare == 0, high, jnp.where(spare == 1, low, 0)).astype(f32)
    pack_out[...] = jnp.concatenate([total[D:, :], codes], axis=0).astype(bf16)


def local_pass(ids, ent, rel, tails, negset, band, band_t, bias, fc, fc_bias):
    number = tails.shape[0]
    return pl.pallas_call(
        pass_kernel,
        out_shape=(
            jax.ShapeDtypeStruct((PACK, number), bf16),
            jax.ShapeDtypeStruct((D, number), f32),
            jax.ShapeDtypeStruct((number, D), f32),
            jax.ShapeDtypeStruct((negset.shape[0], D), f32),
        ),
        in_specs=[VMEM] * 10,
        out_specs=[VMEM] * 4,
        scratch_shapes=[
            pltpu.VMEM((PIXELS, number), f32),
            pltpu.VMEM((PAIRS, number, WIDE), f32),
            pltpu.VMEM((PIXELS, number), f32),
        ],
        compiler_params=PARAMS,
        name="local_pass",
    )(ids, ent, rel, tails, negset, band, band_t, bias, fc, fc_bias)


def step_rows(rows, state_row, gradient):
    state = as_columns(state_row)
    state = state + jnp.mean(gradient * gradient, axis=1, keepdims=True)
    scale = learn_rate * lax.rsqrt(state)
    rows = rows - gradient * scale[:, :1]
    return rows, jnp.transpose(state)[:1, :]


def entity_kernel(
    more, ids_ref, rows_ref, state_ref, head_ref, tail_ref, neg_ref, *outs
):
    rows_out, state_out = outs[:2]
    count = rows_ref.shape[0]
    number = tail_ref.shape[0]
    negatives = neg_ref.shape[0]
    grads = jnp.concatenate([jnp.transpose(head_ref[...]), tail_ref[...], neg_ref[...]], axis=0)
    high, low = halves(grads)
    named = jnp.concatenate(
        [ids_ref[0:1, :], ids_ref[2:3, :], ids_ref[3:4, :negatives]], axis=1
    )
    for block in range(count // LANES):
        at = slice(block * LANES, (block + 1) * LANES)
        place = lax.broadcasted_iota(jnp.int32, (LANES, named.shape[1]), 0) + block * LANES
        hit = jnp.where(place == named, 1.0, 0.0).astype(bf16)
        gradient = jnp.dot(hit, high, preferred_element_type=f32) + jnp.dot(
            hit, low, preferred_element_type=f32
        )
        new_rows, new_state = step_rows(rows_ref[at, :], state_ref[block : block + 1, :], gradient)
        rows_out[at, :] = new_rows
        state_out[block : block + 1, :] = new_state
    if more:
        table = rows_out[...].astype(bf16)
        for index, size in ((4, number), (5, negatives)):
            picked = jnp.dot(
                one_hot_rows(ids_ref[index : index + 1, :], count), table, preferred_element_type=f32
            )
            outs[2][(index - 4) * number : (index - 4) * number + size, :] = picked[:size].astype(bf16)


def entity_update(more, ids, rows, state, head_grad, tail_grad, neg_grad):
    out_shape = [
        jax.ShapeDtypeStruct(rows.shape, f32),
        jax.ShapeDtypeStruct(state.shape, f32),
    ]
    if more:
        out_shape.append(
            jax.ShapeDtypeStruct((tail_grad.shape[0] + neg_grad.shape[0], D), bf16)
        )
    return pl.pallas_call(
        functools.partial(entity_kernel, more),
        out_shape=out_shape,
        in_specs=[VMEM] * 6,
        out_specs=[VMEM] * len(out_shape),
        compiler_params=PARAMS,
        name="entity_update",
    )(ids, rows, state, head_grad, tail_grad, neg_grad)


def relation_kernel(place_ref, packs_ref, rows_ref, state_ref, rows_out, state_out, grads, names):
    sources = packs_ref.shape[0]

    def lay(index, carry):
        for part in range(2):
            block = packs_ref[place_ref[2 * index + part]]
            grads[index, :, part * LANES : (part + 1) * LANES] = block
            codes = block[PACK - 16 :, :].astype(f32)
            names[index, :, part * LANES : (part + 1) * LANES] = (
                codes[8:9, :] * 64.0 + codes[9:10, :]
            ).astype(jnp.int32)
        return carry

    lax.fori_loop(0, sources // 2, lay, 0)

    def block_step(first, size):
        place = lax.broadcasted_iota(jnp.int32, (size, 2 * LANES), 0) + first

        def add(index, acc):
            hit = jnp.where(place == names[index], 1.0, 0.0).astype(bf16)
            return acc + rows_nt(hit, grads[index])

        return lax.fori_loop(0, sources // 2, add, jnp.zeros((size, PACK), f32), unroll=8)

    count = rows_out.shape[0]
    for block in range(rows_ref.shape[0] // LANES):
        first = block * LANES
        gradient = block_step(first, LANES)[:, :D]
        new_rows, new_state = step_rows(
            rows_ref[first : first + LANES, :], state_ref[block : block + 1, :], gradient
        )
        size = min(LANES, count - first)
        rows_out[first : first + size, :] = new_rows[:size, :]
        state_out[block : block + 1, :] = new_state


def relation_update(place, packs, rows, state, out_rows):
    sources = packs.shape[0]
    return pl.pallas_call(
        relation_kernel,
        out_shape=(
            jax.ShapeDtypeStruct((out_rows, D), f32),
            jax.ShapeDtypeStruct(state.shape, f32),
        ),
        in_specs=[SMEM] + [VMEM] * 3,
        out_specs=[VMEM] * 2,
        scratch_shapes=[
            pltpu.VMEM((sources // 2, PACK, 2 * LANES), bf16),
            pltpu.VMEM((sources // 2, 1, 2 * LANES), jnp.int32),
        ],
        compiler_params=PARAMS,
        name="relation_update",
    )(place, packs, rows, state)


def swapped(bits):
    out = list(bits)
    for index in range(0, len(out) - 1, 2):
        out[index], out[index + 1] = out[index + 1], out[index]
    return out


class Plan:
    def __init__(self, groups, shards):
        self.total = groups * shards
        self.shards = shards
        near = [1 << bit for bit in range(1, shards.bit_length() - 1)]
        far = [shards << bit for bit in range(groups.bit_length() - 1)]
        self.even = near + far
        self.odd = swapped(near) + swapped(far)
        steps = [self.route(a, b) for a, b in zip(self.even, self.odd)]
        core = self.route(1, 1)
        self.within = steps[: len(near)] + [core]
        self.across = steps + [core]

    def route(self, even, odd):
        return [(at, at ^ (odd if at & 1 else even)) for at in range(self.total)]

    def partner(self, bit):
        mask = self.shards << bit
        return self.route(mask, mask)

    def places(self, me):
        source = jnp.arange(self.total, dtype=jnp.int32)
        differ = source ^ me
        even = jnp.zeros_like(source)
        odd = jnp.zeros_like(source)
        for step, (one, other) in enumerate(zip(self.even, self.odd)):
            even = even + jnp.where((differ & one) != 0, 1 << step, 0)
            odd = odd + jnp.where((differ & other) != 0, 1 << step, 0)
        spot = jnp.where((source & 1) == 0, even, odd)
        return spot + jnp.where((differ & 1) != 0, 1 << len(self.even), 0)


def send(block, route):
    return lax.ppermute(block, BOTH, route)


def doubled(block, routes):
    for route in routes:
        block = jnp.concatenate([block, send(block, route)], axis=0)
    return block


def halved(block, routes):
    for route in reversed(routes):
        half = block.shape[0] // 2
        block = block[:half] + send(block[half:], route)
    return block


def shards(
    plan,
    entity_rows,
    entity_state,
    relation_rows,
    relation_state,
    conv_weight,
    conv_bias,
    fc_weight,
    fc_bias,
    head_ids,
    rel_ids,
    tail_ids,
    neg_ids,
):
    number = head_ids.shape[1]
    count = relation_rows.shape[0]
    spare = -count % LANES
    me = lax.axis_index("group") * plan.shards + lax.axis_index("shard")
    wanted = jnp.concatenate([tail_ids, neg_ids], axis=1)
    requested = [send(wanted[r], plan.partner(r)) for r in range(ROUNDS)]
    answer = entity_rows[requested[0]].astype(bf16)

    taps = jnp.tile(conv_weight.reshape(FILTERS, 9).T.astype(f32), (1, WIDE // FILTERS))
    bias = jnp.tile(conv_bias[None, :], (1, WIDE // FILTERS))
    fc, band, band_t = prepare(fc_weight, taps)
    fc = fc.reshape(PAIRS, WIDE, D)
    rel = jnp.pad(relation_rows, ((0, spare), (0, 0)))
    rel_state = jnp.pad(relation_state, (0, spare), constant_values=1.0).reshape(-1, LANES)
    ent = entity_rows
    ent_state = entity_state.reshape(-1, LANES)
    place = plan.places(me)

    def lane_row(ids):
        return jnp.pad(ids, (0, LANES - ids.shape[0]))[None, :]

    for r in range(ROUNDS):
        last = r == ROUNDS - 1
        answered = send(answer, plan.partner(r))
        negset = doubled(answered[number:], plan.within)
        following = requested[min(r + 1, ROUNDS - 1)]
        ids = jnp.concatenate(
            [
                head_ids[r][None, :],
                rel_ids[r][None, :],
                requested[r][None, :number],
                lane_row(requested[r][number:]),
                following[None, :number],
                lane_row(following[number:]),
                jnp.zeros((2, LANES), jnp.int32),
            ],
            axis=0,
        )
        pack, head_grad, tail_grad, neg_part = local_pass(
            ids, ent, rel, answered[:number], negset, band, band_t, bias, fc, fc_bias[None, :]
        )
        share = halved(neg_part, plan.within)
        tail_back = send(tail_grad, plan.partner(r))
        neg_back = send(share, plan.partner(r))
        packs = doubled(pack[None], plan.across)
        outs = entity_update(not last, ids, ent, ent_state, head_grad, tail_back, neg_back)
        ent, ent_state = outs[:2]
        if not last:
            answer = outs[2]
        rel, rel_state = relation_update(
            place, packs, rel, rel_state, count if last else count + spare
        )
    return (ent, ent_state.reshape(-1), rel, rel_state.reshape(-1)[:count])


def solution(mesh):
    plan = Plan(mesh.shape["group"], mesh.shape["shard"])
    in_specs = (
        P(BOTH, None),
        P(BOTH),
        P(),
        P(),
        P(),
        P(),
        P(),
        P(),
        P(None, BOTH),
        P(None, BOTH),
        P(None, BOTH),
        P(None, BOTH),
    )
    out_specs = (P(BOTH, None), P(BOTH), P(), P())
    return jax.shard_map(
        functools.partial(shards, plan),
        mesh=mesh,
        in_specs=in_specs,
        out_specs=out_specs,
        check_vma=False,
    )
```

time: 493 us -> 202 us (0.41)
  waiting for transfers between devices: 233 us -> 57 us
  local copies, waits for them, and re-layouts: 118 us -> 33.8 us
  Pallas kernels: 0 us -> 71.5 us
  matrix products: 44.8 us -> 0 us
  other arithmetic: 39 us -> 0.34 us
  blocking collectives: 28.2 us -> 0 us
  starting transfers between devices: 10.2 us -> 37.8 us
  between operations: 16.1 us -> 1.14 us
    psum x2 -> x0, waiting for transfers between devices: 223 us -> none  [shards(): rel_total = lax.psum(rel_part, ('group', 'shard'))]
    pallas_call x0 -> x7, Pallas kernels: none -> 71.5 us  [the longest x2 36.2 us: local_pass(): pl.pallas_call(pass_kernel, out_shape=(jax.ShapeDtypeStruct((PACK, number...]
    ppermute x6 -> x30, waiting for transfers between devices: 4.48 us -> 57 us  [send(): return lax.ppermute(block, BOTH, route)]
    dot_general x10 -> x0, matrix products: 42.9 us -> none  [the longest x2 11.9 us: local_pass(): jnp.einsum('fk,fijt->kijt', filters, pre1_grad, preferred_element_type=jn...]
    reshape x15 -> x1, local copies, waits for them, and re-layouts: 32.9 us -> 0.01 us  [shards(): jnp.pad(relation_state, (0, spare), constant_values=1.0).reshape(-1, LANES)]
    another operation x25 -> x5, local copies, waits for them, and re-layouts: 29.4 us -> 0.21 us  [the longest x2 0.12 us: shards(): jnp.tile(conv_weight.reshape(FILTERS, 9).T.astype(f32), (1, WIDE // FILTE...]
    all_gather x2 -> x0, blocking collectives: 28.2 us -> none  [shards(): negset = lax.all_gather(own_negative, 'shard', axis=0, tiled=True)]
    ppermute x6 -> x30, starting transfers between devices: 9.56 us -> 37.8 us  [send(): return lax.ppermute(block, BOTH, route)]
  transfers between devices with their start and end apart: 10 -> 30, of which waited for: 6 -> 19; matrix products, arithmetic and copies ran while one was open for 35% -> 11% of each run, Pallas kernels for 0% -> 4%
where the time goes in v1:
time: 202 us
  Pallas kernels  71.5 us (35%)
  waiting for transfers between devices  57 us (28%)
  starting transfers between devices  37.8 us (19%)
  local copies, waits for them, and re-layouts  33.8 us (17%)
    ppermute x30, waiting for transfers between devices, send(): return lax.ppermute(block, BOTH, route)  57 us
    ppermute x30, starting transfers between devices, send(): return lax.ppermute(block, BOTH, route)  37.8 us
    pallas_call x2, Pallas kernels, local_pass(): pl.pallas_call(pass_kernel, out_shape=(jax.ShapeDtypeStruct((PACK, number...  36.2 us
    pallas_call x2, Pallas kernels, relation_update(): pl.pallas_call(relation_kernel, out_shape=(jax.ShapeDtypeStruct((out_rows...  27 us
    unnamed x64, local copies, waits for them, and re-layouts  23.1 us
    concatenate x4, local copies, waits for them, and re-layouts, doubled(): block = jnp.concatenate([block, send(block, route)], axis=0)  6.14 us
    pallas_call x1, Pallas kernels, prepare(): pl.pallas_call(prepare_kernel, out_shape=(jax.ShapeDtypeStruct((rows, D),...  5.02 us
  transfers between devices with their start and end apart: 30, of which 19 were waited for; matrix products, arithmetic and copies ran while one was open for 11% of the time, Pallas kernels for 4%

profile of v1, /device:TPU:0, one launch (start us, length us, event | category | flops | bytes accessed | tf_op | source)
XLA Modules:
  0.0 201.6 jit_solution(9961860540007984536)
XLA Ops:
  2.1 2.9 %collective-permute-start.1 = (s32[160]{0:T(256)S(1)}, s32[160]{0:T(256)S(1)}, u32[]{:S(2)}, u32[]{:S(2)}) collective-permute-start(s32[160]{0:T(256)S(1)} %bitcast.42), channel_id=1, source_target_pairs={{0,8},{1,9},{2,10},{3,11},{4,12},{5,13},{6,14},{7,15},{8,0},{9,1},... | collective-permute-start | bytes 1928 | tf_op jit(solution)/shard_map/ppermute | solution.py:365
  7.4 2.1 %collective-permute-start.2 = (bf16[160,200]{1,0:T(8,128)(2,1)S(1)}, bf16[160,200]{1,0:T(8,128)(2,1)S(1)}, u32[]{:S(2)}, u32[]{:S(2)}) collective-permute-start(bf16[160,200]{1,0:T(8,128)(2,1)S(1)} %gather_fusion), channel_id=1, source_target_pairs={{0,8},{1,9},{2,10},{3,11},{4,12},{5,13},{6,14},{7,15},{8,0},{9,1},... | collective-permute-start | bytes 192008 | tf_op jit(solution)/shard_map/ppermute | solution.py:365
  12.0 2.1 %collective-permute-start.3 = (bf16[32,200]{1,0:T(8,128)(2,1)S(1)}, bf16[32,200]{1,0:T(8,128)(2,1)S(1)}, u32[]{:S(2)}, u32[]{:S(2)}) collective-permute-start(bf16[32,200]{1,0:T(8,128)(2,1)S(1)} %slice.117), channel_id=1, source_target_pairs={{0,2},{1,5},{2,0},{3,7},{4,6},{5,1},{6,4},{7,3},{8,10},{9,13},{10,... | collective-permute-start | bytes 38408 | tf_op jit(solution)/shard_map/ppermute | solution.py:365
  16.1 7.3 %copy.25.fc_ref = bf16[10368,200]{1,0:T(8,128)(2,1)} copy(bf16[10368,200]{0,1:T(8,128)(2,1)} %param.18) | data formatting | bytes 8294400 | tf_op args[6]
  25.2 5.0 %prepare.1 = (bf16[10368,200]{1,0:T(8,128)(2,1)S(1)}, bf16[80,1152]{1,0:T(8,128)(2,1)S(1)}, bf16[1152,128]{1,0:T(8,128)(2,1)S(1)}) custom-call(bf16[10368,200]{1,0:T(8,128)(2,1)} %copy.25.fc_ref, f32[9,1152]{1,0:T(8,128)S(1)} %tile.18.taps_ref), custom_call_target="tpu_custom_call" | custom-call | tf_op jit(solution)/shard_map/prepare/pallas_call | solution.py:106
  30.2 2.4 %copy-done = bf16[10368,200]{1,0:T(8,128)(2,1)} copy-done((bf16[10368,200]{1,0:T(8,128)(2,1)}, bf16[10368,200]{1,0:T(8,128)(2,1)S(1)}, u32[]{:S(2)}) %copy-start) | copy-done | bytes 4147224
  32.6 2.7 %collective-permute-start.4 = (bf16[64,200]{1,0:T(8,128)(2,1)S(1)}, bf16[64,200]{1,0:T(8,128)(2,1)S(1)}, u32[]{:S(2)}, u32[]{:S(2)}) collective-permute-start(bf16[64,200]{1,0:T(8,128)(2,1)S(1)} %pad_maximum_fusion.10), channel_id=1, source_target_pairs={{0,4},{1,3},{2,6},{3,1},{4,0},{5,7},{6,2},{7,5},{8,12},{9,11},{10,... | collective-permute-start | bytes 76808 | tf_op jit(solution)/shard_map/ppermute | solution.py:365
  35.3 2.2 %collective-permute-done.4 = bf16[64,200]{1,0:T(8,128)(2,1)S(1)} collective-permute-done((bf16[64,200]{1,0:T(8,128)(2,1)S(1)}, bf16[64,200]{1,0:T(8,128)(2,1)S(1)}, u32[]{:S(2)}, u32[]{:S(2)}) %collective-permute-start.4) | collective-permute-done | bytes 25632 | tf_op jit(solution)/shard_map/ppermute | solution.py:365
  38.8 17.8 %local_pass.2 = (bf16[208,128]{1,0:T(8,128)(2,1)S(1)}, f32[200,128]{1,0:T(8,128)S(1)}, f32[128,200]{1,0:T(8,128)S(1)}, f32[256,200]{1,0:T(8,128)S(1)}) custom-call(s32[8,128]{1,0:T(8,128)S(1)} %concatenate.71.ids_ref, f32[1024,200]{1,0:T(8,128)S(1)} %copy.27.ent_ref.rows_ref, f32[1408,200]{1,0:T(8,128)S(1)} %pad.19.rel_ref.rows_ref, ...), custom_call_target="tpu_custom_call" | custom-call | tf_op jit(solution)/shard_map/local_pass/pallas_call | solution.py:192
  61.1 2.4 %collective-permute-start.12 = (bf16[2,208,128]{2,1,0:T(8,128)(2,1)S(1)}, bf16[2,208,128]{2,1,0:T(8,128)(2,1)S(1)}, u32[]{:S(2)}, u32[]{:S(2)}) collective-permute-start(bf16[2,208,128]{2,1,0:T(8,128)(2,1)S(1)} %pad_maximum_fusion.6), channel_id=1, source_target_pairs={{0,4},{1,3},{2,6},{3,1},{4,0},{5,7},{6,2},{7,5},{8,12},{9,11},{10,... | collective-permute-start | bytes 319496 | tf_op jit(solution)/shard_map/ppermute | solution.py:365
  64.2 3.7 %collective-permute-done.12 = bf16[2,208,128]{2,1,0:T(8,128)(2,1)S(1)} collective-permute-done((bf16[2,208,128]{2,1,0:T(8,128)(2,1)S(1)}, bf16[2,208,128]{2,1,0:T(8,128)(2,1)S(1)}, u32[]{:S(2)}, u32[]{:S(2)}) %collective-permute-start.12) | collective-permute-done | bytes 106528 | tf_op jit(solution)/shard_map/ppermute | solution.py:365
  70.9 4.3 %collective-permute-done.13 = bf16[4,208,128]{2,1,0:T(8,128)(2,1)S(1)} collective-permute-done((bf16[4,208,128]{2,1,0:T(8,128)(2,1)S(1)}, bf16[4,208,128]{2,1,0:T(8,128)(2,1)S(1)}, u32[]{:S(2)}, u32[]{:S(2)}) %collective-permute-start.13) | collective-permute-done | bytes 213024 | tf_op jit(solution)/shard_map/ppermute | solution.py:365
  75.3 2.1 %collective-permute-start.14 = (bf16[8,208,128]{2,1,0:T(8,128)(2,1)S(1)}, bf16[8,208,128]{2,1,0:T(8,128)(2,1)S(1)}, u32[]{:S(2)}, u32[]{:S(2)}) collective-permute-start(bf16[8,208,128]{2,1,0:T(8,128)(2,1)S(1)} %pad_maximum_fusion), channel_id=1, source_target_pairs={{0,16},{1,9},{2,18},{3,11},{4,20},{5,13},{6,22},{7,15},{8,24},{9,1... | collective-permute-start | bytes 1277960 | tf_op jit(solution)/shard_map/ppermute | solution.py:365
  79.0 4.6 %collective-permute-done.14 = bf16[8,208,128]{2,1,0:T(8,128)(2,1)S(1)} collective-permute-done((bf16[8,208,128]{2,1,0:T(8,128)(2,1)S(1)}, bf16[8,208,128]{2,1,0:T(8,128)(2,1)S(1)}, u32[]{:S(2)}, u32[]{:S(2)}) %collective-permute-start.14) | collective-permute-done | bytes 426016 | tf_op jit(solution)/shard_map/ppermute | solution.py:365
  84.4 2.0 collective-permute-start.10
  86.4 2.1 %collective-permute-done.10.neg_ref = f32[32,200]{1,0:T(8,128)S(1)} collective-permute-done((f32[32,200]{1,0:T(8,128)S(1)}, f32[32,200]{1,0:T(8,128)S(1)}, u32[]{:S(2)}, u32[]{:S(2)}) %collective-permute-start.10) | collective-permute-done | bytes 25632 | tf_op jit(solution)/shard_map/ppermute | solution.py:365
  89.9 2.0 %collective-permute-start.16 = (bf16[160,200]{1,0:T(8,128)(2,1)S(1)}, bf16[160,200]{1,0:T(8,128)(2,1)S(1)}, u32[]{:S(2)}, u32[]{:S(2)}) collective-permute-start(bf16[160,200]{1,0:T(8,128)(2,1)S(1)} %get-tuple-element.34), channel_id=1, source_target_pairs={{0,16},{1,17},{2,18},{3,19},{4,20},{5,21},{6,22},{7,23},{8,24},{9,... | collective-permute-start | bytes 192008 | tf_op jit(solution)/shard_map/ppermute | solution.py:365
  91.9 2.5 %collective-permute-done.16 = bf16[160,200]{1,0:T(8,128)(2,1)S(1)} collective-permute-done((bf16[160,200]{1,0:T(8,128)(2,1)S(1)}, bf16[160,200]{1,0:T(8,128)(2,1)S(1)}, u32[]{:S(2)}, u32[]{:S(2)}) %collective-permute-start.16) | collective-permute-done | bytes 64032 | tf_op jit(solution)/shard_map/ppermute | solution.py:365
  94.6 3.6 %collective-permute-done.17 = bf16[32,200]{1,0:T(8,128)(2,1)S(1)} collective-permute-done((bf16[32,200]{1,0:T(8,128)(2,1)S(1)}, bf16[32,200]{1,0:T(8,128)(2,1)S(1)}, u32[]{:S(2)}, u32[]{:S(2)}) %collective-permute-start.17) | collective-permute-done | bytes 12832 | tf_op jit(solution)/shard_map/ppermute | solution.py:365
  100.0 3.1 %collective-permute-done.18 = bf16[64,200]{1,0:T(8,128)(2,1)S(1)} collective-permute-done((bf16[64,200]{1,0:T(8,128)(2,1)S(1)}, bf16[64,200]{1,0:T(8,128)(2,1)S(1)}, u32[]{:S(2)}, u32[]{:S(2)}) %collective-permute-start.18) | collective-permute-done | bytes 25632 | tf_op jit(solution)/shard_map/ppermute | solution.py:365
  104.4 2.1 %constant_dynamic-update-slice_fusion.7.packs_ref = bf16[32,208,128]{2,1,0:T(8,128)(2,1)} fusion(bf16[32,208,128]{2,1,0:T(8,128)(2,1)} %copy-done.3, bf16[16,208,128]{2,1,0:T(8,128)(2,1)} %collective-permute-done.15), kind=kLoop, calls=%fused_computation.22 | loop fusion | bytes 1703936 | tf_op jit(solution)/shard_map/concatenate | solution.py:370
  108.0 12.7 %relation_update.2 = (f32[1408,200]{1,0:T(8,128)S(1)}, f32[11,128]{1,0:T(8,128)S(1)}) custom-call(s32[32]{0:T(128)S(1)} %fusion.6.place_ref, bf16[32,208,128]{2,1,0:T(8,128)(2,1)S(1)} %copy-done.4, f32[1408,200]{1,0:T(8,128)S(1)} %pad.19.rel_ref.rows_ref, f32[11,128]{1,0:T(8,128)S(1)} %pad_bitcast_fusion.state_ref), custom_call_target="tpu_custom_call" | custom-call | tf_op jit(solution)/shard_map/relation_update/pallas_call | solution.py:308
  120.8 18.5 %local_pass.3 = (bf16[208,128]{1,0:T(8,128)(2,1)S(1)}, f32[200,128]{1,0:T(8,128)S(1)}, f32[128,200]{1,0:T(8,128)S(1)}, f32[256,200]{1,0:T(8,128)S(1)}) custom-call(s32[8,128]{1,0:T(8,128)S(1)} %concatenate.70.ids_ref, f32[1024,200]{1,0:T(8,128)S(1)} %get-tuple-element.30.ent_ref.rows_ref, f32[1408,200]{1,0:T(8,128)S(1)} %get-tuple-element.33.rel_ref.rows_ref, ...), custom_call_target="tpu_custom_call" | custom-call | tf_op jit(solution)/shard_map/local_pass/pallas_call | solution.py:192
  140.2 3.8 %collective-permute-done.25 = bf16[1,208,128]{2,1,0:T(8,128)(2,1)S(1)} collective-permute-done((bf16[1,208,128]{2,1,0:T(8,128)(2,1)S(1)}, bf16[1,208,128]{2,1,0:T(8,128)(2,1)S(1)}, u32[]{:S(2)}, u32[]{:S(2)}) %collective-permute-start.25) | collective-permute-done | bytes 53280 | tf_op jit(solution)/shard_map/ppermute | solution.py:365
  145.3 5.5 %collective-permute-done.26 = bf16[2,208,128]{2,1,0:T(8,128)(2,1)S(1)} collective-permute-done((bf16[2,208,128]{2,1,0:T(8,128)(2,1)S(1)}, bf16[2,208,128]{2,1,0:T(8,128)(2,1)S(1)}, u32[]{:S(2)}, u32[]{:S(2)}) %collective-permute-start.26) | collective-permute-done | bytes 106528 | tf_op jit(solution)/shard_map/ppermute | solution.py:365
  152.5 5.6 %collective-permute-done.27 = bf16[4,208,128]{2,1,0:T(8,128)(2,1)S(1)} collective-permute-done((bf16[4,208,128]{2,1,0:T(8,128)(2,1)S(1)}, bf16[4,208,128]{2,1,0:T(8,128)(2,1)S(1)}, u32[]{:S(2)}, u32[]{:S(2)}) %collective-permute-start.27) | collective-permute-done | bytes 213024 | tf_op jit(solution)/shard_map/ppermute | solution.py:365
  162.7 3.7 %collective-permute-done.28 = bf16[8,208,128]{2,1,0:T(8,128)(2,1)S(1)} collective-permute-done((bf16[8,208,128]{2,1,0:T(8,128)(2,1)S(1)}, bf16[8,208,128]{2,1,0:T(8,128)(2,1)S(1)}, u32[]{:S(2)}, u32[]{:S(2)}) %collective-permute-start.28) | collective-permute-done | bytes 426016 | tf_op jit(solution)/shard_map/ppermute | solution.py:365
  167.5 5.2 %collective-permute-done.22 = f32[64,200]{1,0:T(8,128)S(1)} collective-permute-done((f32[64,200]{1,0:T(8,128)S(1)}, f32[64,200]{1,0:T(8,128)S(1)}, u32[]{:S(2)}, u32[]{:S(2)}) %collective-permute-start.22) | collective-permute-done | bytes 51232 | tf_op jit(solution)/shard_map/ppermute | solution.py:365
  174.4 2.3 %collective-permute-done.23 = f32[32,200]{1,0:T(8,128)S(1)} collective-permute-done((f32[32,200]{1,0:T(8,128)S(1)}, f32[32,200]{1,0:T(8,128)S(1)}, u32[]{:S(2)}, u32[]{:S(2)}) %collective-permute-start.23) | collective-permute-done | bytes 25632 | tf_op jit(solution)/shard_map/ppermute | solution.py:365
  178.3 2.4 %collective-permute-done.24.neg_ref = f32[32,200]{1,0:T(8,128)S(1)} collective-permute-done((f32[32,200]{1,0:T(8,128)S(1)}, f32[32,200]{1,0:T(8,128)S(1)}, u32[]{:S(2)}, u32[]{:S(2)}) %collective-permute-start.24) | collective-permute-done | bytes 25632 | tf_op jit(solution)/shard_map/ppermute | solution.py:365
  183.7 2.1 %constant_dynamic-update-slice_fusion.18.packs_ref = bf16[32,208,128]{2,1,0:T(8,128)(2,1)} fusion(bf16[32,208,128]{2,1,0:T(8,128)(2,1)} %get-tuple-element.53, bf16[16,208,128]{2,1,0:T(8,128)(2,1)} %collective-permute-done.29), kind=kLoop, calls=%fused_computation.33 | loop fusion | bytes 1703936 | tf_op jit(solution)/shard_map/concatenate | solution.py:370
  185.9 14.3 %relation_update.3 = (f32[1387,200]{1,0:T(8,128)S(1)}, f32[11,128]{1,0:T(8,128)}) custom-call(s32[32]{0:T(128)S(1)} %copy-done.15, bf16[32,208,128]{2,1,0:T(8,128)(2,1)} %constant_dynamic-update-slice_fusion.18.packs_ref, f32[1408,200]{1,0:T(8,128)S(1)} %copy-done.2, f32[11,128]{1,0:T(8,128)S(1)} %copy-done.10), custom_call_target="tpu_custom_call" | custom-call | tf_op jit(solution)/shard_map/relation_update/pallas_call | solution.py:308
  (152 shorter events, 45.5 us)
Async XLA Ops:
  2.1 4.5 %collective-permute-start.1 = (s32[160]{0:T(256)S(1)}, s32[160]{0:T(256)S(1)}, u32[]{:S(2)}, u32[]{:S(2)}) collective-permute-start(s32[160]{0:T(256)S(1)} %bitcast.42), channel_id=1, source_target_pairs={{0,8},{1,9},{2,10},{3,11},{4,12},{5,13},{6,14},{7,15},{8,0},{9,1},... | collective-permute-start | bytes 1928 | tf_op jit(solution)/shard_map/ppermute | solution.py:365
  7.4 4.5 %collective-permute-start.2 = (bf16[160,200]{1,0:T(8,128)(2,1)S(1)}, bf16[160,200]{1,0:T(8,128)(2,1)S(1)}, u32[]{:S(2)}, u32[]{:S(2)}) collective-permute-start(bf16[160,200]{1,0:T(8,128)(2,1)S(1)} %gather_fusion), channel_id=1, source_target_pairs={{0,8},{1,9},{2,10},{3,11},{4,12},{5,13},{6,14},{7,15},{8,0},{9,1},... | collective-permute-start | bytes 192008 | tf_op jit(solution)/shard_map/ppermute | solution.py:365
  9.5 23.0 %collective-permute-start = (s32[160]{0:T(256)S(1)}, s32[160]{0:T(256)S(1)}, u32[]{:S(2)}, u32[]{:S(2)}) collective-permute-start(s32[160]{0:T(256)S(1)} %bitcast.41), channel_id=1, source_target_pairs={{0,16},{1,17},{2,18},{3,19},{4,20},{5,21},{6,22},{7,23},{8,24},{9,... | collective-permute-start | bytes 1928 | tf_op jit(solution)/shard_map/ppermute | solution.py:365
  12.0 20.6 %collective-permute-start.3 = (bf16[32,200]{1,0:T(8,128)(2,1)S(1)}, bf16[32,200]{1,0:T(8,128)(2,1)S(1)}, u32[]{:S(2)}, u32[]{:S(2)}) collective-permute-start(bf16[32,200]{1,0:T(8,128)(2,1)S(1)} %slice.117), channel_id=1, source_target_pairs={{0,2},{1,5},{2,0},{3,7},{4,6},{5,1},{6,4},{7,3},{8,10},{9,13},{10,... | collective-permute-start | bytes 38408 | tf_op jit(solution)/shard_map/ppermute | solution.py:365
  32.6 24.1 %copy-start.7 = (bf16[80,1152]{1,0:T(8,128)(2,1)}, bf16[80,1152]{1,0:T(8,128)(2,1)S(1)}, u32[]{:S(2)}) copy-start(bf16[80,1152]{1,0:T(8,128)(2,1)S(1)} %get-tuple-element.24.band_ref) | copy-start | bytes 552964
  32.6 4.9 %collective-permute-start.4 = (bf16[64,200]{1,0:T(8,128)(2,1)S(1)}, bf16[64,200]{1,0:T(8,128)(2,1)S(1)}, u32[]{:S(2)}, u32[]{:S(2)}) collective-permute-start(bf16[64,200]{1,0:T(8,128)(2,1)S(1)} %pad_maximum_fusion.10), channel_id=1, source_target_pairs={{0,4},{1,3},{2,6},{3,1},{4,0},{5,7},{6,2},{7,5},{8,12},{9,11},{10,... | collective-permute-start | bytes 76808 | tf_op jit(solution)/shard_map/ppermute | solution.py:365
  35.2 32.6 %copy-start.17 = (s32[1,128]{1,0:T(1,128)}, s32[1,128]{1,0:T(1,128)S(1)}, u32[]{:S(2)}) copy-start(s32[1,128]{1,0:T(1,128)S(1)} %get-tuple-element.78) | copy-start | bytes 1540
  37.5 1.3 collective-permute-start.5
  56.6 4.5 %collective-permute-start.11 = (bf16[1,208,128]{2,1,0:T(8,128)(2,1)S(1)}, bf16[1,208,128]{2,1,0:T(8,128)(2,1)S(1)}, u32[]{:S(2)}, u32[]{:S(2)}) collective-permute-start(bf16[1,208,128]{2,1,0:T(8,128)(2,1)S(1)} %bitcast.29), channel_id=1, source_target_pairs={{0,2},{1,5},{2,0},{3,7},{4,6},{5,1},{6,4},{7,3},{8,10},{9,13},{10,... | collective-permute-start | bytes 159752 | tf_op jit(solution)/shard_map/ppermute | solution.py:365
  57.5 29.0 %collective-permute-start.6 = (f32[128,200]{1,0:T(8,128)S(1)}, f32[128,200]{1,0:T(8,128)S(1)}, u32[]{:S(2)}, u32[]{:S(2)}) collective-permute-start(f32[128,200]{1,0:T(8,128)S(1)} %get-tuple-element.28), channel_id=1, source_target_pairs={{0,8},{1,9},{2,10},{3,11},{4,12},{5,13},{6,14},{7,15},{8,0},{9,1},... | collective-permute-start | bytes 307208 | tf_op jit(solution)/shard_map/ppermute | solution.py:365
  59.3 10.4 %collective-permute-start.7 = (f32[128,200]{1,0:T(8,128)S(1)}, f32[128,200]{1,0:T(8,128)S(1)}, u32[]{:S(2)}, u32[]{:S(2)}) collective-permute-start(f32[128,200]{1,0:T(8,128)S(1)} %slice.98), channel_id=1, source_target_pairs={{0,1},{1,0},{2,3},{3,2},{4,5},{5,4},{6,7},{7,6},{8,9},{9,8},{10,11... | collective-permute-start | bytes 307208 | tf_op jit(solution)/shard_map/ppermute | solution.py:365
  61.1 6.8 %collective-permute-start.12 = (bf16[2,208,128]{2,1,0:T(8,128)(2,1)S(1)}, bf16[2,208,128]{2,1,0:T(8,128)(2,1)S(1)}, u32[]{:S(2)}, u32[]{:S(2)}) collective-permute-start(bf16[2,208,128]{2,1,0:T(8,128)(2,1)S(1)} %pad_maximum_fusion.6), channel_id=1, source_target_pairs={{0,4},{1,3},{2,6},{3,1},{4,0},{5,7},{6,2},{7,5},{8,12},{9,11},{10,... | collective-permute-start | bytes 319496 | tf_op jit(solution)/shard_map/ppermute | solution.py:365
  67.9 7.4 %collective-permute-start.13 = (bf16[4,208,128]{2,1,0:T(8,128)(2,1)S(1)}, bf16[4,208,128]{2,1,0:T(8,128)(2,1)S(1)}, u32[]{:S(2)}, u32[]{:S(2)}) collective-permute-start(bf16[4,208,128]{2,1,0:T(8,128)(2,1)S(1)} %pad_maximum_fusion.2), channel_id=1, source_target_pairs={{0,8},{1,17},{2,10},{3,19},{4,12},{5,21},{6,14},{7,23},{8,0},{9,25... | collective-permute-start | bytes 638984 | tf_op jit(solution)/shard_map/ppermute | solution.py:365
  69.8 7.6 %collective-permute-start.8 = (f32[64,200]{1,0:T(8,128)S(1)}, f32[64,200]{1,0:T(8,128)S(1)}, u32[]{:S(2)}, u32[]{:S(2)}) collective-permute-start(f32[64,200]{1,0:T(8,128)S(1)} %slice.119), channel_id=1, source_target_pairs={{0,4},{1,3},{2,6},{3,1},{4,0},{5,7},{6,2},{7,5},{8,12},{9,11},{10,... | collective-permute-start | bytes 153608 | tf_op jit(solution)/shard_map/ppermute | solution.py:365
  75.3 8.2 %collective-permute-start.14 = (bf16[8,208,128]{2,1,0:T(8,128)(2,1)S(1)}, bf16[8,208,128]{2,1,0:T(8,128)(2,1)S(1)}, u32[]{:S(2)}, u32[]{:S(2)}) collective-permute-start(bf16[8,208,128]{2,1,0:T(8,128)(2,1)S(1)} %pad_maximum_fusion), channel_id=1, source_target_pairs={{0,16},{1,9},{2,18},{3,11},{4,20},{5,13},{6,22},{7,15},{8,24},{9,1... | collective-permute-start | bytes 1277960 | tf_op jit(solution)/shard_map/ppermute | solution.py:365
  77.5 7.0 %collective-permute-start.9 = (f32[32,200]{1,0:T(8,128)S(1)}, f32[32,200]{1,0:T(8,128)S(1)}, u32[]{:S(2)}, u32[]{:S(2)}) collective-permute-start(f32[32,200]{1,0:T(8,128)S(1)} %slice.121), channel_id=1, source_target_pairs={{0,2},{1,5},{2,0},{3,7},{4,6},{5,1},{6,4},{7,3},{8,10},{9,13},{10,... | collective-permute-start | bytes 76808 | tf_op jit(solution)/shard_map/ppermute | solution.py:365
  84.4 20.0 %collective-permute-start.15 = (bf16[16,208,128]{2,1,0:T(8,128)(2,1)}, bf16[16,208,128]{2,1,0:T(8,128)(2,1)}, u32[]{:S(2)}, u32[]{:S(2)}) collective-permute-start(bf16[16,208,128]{2,1,0:T(8,128)(2,1)} %get-tuple-element.54), channel_id=1, source_target_pairs={{0,1},{1,0},{2,3},{3,2},{4,5},{5,4},{6,7},{7,6},{8,9},{9,8},{10,11... | collective-permute-start | bytes 2555912 | tf_op jit(solution)/shard_map/ppermute | solution.py:365
  84.4 4.1 %collective-permute-start.10 = (f32[32,200]{1,0:T(8,128)S(1)}, f32[32,200]{1,0:T(8,128)S(1)}, u32[]{:S(2)}, u32[]{:S(2)}) collective-permute-start(f32[32,200]{1,0:T(8,128)S(1)} %slice_add_fusion.5), channel_id=1, source_target_pairs={{0,8},{1,9},{2,10},{3,11},{4,12},{5,13},{6,14},{7,15},{8,0},{9,1},... | collective-permute-start | bytes 76808 | tf_op jit(solution)/shard_map/ppermute | solution.py:365
  89.9 4.5 %collective-permute-start.16 = (bf16[160,200]{1,0:T(8,128)(2,1)S(1)}, bf16[160,200]{1,0:T(8,128)(2,1)S(1)}, u32[]{:S(2)}, u32[]{:S(2)}) collective-permute-start(bf16[160,200]{1,0:T(8,128)(2,1)S(1)} %get-tuple-element.34), channel_id=1, source_target_pairs={{0,16},{1,17},{2,18},{3,19},{4,20},{5,21},{6,22},{7,23},{8,24},{9,... | collective-permute-start | bytes 192008 | tf_op jit(solution)/shard_map/ppermute | solution.py:365
  94.4 3.7 %collective-permute-start.17 = (bf16[32,200]{1,0:T(8,128)(2,1)S(1)}, bf16[32,200]{1,0:T(8,128)(2,1)S(1)}, u32[]{:S(2)}, u32[]{:S(2)}) collective-permute-start(bf16[32,200]{1,0:T(8,128)(2,1)S(1)} %slice.123), channel_id=1, source_target_pairs={{0,2},{1,5},{2,0},{3,7},{4,6},{5,1},{6,4},{7,3},{8,10},{9,13},{10,... | collective-permute-start | bytes 38408 | tf_op jit(solution)/shard_map/ppermute | solution.py:365
  98.1 4.9 %collective-permute-start.18 = (bf16[64,200]{1,0:T(8,128)(2,1)S(1)}, bf16[64,200]{1,0:T(8,128)(2,1)S(1)}, u32[]{:S(2)}, u32[]{:S(2)}) collective-permute-start(bf16[64,200]{1,0:T(8,128)(2,1)S(1)} %pad_maximum_fusion.11), channel_id=1, source_target_pairs={{0,4},{1,3},{2,6},{3,1},{4,0},{5,7},{6,2},{7,5},{8,12},{9,11},{10,... | collective-permute-start | bytes 76808 | tf_op jit(solution)/shard_map/ppermute | solution.py:365
  103.1 1.3 collective-permute-start.19
  139.2 4.8 %collective-permute-start.25 = (bf16[1,208,128]{2,1,0:T(8,128)(2,1)S(1)}, bf16[1,208,128]{2,1,0:T(8,128)(2,1)S(1)}, u32[]{:S(2)}, u32[]{:S(2)}) collective-permute-start(bf16[1,208,128]{2,1,0:T(8,128)(2,1)S(1)} %bitcast.33), channel_id=1, source_target_pairs={{0,2},{1,5},{2,0},{3,7},{4,6},{5,1},{6,4},{7,3},{8,10},{9,13},{10,... | collective-permute-start | bytes 159752 | tf_op jit(solution)/shard_map/ppermute | solution.py:365
  144.0 6.8 %collective-permute-start.26 = (bf16[2,208,128]{2,1,0:T(8,128)(2,1)S(1)}, bf16[2,208,128]{2,1,0:T(8,128)(2,1)S(1)}, u32[]{:S(2)}, u32[]{:S(2)}) collective-permute-start(bf16[2,208,128]{2,1,0:T(8,128)(2,1)S(1)} %pad_maximum_fusion.7), channel_id=1, source_target_pairs={{0,4},{1,3},{2,6},{3,1},{4,0},{5,7},{6,2},{7,5},{8,12},{9,11},{10,... | collective-permute-start | bytes 319496 | tf_op jit(solution)/shard_map/ppermute | solution.py:365
  150.9 7.3 %collective-permute-start.27 = (bf16[4,208,128]{2,1,0:T(8,128)(2,1)S(1)}, bf16[4,208,128]{2,1,0:T(8,128)(2,1)S(1)}, u32[]{:S(2)}, u32[]{:S(2)}) collective-permute-start(bf16[4,208,128]{2,1,0:T(8,128)(2,1)S(1)} %pad_maximum_fusion.3), channel_id=1, source_target_pairs={{0,8},{1,17},{2,10},{3,19},{4,12},{5,21},{6,14},{7,23},{8,0},{9,25... | collective-permute-start | bytes 638984 | tf_op jit(solution)/shard_map/ppermute | solution.py:365
  158.2 8.2 %collective-permute-start.28 = (bf16[8,208,128]{2,1,0:T(8,128)(2,1)S(1)}, bf16[8,208,128]{2,1,0:T(8,128)(2,1)S(1)}, u32[]{:S(2)}, u32[]{:S(2)}) collective-permute-start(bf16[8,208,128]{2,1,0:T(8,128)(2,1)S(1)} %pad_maximum_fusion.1), channel_id=1, source_target_pairs={{0,16},{1,9},{2,18},{3,11},{4,20},{5,13},{6,22},{7,15},{8,24},{9,1... | collective-permute-start | bytes 1277960 | tf_op jit(solution)/shard_map/ppermute | solution.py:365
  160.5 6.9 %collective-permute-start.21 = (f32[128,200]{1,0:T(8,128)S(1)}, f32[128,200]{1,0:T(8,128)S(1)}, u32[]{:S(2)}, u32[]{:S(2)}) collective-permute-start(f32[128,200]{1,0:T(8,128)S(1)} %slice.106), channel_id=1, source_target_pairs={{0,1},{1,0},{2,3},{3,2},{4,5},{5,4},{6,7},{7,6},{8,9},{9,8},{10,11... | collective-permute-start | bytes 307208 | tf_op jit(solution)/shard_map/ppermute | solution.py:365
  167.4 16.3 %collective-permute-start.29 = (bf16[16,208,128]{2,1,0:T(8,128)(2,1)}, bf16[16,208,128]{2,1,0:T(8,128)(2,1)}, u32[]{:S(2)}, u32[]{:S(2)}) collective-permute-start(bf16[16,208,128]{2,1,0:T(8,128)(2,1)} %get-tuple-element.52), channel_id=1, source_target_pairs={{0,1},{1,0},{2,3},{3,2},{4,5},{5,4},{6,7},{7,6},{8,9},{9,8},{10,11... | collective-permute-start | bytes 2555912 | tf_op jit(solution)/shard_map/ppermute | solution.py:365
  167.5 5.2 %collective-permute-start.22 = (f32[64,200]{1,0:T(8,128)S(1)}, f32[64,200]{1,0:T(8,128)S(1)}, u32[]{:S(2)}, u32[]{:S(2)}) collective-permute-start(f32[64,200]{1,0:T(8,128)S(1)} %slice.125), channel_id=1, source_target_pairs={{0,4},{1,3},{2,6},{3,1},{4,0},{5,7},{6,2},{7,5},{8,12},{9,11},{10,... | collective-permute-start | bytes 153608 | tf_op jit(solution)/shard_map/ppermute | solution.py:365
  172.7 4.0 %collective-permute-start.23 = (f32[32,200]{1,0:T(8,128)S(1)}, f32[32,200]{1,0:T(8,128)S(1)}, u32[]{:S(2)}, u32[]{:S(2)}) collective-permute-start(f32[32,200]{1,0:T(8,128)S(1)} %slice.127), channel_id=1, source_target_pairs={{0,2},{1,5},{2,0},{3,7},{4,6},{5,1},{6,4},{7,3},{8,10},{9,13},{10,... | collective-permute-start | bytes 76808 | tf_op jit(solution)/shard_map/ppermute | solution.py:365
  172.8 5.5 %collective-permute-start.20 = (f32[128,200]{1,0:T(8,128)S(1)}, f32[128,200]{1,0:T(8,128)S(1)}, u32[]{:S(2)}, u32[]{:S(2)}) collective-permute-start(f32[128,200]{1,0:T(8,128)S(1)} %get-tuple-element.36), channel_id=1, source_target_pairs={{0,16},{1,17},{2,18},{3,19},{4,20},{5,21},{6,22},{7,23},{8,24},{9,... | collective-permute-start | bytes 307208 | tf_op jit(solution)/shard_map/ppermute | solution.py:365
  176.7 3.9 %collective-permute-start.24 = (f32[32,200]{1,0:T(8,128)S(1)}, f32[32,200]{1,0:T(8,128)S(1)}, u32[]{:S(2)}, u32[]{:S(2)}) collective-permute-start(f32[32,200]{1,0:T(8,128)S(1)} %slice_add_fusion.4), channel_id=1, source_target_pairs={{0,16},{1,17},{2,18},{3,19},{4,20},{5,21},{6,22},{7,23},{8,24},{9,... | collective-permute-start | bytes 76808 | tf_op jit(solution)/shard_map/ppermute | solution.py:365
  (23 other events, 285.1 us)

commit v2 on v1

v2 whole, which is shorter than its diff:
```python
import functools

import jax
import jax.numpy as jnp
from jax import lax
from jax.experimental import pallas as pl
from jax.experimental.pallas import tpu as pltpu
from jax.sharding import PartitionSpec as P

EMB_W = 20
D = 200
FILTERS = 32
PIXELS = 400
SIDE = 18
PAIRS = 9
WINDOW = 80
WIDE = 1152
PACK = 208
LANES = 128
ROUNDS = 2

negative_weight = 0.03125
learn_rate = 0.5

f32 = jnp.float32
bf16 = jnp.bfloat16
i32 = jnp.int32
BOTH = ("group", "shard")
VMEM = pl.BlockSpec(memory_space=pltpu.VMEM)
SMEM = pl.BlockSpec(memory_space=pltpu.SMEM)


def shaped(shape, dtype=f32):
    return jax.ShapeDtypeStruct(shape, dtype)


def call(kernel, name, micros, out_shape, args, scratch=(), scalars=0, limit=40):
    return pl.pallas_call(
        kernel,
        out_shape=out_shape,
        in_specs=[SMEM] * scalars + [VMEM] * (len(args) - scalars),
        out_specs=[VMEM] * len(out_shape),
        scratch_shapes=list(scratch),
        compiler_params=pltpu.CompilerParams(vmem_limit_bytes=limit * 1024 * 1024),
        cost_estimate=pl.CostEstimate(
            flops=int(micros * 1e9), bytes_accessed=int(micros * 3e6), transcendentals=0
        ),
        name=name,
    )(*args)


def sigmoid(values):
    return 0.5 * jnp.tanh(0.5 * values) + 0.5


def dot(left, right):
    return jnp.dot(left, right, preferred_element_type=f32)


def dot_nt(left, right):
    return lax.dot_general(left, right, (((1,), (1,)), ((), ())), preferred_element_type=f32)


def dot_tn(left, right):
    return lax.dot_general(left, right, (((0,), (0,)), ((), ())), preferred_element_type=f32)


def as_column(row):
    return jnp.transpose(jnp.broadcast_to(row.astype(f32), (LANES, LANES)))


def hits(names_row, count, first=0):
    spot = lax.broadcasted_iota(i32, (count, names_row.shape[1]), 0) + first
    return jnp.where(spot == names_row, 1.0, 0.0).astype(bf16)


def halves(values):
    high = values.astype(bf16)
    return high, (values - high.astype(f32)).astype(bf16)


def padded(values, lanes):
    rest = lanes - values.shape[1]
    return jnp.concatenate([values, jnp.zeros((values.shape[0], rest), values.dtype)], axis=1)


def turned(values):
    rows = values.shape[0]
    if rows < LANES:
        values = jnp.concatenate([values, jnp.zeros((LANES - rows, values.shape[1]), f32)], axis=0)
    return jnp.transpose(values)


def wanted_kernel(tails_ref, negatives_ref, *outs):
    for index, out in enumerate(outs):
        out[0:1, :] = tails_ref[index : index + 1, :]
        out[1:2, :] = padded(negatives_ref[index : index + 1, :], LANES)


def pick_answer(table, ids_ref, negatives, out):
    count = table.shape[1]
    number = out.shape[0] - negatives
    tails = dot(table, hits(ids_ref[0:1, :], count))
    out[:number, :] = jnp.transpose(tails).astype(bf16)
    negs = dot(table, hits(ids_ref[1:2, :], count))
    out[number:, :] = jnp.transpose(negs)[:negatives, :].astype(bf16)


def answer_kernel(negatives, ids_ref, ent_ref, out):
    pick_answer(ent_ref[...].astype(bf16), ids_ref, negatives, out)


def prepare_kernel(fc_ref, taps_ref, fc_out, band_out, band_t_out, left, right):
    blank = jnp.zeros((2 * LANES - D, LANES), f32)
    for index in range(fc_ref.shape[1] // LANES):
        at = slice(index * LANES, (index + 1) * LANES)
        block = fc_ref[:, at].astype(f32)
        left[at, :] = jnp.transpose(block[:LANES])
        right[at, :] = jnp.transpose(jnp.concatenate([block[LANES:], blank], axis=0))
    spots = SIDE * SIDE

    def regroup(index, carry):
        low = left[pl.ds(index, FILTERS, stride=spots), :]
        high = right[pl.ds(index, FILTERS, stride=spots), :]
        at = pl.ds(pl.multiple_of(index * FILTERS, FILTERS), FILTERS)
        fc_out[at, :LANES] = low.astype(bf16)
        fc_out[at, LANES:] = high[:, : D - LANES].astype(bf16)
        return carry

    lax.fori_loop(0, spots, regroup, 0, unroll=9)
    group = lax.broadcasted_iota(i32, (WINDOW, WIDE), 1) >> 5
    start = group + jnp.where(group >= SIDE, EMB_W - SIDE, 0)
    gap = lax.broadcasted_iota(i32, (WINDOW, WIDE), 0) - start
    band = jnp.zeros((WINDOW, WIDE), f32)
    for row_off in range(3):
        for col_off in range(3):
            tap = row_off * 3 + col_off
            hit = gap == EMB_W * row_off + col_off
            band = jnp.where(hit, taps_ref[tap : tap + 1, :], band)
    band_out[...] = band.astype(bf16)
    band_t_out[...] = jnp.transpose(
        jnp.concatenate([band, jnp.zeros((LANES - WINDOW, WIDE), f32)], axis=0)
    ).astype(bf16)


def rows_kernel(ids_ref, rel_ref, state_ref, first_out, later_out, state_out, table):
    count = rel_ref.shape[1]
    whole = count // LANES * LANES
    table[:, :whole] = rel_ref[:, :whole]
    rest = jnp.concatenate(
        [rel_ref[:, whole:], jnp.zeros((D, LANES - count + whole), f32)], axis=1
    )
    table[:, whole:] = rest
    values = table[...]
    wide = values.shape[1]
    high = values.astype(bf16)
    first_out[...] = dot(high, hits(ids_ref[0:1, :], wide))
    left = values - high.astype(f32)
    middle = left.astype(bf16)
    low = (left - middle.astype(f32)).astype(bf16)
    hit = hits(ids_ref[1:2, :], wide)
    later_out[...] = dot(high, hit) + dot(middle, hit) + dot(low, hit)
    sums = padded(state_ref[...], wide)
    column = lax.broadcasted_iota(i32, (wide // LANES, LANES, LANES), 1)
    names = ids_ref[1:2, :]
    total = jnp.zeros((LANES, LANES), f32)
    for block in range(wide // LANES):
        states = as_column(sums[:, block * LANES : (block + 1) * LANES])
        spot = lax.broadcasted_iota(i32, (LANES, LANES), 0) + block * LANES
        total = total + jnp.where(spot == names, states, 0.0)
    state_out[...] = jnp.sum(total, axis=0, keepdims=True)


def pass_kernel(
    round_index, heads_ref, relations_ref, ent_ref, *refs
):
    if round_index == 0:
        rel_rows = refs[0][...]
        refs = refs[1:]
    else:
        gradient = (refs[0][...] + refs[1][...])[:D, :]
        state = refs[3][...] + jnp.mean(gradient * gradient, axis=0, keepdims=True)
        rel_rows = refs[2][...] - gradient * (learn_rate * lax.rsqrt(state))
        rel_rows = rel_rows.astype(bf16).astype(f32)
        refs = refs[4:]
    tail_ref, neg_ref, band_ref, band_t_ref, bias_ref, fc_ref, fcb_ref = refs[:7]
    pack_out, head_out, tail_out, neg_out, picture, slopes, work, total = refs[7:]
    heads = heads_ref[round_index : round_index + 1, :]
    relations = relations_ref[round_index : round_index + 1, :]
    table = ent_ref[...].astype(bf16)
    picture[:D, :] = dot(table, hits(heads, table.shape[1]))
    picture[D:, :] = rel_rows
    number = LANES
    pre2 = jnp.zeros((number, D), f32)
    for pair in range(PAIRS):
        first = pair * 2 * EMB_W
        window = jnp.transpose(picture[first : first + WINDOW, :]).astype(bf16)
        pre1 = dot(window, band_ref[...]) + bias_ref[...]
        sigma = sigmoid(pre1)
        act = pre1 * sigma
        slopes[pair] = sigma + act * (1.0 - sigma)
        work[pair] = act.astype(bf16)
        pre2 = pre2 + dot(work[pair], fc_ref[pair])
    pre2 = pre2 + fcb_ref[...]
    sigma = sigmoid(pre2)
    value = pre2 * sigma
    slope2 = sigma + value * (1.0 - sigma)
    query = value.astype(bf16)
    query32 = query.astype(f32)
    tails = tail_ref[...].astype(f32)
    pos_grad = -sigmoid(-jnp.sum(query32 * tails, axis=1, keepdims=True))
    negset = neg_ref[...]
    neg_grad = (negative_weight * sigmoid(dot_nt(query, negset))).astype(bf16)
    query_grad = pos_grad * tails + dot(neg_grad, negset)
    pre2_grad = (query_grad * slope2).astype(bf16)
    tail_out[...] = jnp.transpose(pos_grad * query32)
    neg_out[...] = dot_tn(neg_grad, query)
    total[...] = jnp.zeros_like(total)
    for pair in range(PAIRS):
        act_grad = dot_nt(pre2_grad, fc_ref[pair])
        work[pair] = (act_grad * slopes[pair]).astype(bf16)
        part = dot(work[pair], band_t_ref[...])
        at = slice(pair * 2 * EMB_W, pair * 2 * EMB_W + WINDOW)
        total[at, :] = total[at, :] + jnp.transpose(part)[:WINDOW, :]
    head_out[...] = total[:D, :]
    high = relations >> 6
    low = relations - (high << 6)
    spare = lax.broadcasted_iota(i32, (PACK - D, number), 0)
    codes = jnp.where(spare == 0, high, jnp.where(spare == 1, low, 0)).astype(f32)
    pack_out[...] = jnp.concatenate([total[D:, :], codes], axis=0).astype(bf16)


def entity_kernel(
    round_index, heads_ref, asked_ref, next_ref, ent_ref, state_ref, head_ref, tail_ref, neg_ref, *outs
):
    count = ent_ref.shape[1]
    grads = jnp.concatenate([head_ref[...], tail_ref[...], turned(neg_ref[...])], axis=1)
    high, low = halves(grads)
    named = jnp.concatenate(
        [heads_ref[round_index : round_index + 1, :], asked_ref[0:1, :], asked_ref[1:2, :]], axis=1
    )
    both = dot_nt(jnp.concatenate([high, low], axis=0), hits(named, count))
    gradient = both[:D, :] + both[D:, :]
    state = state_ref[...] + jnp.mean(gradient * gradient, axis=0, keepdims=True)
    rows = ent_ref[...] - gradient * (learn_rate * lax.rsqrt(state))
    outs[0][...] = rows
    outs[1][...] = state
    if len(outs) > 2:
        pick_answer(rows.astype(bf16), next_ref, neg_ref.shape[0], outs[2])


def lay_packs(place_ref, mine_ref, other_ref, grads, names):
    half = mine_ref.shape[0]
    for index in range(2 * half):
        spot = place_ref[index]
        at = slice(index * LANES, (index + 1) * LANES)
        inner = lax.rem(spot, half)
        block = jnp.where(spot < half, mine_ref[inner].astype(f32), other_ref[inner].astype(f32))
        grads[:, at] = block.astype(bf16)
        names[0:1, at] = (block[D : D + 1, :] * 64.0 + block[D + 1 : D + 2, :]).astype(i32)


def need_kernel(round_index, place_ref, mine_ref, other_ref, ids_ref, others_ref, own_out, send_out, grads, names):
    lay_packs(place_ref, mine_ref, other_ref, grads, names)
    wide = names.shape[1]
    for ids, out in ((ids_ref, own_out), (others_ref, send_out)):
        column = as_column(ids[round_index : round_index + 1, :])
        hit = jnp.concatenate(
            [
                jnp.where(
                    column == names[0:1, at : at + LANES].astype(f32), 1.0, 0.0
                ).astype(bf16)
                for at in range(0, wide, LANES)
            ],
            axis=1,
        )
        out[...] = jnp.transpose(dot_nt(hit, grads[...]))


def sums_kernel(place_ref, mine_ref, other_ref, out, grads, names):
    lay_packs(place_ref, mine_ref, other_ref, grads, names)
    for first in range(0, out.shape[1], LANES):
        out[:, first : first + LANES] = dot_nt(grads[...], hits(names[0:1, :], LANES, first))[:D, :]


def relation_kernel(rel_ref, state_ref, *refs):
    rows = rel_ref[...]
    state = state_ref[...]
    count = rows.shape[1]
    for index in range(ROUNDS):
        gradient = refs[2 * index][:, :count] + refs[2 * index + 1][:, :count]
        state = state + jnp.mean(gradient * gradient, axis=0, keepdims=True)
        rows = rows - gradient * (learn_rate * lax.rsqrt(state))
    refs[2 * ROUNDS][...] = rows
    refs[2 * ROUNDS + 1][...] = state


def swapped(bits):
    out = list(bits)
    for index in range(0, len(out) - 1, 2):
        out[index], out[index + 1] = out[index + 1], out[index]
    return out


class Plan:
    def __init__(self, groups, shards):
        self.total = groups * shards
        self.shards = shards
        near = [1 << bit for bit in range(1, shards.bit_length() - 1)]
        far = [shards << bit for bit in range(groups.bit_length() - 1)]
        self.even = near + far
        self.odd = swapped(near) + swapped(far)
        self.across = [self.route(a, b) for a, b in zip(self.even, self.odd)]
        self.core = self.route(1, 1)
        self.within = self.across[: len(near)] + [self.core]

    def route(self, even, odd):
        return [(at, at ^ (odd if at & 1 else even)) for at in range(self.total)]

    def partner(self, bit):
        mask = self.shards << bit
        return self.route(mask, mask)

    def places(self, me):
        source = jnp.arange(0, self.total, 2, dtype=i32)
        differ = source ^ me
        even = jnp.zeros_like(source)
        odd = jnp.zeros_like(source)
        for step, (one, other) in enumerate(zip(self.even, self.odd)):
            even = even + jnp.where((differ & one) != 0, 1 << step, 0)
            odd = odd + jnp.where((differ & other) != 0, 1 << step, 0)
        return jnp.where((me & 1) == 0, even, odd)


def send(block, route):
    return lax.ppermute(block, BOTH, route)


def doubled(block, routes):
    for route in routes:
        block = jnp.concatenate([block, send(block, route)], axis=0)
    return block


def halved(block, routes):
    for route in reversed(routes):
        half = block.shape[0] // 2
        block = block[:half] + send(block[half:], route)
    return block


def shards(
    plan,
    entity_rows,
    entity_state,
    relation_rows,
    relation_state,
    conv_weight,
    conv_bias,
    fc_weight,
    fc_bias,
    head_ids,
    rel_ids,
    tail_ids,
    neg_ids,
):
    number = head_ids.shape[1]
    negatives = neg_ids.shape[1]
    count = relation_rows.shape[0]
    wide = count + -count % LANES
    sources = plan.total // 2
    me = lax.axis_index("group") * plan.shards + lax.axis_index("shard")
    ent = entity_rows.T
    ent_state = entity_state[None, :]
    rel = relation_rows.T
    rel_state = relation_state[None, :]

    wanted = call(
        wanted_kernel, "wanted", 1, [shaped((2, LANES), i32)] * ROUNDS, (tail_ids, neg_ids)
    )
    requested = [send(wanted[r], plan.partner(r)) for r in range(ROUNDS)]
    rel_others = send(rel_ids, plan.core)
    answer_shape = shaped((number + negatives, D), bf16)
    (answer,) = call(
        functools.partial(answer_kernel, negatives), "answer", 1, [answer_shape], (requested[0], ent)
    )
    taps = jnp.tile(conv_weight.reshape(FILTERS, 9).T.astype(f32), (1, WIDE // FILTERS))
    bias = jnp.tile(conv_bias[None, :], (1, WIDE // FILTERS))
    features = fc_weight.shape[0]
    fc, band, band_t = call(
        prepare_kernel,
        "prepare",
        5,
        [shaped((features, D), bf16), shaped((WINDOW, WIDE), bf16), shaped((WIDE, LANES), bf16)],
        (fc_weight.T, taps),
        [pltpu.VMEM((features, LANES), f32), pltpu.VMEM((features, LANES), f32)],
    )
    fc = fc.reshape(PAIRS, WIDE, D)
    rel_first, rel_later, state_later = call(
        rows_kernel,
        "relation_rows",
        2,
        [shaped((D, number)), shaped((D, number)), shaped((1, number))],
        (rel_ids, rel, rel_state),
        [pltpu.VMEM((D, wide), f32)],
    )
    rel_inputs = (rel_first,)
    place = plan.places(me)
    lay = [pltpu.VMEM((PACK, sources * LANES), bf16), pltpu.VMEM((8, sources * LANES), i32)]

    sums = []
    for r in range(ROUNDS):
        last = r == ROUNDS - 1
        answered = send(answer, plan.partner(r))
        negset = doubled(answered[number:], plan.within)
        pack, head_grad, tail_grad, neg_part = call(
            functools.partial(pass_kernel, r),
            "local_pass",
            6,
            [
                shaped((PACK, number), bf16),
                shaped((D, number)),
                shaped((D, number)),
                shaped((negset.shape[0], D)),
            ],
            (head_ids, rel_ids, ent, *rel_inputs, answered[:number], negset, band, band_t, bias, fc, fc_bias[None, :]),
            [
                pltpu.VMEM((PIXELS, number), f32),
                pltpu.VMEM((PAIRS, number, WIDE), f32),
                pltpu.VMEM((PAIRS, number, WIDE), bf16),
                pltpu.VMEM((PIXELS, number), f32),
            ],
        )
        packs = doubled(pack[None], plan.across[:-1])
        arrived = send(packs, plan.across[-1])
        tail_back = send(tail_grad, plan.partner(r))
        neg_back = send(halved(neg_part, plan.within), plan.partner(r))
        if not last:
            own, partial = call(
                functools.partial(need_kernel, r + 1),
                "need",
                1.5,
                [shaped((PACK, number))] * 2,
                (place, packs, arrived, rel_ids, rel_others),
                lay,
                scalars=1,
            )
            rel_inputs = (own, send(partial, plan.core), rel_later, state_later)
        out_shape = [shaped(ent.shape), shaped(ent_state.shape)]
        outs = call(
            functools.partial(entity_kernel, r),
            "entity_update",
            2,
            out_shape if last else out_shape + [answer_shape],
            (head_ids, requested[r], requested[min(r + 1, ROUNDS - 1)], ent, ent_state, head_grad, tail_back, neg_back),
        )
        ent, ent_state = outs[:2]
        if not last:
            answer = outs[2]
        (part,) = call(
            sums_kernel, "relation_sums", 3, [shaped((D, wide))], (place, packs, arrived), lay, scalars=1
        )
        sums += [part, send(part, plan.core)]
    rel, rel_state = call(
        relation_kernel, "relation_update", 2, [shaped((D, count)), shaped((1, count))], (rel, rel_state, *sums)
    )
    return (ent.T, ent_state.reshape(-1), rel.T, rel_state.reshape(-1))


def solution(mesh):
    plan = Plan(mesh.shape["group"], mesh.shape["shard"])
    in_specs = (
        P(BOTH, None),
        P(BOTH),
        P(),
        P(),
        P(),
        P(),
        P(),
        P(),
        P(None, BOTH),
        P(None, BOTH),
        P(None, BOTH),
        P(None, BOTH),
    )
    out_specs = (P(BOTH, None), P(BOTH), P(), P())
    return jax.shard_map(
        functools.partial(shards, plan),
        mesh=mesh,
        in_specs=in_specs,
        out_specs=out_specs,
        check_vma=False,
    )
```

time: 202 us -> 137 us (0.68)
  Pallas kernels: 71.5 us -> 28.9 us
  local copies, waits for them, and re-layouts: 33.8 us -> 11.1 us
  starting transfers between devices: 37.8 us -> 24 us
  waiting for transfers between devices: 57 us -> 70.4 us
    pallas_call x7 -> x12, Pallas kernels: 71.5 us -> 28.9 us  [call(): pl.pallas_call(kernel, out_shape=out_shape, in_specs=[SMEM] * scalars + [...]
    ppermute x30 -> x32, starting transfers between devices: 37.8 us -> 24 us  [send(): return lax.ppermute(block, BOTH, route)]
    ppermute x30 -> x32, waiting for transfers between devices: 57 us -> 70.4 us  [send(): return lax.ppermute(block, BOTH, route)]
    unnamed x64 -> x34, local copies, waits for them, and re-layouts: 23.1 us -> 10.8 us
    concatenate x7 -> x0, local copies, waits for them, and re-layouts: 7.63 us -> none  [the longest x4 6.14 us: doubled(): block = jnp.concatenate([block, send(block, route)], axis=0)]
  transfers between devices with their start and end apart: 30 -> 32, of which waited for: 19 -> 21; matrix products, arithmetic and copies ran while one was open for 11% -> 0% of each run, Pallas kernels for 4% -> 11%
where the time goes in v2:
time: 137 us; the launch traced here: 136 us
  waiting for transfers between devices  70.4 us (51%)
  Pallas kernels  28.9 us (21%)
  starting transfers between devices  24 us (18%)
  local copies, waits for them, and re-layouts  11.1 us (8%)
    ppermute x32, waiting for transfers between devices, send(): return lax.ppermute(block, BOTH, route)  70.4 us
    pallas_call x12, Pallas kernels, call(): pl.pallas_call(kernel, out_shape=out_shape, in_specs=[SMEM] * scalars + [...  28.9 us
    ppermute x32, starting transfers between devices, send(): return lax.ppermute(block, BOTH, route)  24 us
    unnamed x34, local copies, waits for them, and re-layouts  10.8 us
  transfers between devices with their start and end apart: 32, of which 21 were waited for; matrix products, arithmetic and copies ran while one was open for 0% of the time, Pallas kernels for 11%

profile of v2, /device:TPU:0, one launch (start us, length us, event | category | flops | bytes accessed | tf_op | source)
XLA Modules:
  0.0 136.3 jit_solution(1572956443944445821)
XLA Ops:
  2.1 2.9 %collective-permute-start.1 = (s32[2,128]{1,0:T(2,128)S(1)}, s32[2,128]{1,0:T(2,128)S(1)}, u32[]{:S(2)}, u32[]{:S(2)}) collective-permute-start(s32[2,128]{1,0:T(2,128)S(1)} %get-tuple-element.30), channel_id=1, source_target_pairs={{0,8},{1,9},{2,10},{3,11},{4,12},{5,13},{6,14},{7,15},{8,0},{9,1},... | collective-permute-start | bytes 3080 | tf_op jit(solution)/shard_map/ppermute | solution.py:336
  7.0 2.1 %collective-permute-start.2 = (bf16[160,200]{1,0:T(8,128)(2,1)S(1)}, bf16[160,200]{1,0:T(8,128)(2,1)S(1)}, u32[]{:S(2)}, u32[]{:S(2)}) collective-permute-start(bf16[160,200]{1,0:T(8,128)(2,1)S(1)} %answer.1), channel_id=1, source_target_pairs={{0,8},{1,9},{2,10},{3,11},{4,12},{5,13},{6,14},{7,15},{8,0},{9,1},... | collective-permute-start | bytes 192008 | tf_op jit(solution)/shard_map/ppermute | solution.py:336
  9.1 2.4 %collective-permute-done.2 = bf16[160,200]{1,0:T(8,128)(2,1)S(1)} collective-permute-done((bf16[160,200]{1,0:T(8,128)(2,1)S(1)}, bf16[160,200]{1,0:T(8,128)(2,1)S(1)}, u32[]{:S(2)}, u32[]{:S(2)}) %collective-permute-start.2) | collective-permute-done | bytes 64032 | tf_op jit(solution)/shard_map/ppermute | solution.py:336
  11.5 2.1 %collective-permute-start.3 = (bf16[32,200]{1,0:T(8,128)(2,1)S(1)}, bf16[32,200]{1,0:T(8,128)(2,1)S(1)}, u32[]{:S(2)}, u32[]{:S(2)}) collective-permute-start(bf16[32,200]{1,0:T(8,128)(2,1)S(1)} %slice.65), channel_id=1, source_target_pairs={{0,2},{1,5},{2,0},{3,7},{4,6},{5,1},{6,4},{7,3},{8,10},{9,13},{10,... | collective-permute-start | bytes 38408 | tf_op jit(solution)/shard_map/ppermute | solution.py:336
  13.7 1.6 %collective-permute-done.3 = bf16[32,200]{1,0:T(8,128)(2,1)S(1)} collective-permute-done((bf16[32,200]{1,0:T(8,128)(2,1)S(1)}, bf16[32,200]{1,0:T(8,128)(2,1)S(1)}, u32[]{:S(2)}, u32[]{:S(2)}) %collective-permute-start.3) | collective-permute-done | bytes 12832 | tf_op jit(solution)/shard_map/ppermute | solution.py:336
  15.3 3.1 %collective-permute-start.4 = (bf16[64,200]{1,0:T(8,128)(2,1)S(1)}, bf16[64,200]{1,0:T(8,128)(2,1)S(1)}, u32[]{:S(2)}, u32[]{:S(2)}) collective-permute-start(bf16[64,200]{1,0:T(8,128)(2,1)S(1)} %pad_maximum_fusion.10), channel_id=1, source_target_pairs={{0,4},{1,3},{2,6},{3,1},{4,0},{5,7},{6,2},{7,5},{8,12},{9,11},{10,... | collective-permute-start | bytes 76808 | tf_op jit(solution)/shard_map/ppermute | solution.py:336
  18.4 2.2 %copy-done = bf16[10368,200]{0,1:T(8,128)(2,1)S(1)} copy-done((bf16[10368,200]{0,1:T(8,128)(2,1)S(1)}, bf16[10368,200]{0,1:T(8,128)(2,1)}, u32[]{:S(2)}) %copy-start) | copy-done | bytes 4147224
  20.6 3.1 %prepare.1 = (bf16[10368,200]{1,0:T(8,128)(2,1)S(1)}, bf16[80,1152]{1,0:T(8,128)(2,1)S(1)}, bf16[1152,128]{1,0:T(8,128)(2,1)S(1)}) custom-call(bf16[200,10368]{1,0:T(8,128)(2,1)S(1)} %bitcast.22, f32[9,1152]{1,0:T(8,128)S(1)} %tile.18.taps_ref), custom_call_target="tpu_custom_call" | custom-call | flops 5000000000 | bytes 15000000 | tf_op jit(solution)/shard_map/prepare/pallas_call | solution.py:38
  26.3 2.5 %copy-done.10 = bf16[10368,200]{1,0:T(8,128)(2,1)S(1)} copy-done((bf16[10368,200]{1,0:T(8,128)(2,1)S(1)}, bf16[10368,200]{1,0:T(8,128)(2,1)}, u32[]{:S(2)}) %copy-start.10) | copy-done | bytes 4147224
  28.8 5.8 %local_pass.2 = (bf16[208,128]{1,0:T(8,128)(2,1)S(1)}, f32[200,128]{1,0:T(8,128)S(1)}, f32[200,128]{1,0:T(8,128)S(1)}, f32[256,200]{1,0:T(8,128)S(1)}) custom-call(s32[2,128]{1,0:T(2,128)S(1)} %copy-done.8, s32[2,128]{1,0:T(2,128)S(1)} %copy-done.6, f32[200,1024]{1,0:T(8,128)S(1)} %bitcast.26, f32[200,128]{1,0:T(8,128)S(1)} %get-tuple-element.31.refs_0_, ...), custom_call_target="tpu_custom_call" | custom-call | flops 6000000000 | bytes 18000000 | tf_op jit(solution)/shard_map/local_pass/pallas_call | solution.py:38
  34.7 1.6 %collective-permute-start = (s32[2,128]{1,0:T(2,128)S(1)}, s32[2,128]{1,0:T(2,128)S(1)}, u32[]{:S(2)}, u32[]{:S(2)}) collective-permute-start(s32[2,128]{1,0:T(2,128)S(1)} %get-tuple-element.29), channel_id=1, source_target_pairs={{0,16},{1,17},{2,18},{3,19},{4,20},{5,21},{6,22},{7,23},{8,24},{9,... | collective-permute-start | bytes 3080 | tf_op jit(solution)/shard_map/ppermute | solution.py:336
  39.7 2.5 %collective-permute-done.11 = bf16[1,208,128]{2,1,0:T(8,128)(2,1)S(1)} collective-permute-done((bf16[1,208,128]{2,1,0:T(8,128)(2,1)S(1)}, bf16[1,208,128]{2,1,0:T(8,128)(2,1)S(1)}, u32[]{:S(2)}, u32[]{:S(2)}) %collective-permute-start.11) | collective-permute-done | bytes 53280 | tf_op jit(solution)/shard_map/ppermute | solution.py:336
  42.4 2.8 %collective-permute-done.8 = f32[64,200]{1,0:T(8,128)S(1)} collective-permute-done((f32[64,200]{1,0:T(8,128)S(1)}, f32[64,200]{1,0:T(8,128)S(1)}, u32[]{:S(2)}, u32[]{:S(2)}) %collective-permute-start.8) | collective-permute-done | bytes 51232 | tf_op jit(solution)/shard_map/ppermute | solution.py:336
  45.3 4.1 %collective-permute-done.12 = bf16[2,208,128]{2,1,0:T(8,128)(2,1)S(1)} collective-permute-done((bf16[2,208,128]{2,1,0:T(8,128)(2,1)S(1)}, bf16[2,208,128]{2,1,0:T(8,128)(2,1)S(1)}, u32[]{:S(2)}, u32[]{:S(2)}) %collective-permute-start.12) | collective-permute-done | bytes 106528 | tf_op jit(solution)/shard_map/ppermute | solution.py:336
  51.6 5.8 %collective-permute-done.13 = bf16[4,208,128]{2,1,0:T(8,128)(2,1)S(1)} collective-permute-done((bf16[4,208,128]{2,1,0:T(8,128)(2,1)S(1)}, bf16[4,208,128]{2,1,0:T(8,128)(2,1)S(1)}, u32[]{:S(2)}, u32[]{:S(2)}) %collective-permute-start.13) | collective-permute-done | bytes 213024 | tf_op jit(solution)/shard_map/ppermute | solution.py:336
  61.6 4.9 %collective-permute-done.17 = bf16[160,200]{1,0:T(8,128)(2,1)S(1)} collective-permute-done((bf16[160,200]{1,0:T(8,128)(2,1)S(1)}, bf16[160,200]{1,0:T(8,128)(2,1)S(1)}, u32[]{:S(2)}, u32[]{:S(2)}) %collective-permute-start.17) | collective-permute-done | bytes 64032 | tf_op jit(solution)/shard_map/ppermute | solution.py:336
  66.5 3.9 %collective-permute-done.18 = bf16[32,200]{1,0:T(8,128)(2,1)S(1)} collective-permute-done((bf16[32,200]{1,0:T(8,128)(2,1)S(1)}, bf16[32,200]{1,0:T(8,128)(2,1)S(1)}, u32[]{:S(2)}, u32[]{:S(2)}) %collective-permute-start.18) | collective-permute-done | bytes 12832 | tf_op jit(solution)/shard_map/ppermute | solution.py:336
  70.7 4.6 %collective-permute-done.19 = bf16[64,200]{1,0:T(8,128)(2,1)S(1)} collective-permute-done((bf16[64,200]{1,0:T(8,128)(2,1)S(1)}, bf16[64,200]{1,0:T(8,128)(2,1)S(1)}, u32[]{:S(2)}, u32[]{:S(2)}) %collective-permute-start.19) | collective-permute-done | bytes 25632 | tf_op jit(solution)/shard_map/ppermute | solution.py:336
  78.4 2.5 %copy-done.11 = bf16[10368,200]{1,0:T(8,128)(2,1)S(1)} copy-done((bf16[10368,200]{1,0:T(8,128)(2,1)S(1)}, bf16[10368,200]{1,0:T(8,128)(2,1)}, u32[]{:S(2)}) %copy-start.11) | copy-done | bytes 4147224
  80.9 6.0 %local_pass.3 = (bf16[208,128]{1,0:T(8,128)(2,1)S(1)}, f32[200,128]{1,0:T(8,128)S(1)}, f32[200,128]{1,0:T(8,128)S(1)}, f32[256,200]{1,0:T(8,128)S(1)}) custom-call(s32[2,128]{1,0:T(2,128)S(1)} %copy-done.8, s32[2,128]{1,0:T(2,128)S(1)} %copy-done.6, f32[200,1024]{1,0:T(8,128)S(1)} %copy-done.13, f32[208,128]{1,0:T(8,128)S(1)} %get-tuple-element.41.refs_0_, ...), custom_call_target="tpu_custom_call" | custom-call | flops 6000000000 | bytes 18000000 | tf_op jit(solution)/shard_map/local_pass/pallas_call | solution.py:38
  86.9 4.7 %collective-permute-done.27 = bf16[1,208,128]{2,1,0:T(8,128)(2,1)S(1)} collective-permute-done((bf16[1,208,128]{2,1,0:T(8,128)(2,1)S(1)}, bf16[1,208,128]{2,1,0:T(8,128)(2,1)S(1)}, u32[]{:S(2)}, u32[]{:S(2)}) %collective-permute-start.27) | collective-permute-done | bytes 53280 | tf_op jit(solution)/shard_map/ppermute | solution.py:336
  91.8 5.7 %collective-permute-done.28 = bf16[2,208,128]{2,1,0:T(8,128)(2,1)S(1)} collective-permute-done((bf16[2,208,128]{2,1,0:T(8,128)(2,1)S(1)}, bf16[2,208,128]{2,1,0:T(8,128)(2,1)S(1)}, u32[]{:S(2)}, u32[]{:S(2)}) %collective-permute-start.28) | collective-permute-done | bytes 106528 | tf_op jit(solution)/shard_map/ppermute | solution.py:336
  98.2 6.3 %collective-permute-done.29 = bf16[4,208,128]{2,1,0:T(8,128)(2,1)S(1)} collective-permute-done((bf16[4,208,128]{2,1,0:T(8,128)(2,1)S(1)}, bf16[4,208,128]{2,1,0:T(8,128)(2,1)S(1)}, u32[]{:S(2)}, u32[]{:S(2)}) %collective-permute-start.29) | collective-permute-done | bytes 213024 | tf_op jit(solution)/shard_map/ppermute | solution.py:336
  105.1 3.3 %relation_sums.2.refs_0_ = f32[200,1408]{1,0:T(8,128)S(1)} custom-call(s32[16]{0:T(128)S(1)} %broadcast_select_fusion.place_ref, bf16[8,208,128]{2,1,0:T(8,128)(2,1)S(1)} %pad_maximum_fusion.mine_ref, bf16[8,208,128]{2,1,0:T(8,128)(2,1)S(1)} %collective-permute-done.14.other_ref), custom_call_target="tpu_custom_call" | custom-call | flops 3000000000 | bytes 9000000 | tf_op jit(solution)/shard_map/relation_sums/pallas_call | solution.py:38
  108.5 4.2 %collective-permute-done.30.other_ref = bf16[8,208,128]{2,1,0:T(8,128)(2,1)S(1)} collective-permute-done((bf16[8,208,128]{2,1,0:T(8,128)(2,1)S(1)}, bf16[8,208,128]{2,1,0:T(8,128)(2,1)S(1)}, u32[]{:S(2)}, u32[]{:S(2)}) %collective-permute-start.30) | collective-permute-done | bytes 426016 | tf_op jit(solution)/shard_map/ppermute | solution.py:336
  112.7 3.3 %relation_sums.3.refs_2_ = f32[200,1408]{1,0:T(8,128)S(1)} custom-call(s32[16]{0:T(128)S(1)} %broadcast_select_fusion.place_ref, bf16[8,208,128]{2,1,0:T(8,128)(2,1)S(1)} %pad_maximum_fusion.1.mine_ref, bf16[8,208,128]{2,1,0:T(8,128)(2,1)S(1)} %collective-permute-done.30.other_ref), custom_call_target="tpu_custom_call" | custom-call | flops 3000000000 | bytes 9000000 | tf_op jit(solution)/shard_map/relation_sums/pallas_call | solution.py:38
  116.7 2.4 %collective-permute-done.22 = f32[128,200]{1,0:T(8,128)S(1)} collective-permute-done((f32[128,200]{1,0:T(8,128)S(1)}, f32[128,200]{1,0:T(8,128)S(1)}, u32[]{:S(2)}, u32[]{:S(2)}) %collective-permute-start.22) | collective-permute-done | bytes 102432 | tf_op jit(solution)/shard_map/ppermute | solution.py:336
  119.2 5.2 %collective-permute-done.23 = f32[64,200]{1,0:T(8,128)S(1)} collective-permute-done((f32[64,200]{1,0:T(8,128)S(1)}, f32[64,200]{1,0:T(8,128)S(1)}, u32[]{:S(2)}, u32[]{:S(2)}) %collective-permute-start.23) | collective-permute-done | bytes 51232 | tf_op jit(solution)/shard_map/ppermute | solution.py:336
  125.1 3.3 %collective-permute-done.24 = f32[32,200]{1,0:T(8,128)S(1)} collective-permute-done((f32[32,200]{1,0:T(8,128)S(1)}, f32[32,200]{1,0:T(8,128)S(1)}, u32[]{:S(2)}, u32[]{:S(2)}) %collective-permute-start.24) | collective-permute-done | bytes 25632 | tf_op jit(solution)/shard_map/ppermute | solution.py:336
  129.3 3.0 %collective-permute-done.25.neg_ref = f32[32,200]{1,0:T(8,128)S(1)} collective-permute-done((f32[32,200]{1,0:T(8,128)S(1)}, f32[32,200]{1,0:T(8,128)S(1)}, u32[]{:S(2)}, u32[]{:S(2)}) %collective-permute-start.25) | collective-permute-done | bytes 25632 | tf_op jit(solution)/shard_map/ppermute | solution.py:336
  132.3 1.7 %entity_update.3 = (f32[200,1024]{1,0:T(8,128)}, f32[1,1024]{1,0:T(1,128)}) custom-call(s32[2,128]{1,0:T(2,128)S(1)} %copy-done.8, s32[2,128]{1,0:T(2,128)S(1)} %collective-permute-done.next_ref.asked_ref, s32[2,128]{1,0:T(2,128)S(1)} %collective-permute-done.next_ref.asked_ref, f32[200,1024]{1,0:T(8,128)S(1)} %copy-done.13, ...), custom_call_target="tpu_custom_call" | custom-call | flops 2000000000 | bytes 6000000 | tf_op jit(solution)/shard_map/entity_update/pallas_call | solution.py:38
  134.0 1.7 %relation_update.1 = (f32[200,1387]{1,0:T(8,128)}, f32[1,1387]{1,0:T(1,128)S(1)}) custom-call(f32[200,1387]{1,0:T(8,128)S(1)} %bitcast.24, f32[1,1387]{1,0:T(1,128)S(1)} %broadcast_in_dim.37.state_ref, f32[200,1408]{1,0:T(8,128)S(1)} %relation_sums.2.refs_0_, f32[200,1408]{1,0:T(8,128)S(1)} %collective-permute-done.26.refs_1_, ...), custom_call_target="tpu_custom_call" | custom-call | flops 2000000000 | bytes 6000000 | tf_op jit(solution)/shard_map/relation_update/pallas_call | solution.py:38
  (114 shorter events, 24.0 us)
Async XLA Ops:
  2.1 4.5 %collective-permute-start.1 = (s32[2,128]{1,0:T(2,128)S(1)}, s32[2,128]{1,0:T(2,128)S(1)}, u32[]{:S(2)}, u32[]{:S(2)}) collective-permute-start(s32[2,128]{1,0:T(2,128)S(1)} %get-tuple-element.30), channel_id=1, source_target_pairs={{0,8},{1,9},{2,10},{3,11},{4,12},{5,13},{6,14},{7,15},{8,0},{9,1},... | collective-permute-start | bytes 3080 | tf_op jit(solution)/shard_map/ppermute | solution.py:336
  7.0 4.5 %collective-permute-start.2 = (bf16[160,200]{1,0:T(8,128)(2,1)S(1)}, bf16[160,200]{1,0:T(8,128)(2,1)S(1)}, u32[]{:S(2)}, u32[]{:S(2)}) collective-permute-start(bf16[160,200]{1,0:T(8,128)(2,1)S(1)} %answer.1), channel_id=1, source_target_pairs={{0,8},{1,9},{2,10},{3,11},{4,12},{5,13},{6,14},{7,15},{8,0},{9,1},... | collective-permute-start | bytes 192008 | tf_op jit(solution)/shard_map/ppermute | solution.py:336
  11.5 3.8 %collective-permute-start.3 = (bf16[32,200]{1,0:T(8,128)(2,1)S(1)}, bf16[32,200]{1,0:T(8,128)(2,1)S(1)}, u32[]{:S(2)}, u32[]{:S(2)}) collective-permute-start(bf16[32,200]{1,0:T(8,128)(2,1)S(1)} %slice.65), channel_id=1, source_target_pairs={{0,2},{1,5},{2,0},{3,7},{4,6},{5,1},{6,4},{7,3},{8,10},{9,13},{10,... | collective-permute-start | bytes 38408 | tf_op jit(solution)/shard_map/ppermute | solution.py:336
  15.3 8.5 %collective-permute-start.4 = (bf16[64,200]{1,0:T(8,128)(2,1)S(1)}, bf16[64,200]{1,0:T(8,128)(2,1)S(1)}, u32[]{:S(2)}, u32[]{:S(2)}) collective-permute-start(bf16[64,200]{1,0:T(8,128)(2,1)S(1)} %pad_maximum_fusion.10), channel_id=1, source_target_pairs={{0,4},{1,3},{2,6},{3,1},{4,0},{5,7},{6,2},{7,5},{8,12},{9,11},{10,... | collective-permute-start | bytes 76808 | tf_op jit(solution)/shard_map/ppermute | solution.py:336
  23.8 2.4 %collective-permute-start.5 = (bf16[128,200]{1,0:T(8,128)(2,1)S(1)}, bf16[128,200]{1,0:T(8,128)(2,1)S(1)}, u32[]{:S(2)}, u32[]{:S(2)}) collective-permute-start(bf16[128,200]{1,0:T(8,128)(2,1)S(1)} %pad_maximum_fusion.8), channel_id=1, source_target_pairs={{0,1},{1,0},{2,3},{3,2},{4,5},{5,4},{6,7},{7,6},{8,9},{9,8},{10,11... | collective-permute-start | bytes 153608 | tf_op jit(solution)/shard_map/ppermute | solution.py:336
  34.6 4.7 %collective-permute-start.7 = (f32[128,200]{1,0:T(8,128)S(1)}, f32[128,200]{1,0:T(8,128)S(1)}, u32[]{:S(2)}, u32[]{:S(2)}) collective-permute-start(f32[128,200]{1,0:T(8,128)S(1)} %slice.51), channel_id=1, source_target_pairs={{0,1},{1,0},{2,3},{3,2},{4,5},{5,4},{6,7},{7,6},{8,9},{9,8},{10,11... | collective-permute-start | bytes 307208 | tf_op jit(solution)/shard_map/ppermute | solution.py:336
  34.7 23.4 %collective-permute-start = (s32[2,128]{1,0:T(2,128)S(1)}, s32[2,128]{1,0:T(2,128)S(1)}, u32[]{:S(2)}, u32[]{:S(2)}) collective-permute-start(s32[2,128]{1,0:T(2,128)S(1)} %get-tuple-element.29), channel_id=1, source_target_pairs={{0,16},{1,17},{2,18},{3,19},{4,20},{5,21},{6,22},{7,23},{8,24},{9,... | collective-permute-start | bytes 3080 | tf_op jit(solution)/shard_map/ppermute | solution.py:336
  36.2 21.8 %collective-permute-start.6 = (f32[200,128]{1,0:T(8,128)S(1)}, f32[200,128]{1,0:T(8,128)S(1)}, u32[]{:S(2)}, u32[]{:S(2)}) collective-permute-start(f32[200,128]{1,0:T(8,128)S(1)} %get-tuple-element.36), channel_id=1, source_target_pairs={{0,8},{1,9},{2,10},{3,11},{4,12},{5,13},{6,14},{7,15},{8,0},{9,1},... | collective-permute-start | bytes 307208 | tf_op jit(solution)/shard_map/ppermute | solution.py:336
  37.7 4.5 %collective-permute-start.11 = (bf16[1,208,128]{2,1,0:T(8,128)(2,1)S(1)}, bf16[1,208,128]{2,1,0:T(8,128)(2,1)S(1)}, u32[]{:S(2)}, u32[]{:S(2)}) collective-permute-start(bf16[1,208,128]{2,1,0:T(8,128)(2,1)S(1)} %bitcast.14), channel_id=1, source_target_pairs={{0,2},{1,5},{2,0},{3,7},{4,6},{5,1},{6,4},{7,3},{8,10},{9,13},{10,... | collective-permute-start | bytes 159752 | tf_op jit(solution)/shard_map/ppermute | solution.py:336
  39.3 5.9 %collective-permute-start.8 = (f32[64,200]{1,0:T(8,128)S(1)}, f32[64,200]{1,0:T(8,128)S(1)}, u32[]{:S(2)}, u32[]{:S(2)}) collective-permute-start(f32[64,200]{1,0:T(8,128)S(1)} %slice.67), channel_id=1, source_target_pairs={{0,4},{1,3},{2,6},{3,1},{4,0},{5,7},{6,2},{7,5},{8,12},{9,11},{10,... | collective-permute-start | bytes 153608 | tf_op jit(solution)/shard_map/ppermute | solution.py:336
  42.3 7.2 %collective-permute-start.12 = (bf16[2,208,128]{2,1,0:T(8,128)(2,1)S(1)}, bf16[2,208,128]{2,1,0:T(8,128)(2,1)S(1)}, u32[]{:S(2)}, u32[]{:S(2)}) collective-permute-start(bf16[2,208,128]{2,1,0:T(8,128)(2,1)S(1)} %pad_maximum_fusion.6), channel_id=1, source_target_pairs={{0,4},{1,3},{2,6},{3,1},{4,0},{5,7},{6,2},{7,5},{8,12},{9,11},{10,... | collective-permute-start | bytes 319496 | tf_op jit(solution)/shard_map/ppermute | solution.py:336
  45.3 4.8 %collective-permute-start.9 = (f32[32,200]{1,0:T(8,128)S(1)}, f32[32,200]{1,0:T(8,128)S(1)}, u32[]{:S(2)}, u32[]{:S(2)}) collective-permute-start(f32[32,200]{1,0:T(8,128)S(1)} %slice.69), channel_id=1, source_target_pairs={{0,2},{1,5},{2,0},{3,7},{4,6},{5,1},{6,4},{7,3},{8,10},{9,13},{10,... | collective-permute-start | bytes 76808 | tf_op jit(solution)/shard_map/ppermute | solution.py:336
  49.5 7.9 %collective-permute-start.13 = (bf16[4,208,128]{2,1,0:T(8,128)(2,1)S(1)}, bf16[4,208,128]{2,1,0:T(8,128)(2,1)S(1)}, u32[]{:S(2)}, u32[]{:S(2)}) collective-permute-start(bf16[4,208,128]{2,1,0:T(8,128)(2,1)S(1)} %pad_maximum_fusion.2), channel_id=1, source_target_pairs={{0,8},{1,17},{2,10},{3,19},{4,12},{5,21},{6,14},{7,23},{8,0},{9,25... | collective-permute-start | bytes 638984 | tf_op jit(solution)/shard_map/ppermute | solution.py:336
  50.1 8.0 %collective-permute-start.10 = (f32[32,200]{1,0:T(8,128)S(1)}, f32[32,200]{1,0:T(8,128)S(1)}, u32[]{:S(2)}, u32[]{:S(2)}) collective-permute-start(f32[32,200]{1,0:T(8,128)S(1)} %slice_add_fusion.5), channel_id=1, source_target_pairs={{0,8},{1,9},{2,10},{3,11},{4,12},{5,13},{6,14},{7,15},{8,0},{9,1},... | collective-permute-start | bytes 76808 | tf_op jit(solution)/shard_map/ppermute | solution.py:336
  57.4 18.0 %collective-permute-start.14 = (bf16[8,208,128]{2,1,0:T(8,128)(2,1)S(1)}, bf16[8,208,128]{2,1,0:T(8,128)(2,1)S(1)}, u32[]{:S(2)}, u32[]{:S(2)}) collective-permute-start(bf16[8,208,128]{2,1,0:T(8,128)(2,1)S(1)} %pad_maximum_fusion.mine_ref), channel_id=1, source_target_pairs={{0,16},{1,9},{2,18},{3,11},{4,20},{5,13},{6,22},{7,15},{8,24},{9,1... | collective-permute-start | bytes 1277960 | tf_op jit(solution)/shard_map/ppermute | solution.py:336
  60.1 6.4 %collective-permute-start.17 = (bf16[160,200]{1,0:T(8,128)(2,1)S(1)}, bf16[160,200]{1,0:T(8,128)(2,1)S(1)}, u32[]{:S(2)}, u32[]{:S(2)}) collective-permute-start(bf16[160,200]{1,0:T(8,128)(2,1)S(1)} %get-tuple-element.45), channel_id=1, source_target_pairs={{0,16},{1,17},{2,18},{3,19},{4,20},{5,21},{6,22},{7,23},{8,24},{9,... | collective-permute-start | bytes 192008 | tf_op jit(solution)/shard_map/ppermute | solution.py:336
  66.5 3.9 %collective-permute-start.18 = (bf16[32,200]{1,0:T(8,128)(2,1)S(1)}, bf16[32,200]{1,0:T(8,128)(2,1)S(1)}, u32[]{:S(2)}, u32[]{:S(2)}) collective-permute-start(bf16[32,200]{1,0:T(8,128)(2,1)S(1)} %slice.71), channel_id=1, source_target_pairs={{0,2},{1,5},{2,0},{3,7},{4,6},{5,1},{6,4},{7,3},{8,10},{9,13},{10,... | collective-permute-start | bytes 38408 | tf_op jit(solution)/shard_map/ppermute | solution.py:336
  66.5 8.9 %collective-permute-start.15 = (s32[2,128]{1,0:T(2,128)S(1)}, s32[2,128]{1,0:T(2,128)S(1)}, u32[]{:S(2)}, u32[]{:S(2)}) collective-permute-start(s32[2,128]{1,0:T(2,128)S(1)} %copy-done.6), channel_id=1, source_target_pairs={{0,1},{1,0},{2,3},{3,2},{4,5},{5,4},{6,7},{7,6},{8,9},{9,8},{10,11... | collective-permute-start | bytes 3080 | tf_op jit(solution)/shard_map/ppermute | solution.py:336
  70.4 4.9 %collective-permute-start.19 = (bf16[64,200]{1,0:T(8,128)(2,1)S(1)}, bf16[64,200]{1,0:T(8,128)(2,1)S(1)}, u32[]{:S(2)}, u32[]{:S(2)}) collective-permute-start(bf16[64,200]{1,0:T(8,128)(2,1)S(1)} %pad_maximum_fusion.11), channel_id=1, source_target_pairs={{0,4},{1,3},{2,6},{3,1},{4,0},{5,7},{6,2},{7,5},{8,12},{9,11},{10,... | collective-permute-start | bytes 76808 | tf_op jit(solution)/shard_map/ppermute | solution.py:336
  75.3 2.1 %collective-permute-start.20 = (bf16[128,200]{1,0:T(8,128)(2,1)S(1)}, bf16[128,200]{1,0:T(8,128)(2,1)S(1)}, u32[]{:S(2)}, u32[]{:S(2)}) collective-permute-start(bf16[128,200]{1,0:T(8,128)(2,1)S(1)} %pad_maximum_fusion.9), channel_id=1, source_target_pairs={{0,1},{1,0},{2,3},{3,2},{4,5},{5,4},{6,7},{7,6},{8,9},{9,8},{10,11... | collective-permute-start | bytes 153608 | tf_op jit(solution)/shard_map/ppermute | solution.py:336
  76.9 1.5 %collective-permute-start.16 = (f32[208,128]{1,0:T(8,128)S(1)}, f32[208,128]{1,0:T(8,128)S(1)}, u32[]{:S(2)}, u32[]{:S(2)}) collective-permute-start(f32[208,128]{1,0:T(8,128)S(1)} %get-tuple-element.42), channel_id=1, source_target_pairs={{0,1},{1,0},{2,3},{3,2},{4,5},{5,4},{6,7},{7,6},{8,9},{9,8},{10,11... | collective-permute-start | bytes 319496 | tf_op jit(solution)/shard_map/ppermute | solution.py:336
  86.9 4.8 %collective-permute-start.27 = (bf16[1,208,128]{2,1,0:T(8,128)(2,1)S(1)}, bf16[1,208,128]{2,1,0:T(8,128)(2,1)S(1)}, u32[]{:S(2)}, u32[]{:S(2)}) collective-permute-start(bf16[1,208,128]{2,1,0:T(8,128)(2,1)S(1)} %bitcast.18), channel_id=1, source_target_pairs={{0,2},{1,5},{2,0},{3,7},{4,6},{5,1},{6,4},{7,3},{8,10},{9,13},{10,... | collective-permute-start | bytes 159752 | tf_op jit(solution)/shard_map/ppermute | solution.py:336
  91.6 5.9 %collective-permute-start.28 = (bf16[2,208,128]{2,1,0:T(8,128)(2,1)S(1)}, bf16[2,208,128]{2,1,0:T(8,128)(2,1)S(1)}, u32[]{:S(2)}, u32[]{:S(2)}) collective-permute-start(bf16[2,208,128]{2,1,0:T(8,128)(2,1)S(1)} %pad_maximum_fusion.7), channel_id=1, source_target_pairs={{0,4},{1,3},{2,6},{3,1},{4,0},{5,7},{6,2},{7,5},{8,12},{9,11},{10,... | collective-permute-start | bytes 319496 | tf_op jit(solution)/shard_map/ppermute | solution.py:336
  97.6 6.9 %collective-permute-start.29 = (bf16[4,208,128]{2,1,0:T(8,128)(2,1)S(1)}, bf16[4,208,128]{2,1,0:T(8,128)(2,1)S(1)}, u32[]{:S(2)}, u32[]{:S(2)}) collective-permute-start(bf16[4,208,128]{2,1,0:T(8,128)(2,1)S(1)} %pad_maximum_fusion.3), channel_id=1, source_target_pairs={{0,8},{1,17},{2,10},{3,19},{4,12},{5,21},{6,14},{7,23},{8,0},{9,25... | collective-permute-start | bytes 638984 | tf_op jit(solution)/shard_map/ppermute | solution.py:336
  104.5 8.2 %collective-permute-start.30 = (bf16[8,208,128]{2,1,0:T(8,128)(2,1)S(1)}, bf16[8,208,128]{2,1,0:T(8,128)(2,1)S(1)}, u32[]{:S(2)}, u32[]{:S(2)}) collective-permute-start(bf16[8,208,128]{2,1,0:T(8,128)(2,1)S(1)} %pad_maximum_fusion.1.mine_ref), channel_id=1, source_target_pairs={{0,16},{1,9},{2,18},{3,11},{4,20},{5,13},{6,22},{7,15},{8,24},{9,1... | collective-permute-start | bytes 1277960 | tf_op jit(solution)/shard_map/ppermute | solution.py:336
  108.5 25.5 %collective-permute-start.26 = (f32[200,1408]{1,0:T(8,128)S(1)}, f32[200,1408]{1,0:T(8,128)S(1)}, u32[]{:S(2)}, u32[]{:S(2)}) collective-permute-start(f32[200,1408]{1,0:T(8,128)S(1)} %relation_sums.2.refs_0_), channel_id=1, source_target_pairs={{0,1},{1,0},{2,3},{3,2},{4,5},{5,4},{6,7},{7,6},{8,9},{9,8},{10,11... | collective-permute-start | bytes 3379208 | tf_op jit(solution)/shard_map/ppermute | solution.py:336
  116.1 17.9 %collective-permute-start.31 = (f32[200,1408]{1,0:T(8,128)S(1)}, f32[200,1408]{1,0:T(8,128)S(1)}, u32[]{:S(2)}, u32[]{:S(2)}) collective-permute-start(f32[200,1408]{1,0:T(8,128)S(1)} %relation_sums.3.refs_2_), channel_id=1, source_target_pairs={{0,1},{1,0},{2,3},{3,2},{4,5},{5,4},{6,7},{7,6},{8,9},{9,8},{10,11... | collective-permute-start | bytes 3379208 | tf_op jit(solution)/shard_map/ppermute | solution.py:336
  116.2 2.9 %collective-permute-start.22 = (f32[128,200]{1,0:T(8,128)S(1)}, f32[128,200]{1,0:T(8,128)S(1)}, u32[]{:S(2)}, u32[]{:S(2)}) collective-permute-start(f32[128,200]{1,0:T(8,128)S(1)} %slice.59), channel_id=1, source_target_pairs={{0,1},{1,0},{2,3},{3,2},{4,5},{5,4},{6,7},{7,6},{8,9},{9,8},{10,11... | collective-permute-start | bytes 307208 | tf_op jit(solution)/shard_map/ppermute | solution.py:336
  119.1 5.2 %collective-permute-start.23 = (f32[64,200]{1,0:T(8,128)S(1)}, f32[64,200]{1,0:T(8,128)S(1)}, u32[]{:S(2)}, u32[]{:S(2)}) collective-permute-start(f32[64,200]{1,0:T(8,128)S(1)} %slice.73), channel_id=1, source_target_pairs={{0,4},{1,3},{2,6},{3,1},{4,0},{5,7},{6,2},{7,5},{8,12},{9,11},{10,... | collective-permute-start | bytes 153608 | tf_op jit(solution)/shard_map/ppermute | solution.py:336
  124.4 4.0 %collective-permute-start.24 = (f32[32,200]{1,0:T(8,128)S(1)}, f32[32,200]{1,0:T(8,128)S(1)}, u32[]{:S(2)}, u32[]{:S(2)}) collective-permute-start(f32[32,200]{1,0:T(8,128)S(1)} %slice.75), channel_id=1, source_target_pairs={{0,2},{1,5},{2,0},{3,7},{4,6},{5,1},{6,4},{7,3},{8,10},{9,13},{10,... | collective-permute-start | bytes 76808 | tf_op jit(solution)/shard_map/ppermute | solution.py:336
  124.5 4.8 %collective-permute-start.21 = (f32[200,128]{1,0:T(8,128)S(1)}, f32[200,128]{1,0:T(8,128)S(1)}, u32[]{:S(2)}, u32[]{:S(2)}) collective-permute-start(f32[200,128]{1,0:T(8,128)S(1)} %get-tuple-element.47), channel_id=1, source_target_pairs={{0,16},{1,17},{2,18},{3,19},{4,20},{5,21},{6,22},{7,23},{8,24},{9,... | collective-permute-start | bytes 307208 | tf_op jit(solution)/shard_map/ppermute | solution.py:336
  128.4 3.9 %collective-permute-start.25 = (f32[32,200]{1,0:T(8,128)S(1)}, f32[32,200]{1,0:T(8,128)S(1)}, u32[]{:S(2)}, u32[]{:S(2)}) collective-permute-start(f32[32,200]{1,0:T(8,128)S(1)} %slice_add_fusion.4), channel_id=1, source_target_pairs={{0,16},{1,17},{2,18},{3,19},{4,20},{5,21},{6,22},{7,23},{8,24},{9,... | collective-permute-start | bytes 76808 | tf_op jit(solution)/shard_map/ppermute | solution.py:336
  (17 other events, 64.7 us)

commit v3 on v2

--- a/solution.py
+++ b/solution.py
@@ -34,7 +34,7 @@
     return jax.ShapeDtypeStruct(shape, dtype)
 
 
-def call(kernel, name, micros, out_shape, args, scratch=(), scalars=0, limit=40):
+def call(kernel, name, micros, out_shape, args, scratch=(), scalars=0, limit=16):
     return pl.pallas_call(
         kernel,
         out_shape=out_shape,
@@ -85,10 +85,8 @@
 
 
 def turned(values):
-    rows = values.shape[0]
-    if rows < LANES:
-        values = jnp.concatenate([values, jnp.zeros((LANES - rows, values.shape[1]), f32)], axis=0)
-    return jnp.transpose(values)
+    rest = -values.shape[0] % LANES
+    return jnp.transpose(jnp.concatenate([values, jnp.zeros((rest, D), f32)], axis=0))
 
 
 def wanted_kernel(tails_ref, negatives_ref, *outs):
@@ -161,7 +159,6 @@
     hit = hits(ids_ref[1:2, :], wide)
     later_out[...] = dot(high, hit) + dot(middle, hit) + dot(low, hit)
     sums = padded(state_ref[...], wide)
-    column = lax.broadcasted_iota(i32, (wide // LANES, LANES, LANES), 1)
     names = ids_ref[1:2, :]
     total = jnp.zeros((LANES, LANES), f32)
     for block in range(wide // LANES):
@@ -171,9 +168,7 @@
     state_out[...] = jnp.sum(total, axis=0, keepdims=True)
 
 
-def pass_kernel(
-    round_index, heads_ref, relations_ref, ent_ref, *refs
-):
+def forward_kernel(round_index, heads_ref, ent_ref, *refs):
     if round_index == 0:
         rel_rows = refs[0][...]
         refs = refs[1:]
@@ -183,15 +178,12 @@
         rel_rows = refs[2][...] - gradient * (learn_rate * lax.rsqrt(state))
         rel_rows = rel_rows.astype(bf16).astype(f32)
         refs = refs[4:]
-    tail_ref, neg_ref, band_ref, band_t_ref, bias_ref, fc_ref, fcb_ref = refs[:7]
-    pack_out, head_out, tail_out, neg_out, picture, slopes, work, total = refs[7:]
+    band_ref, bias_ref, fc_ref, fcb_ref, pre2_out, slopes, picture, work = refs
     heads = heads_ref[round_index : round_index + 1, :]
-    relations = relations_ref[round_index : round_index + 1, :]
     table = ent_ref[...].astype(bf16)
     picture[:D, :] = dot(table, hits(heads, table.shape[1]))
     picture[D:, :] = rel_rows
-    number = LANES
-    pre2 = jnp.zeros((number, D), f32)
+    pre2 = jnp.zeros(pre2_out.shape, f32)
     for pair in range(PAIRS):
         first = pair * 2 * EMB_W
         window = jnp.transpose(picture[first : first + WINDOW, :]).astype(bf16)
@@ -201,10 +193,14 @@
         slopes[pair] = sigma + act * (1.0 - sigma)
         work[pair] = act.astype(bf16)
         pre2 = pre2 + dot(work[pair], fc_ref[pair])
-    pre2 = pre2 + fcb_ref[...]
+    pre2_out[...] = pre2 + fcb_ref[...]
+
+
+def score_kernel(pre2_ref, tail_ref, neg_ref, grad_out, tail_out, neg_out):
+    pre2 = pre2_ref[...]
     sigma = sigmoid(pre2)
     value = pre2 * sigma
-    slope2 = sigma + value * (1.0 - sigma)
+    slope = sigma + value * (1.0 - sigma)
     query = value.astype(bf16)
     query32 = query.astype(f32)
     tails = tail_ref[...].astype(f32)
@@ -212,9 +208,13 @@
     negset = neg_ref[...]
     neg_grad = (negative_weight * sigmoid(dot_nt(query, negset))).astype(bf16)
     query_grad = pos_grad * tails + dot(neg_grad, negset)
-    pre2_grad = (query_grad * slope2).astype(bf16)
-    tail_out[...] = jnp.transpose(pos_grad * query32)
+    grad_out[...] = (query_grad * slope).astype(bf16)
+    tail_out[...] = pos_grad * query32
     neg_out[...] = dot_tn(neg_grad, query)
+
+
+def backward_kernel(round_index, relations_ref, grad_ref, slopes, band_t_ref, fc_ref, pack_out, head_out, work, total):
+    pre2_grad = grad_ref[...]
     total[...] = jnp.zeros_like(total)
     for pair in range(PAIRS):
         act_grad = dot_nt(pre2_grad, fc_ref[pair])
@@ -223,18 +223,21 @@
         at = slice(pair * 2 * EMB_W, pair * 2 * EMB_W + WINDOW)
         total[at, :] = total[at, :] + jnp.transpose(part)[:WINDOW, :]
     head_out[...] = total[:D, :]
+    relations = relations_ref[round_index : round_index + 1, :]
     high = relations >> 6
     low = relations - (high << 6)
-    spare = lax.broadcasted_iota(i32, (PACK - D, number), 0)
+    spare = lax.broadcasted_iota(i32, (PACK - D, LANES), 0)
     codes = jnp.where(spare == 0, high, jnp.where(spare == 1, low, 0)).astype(f32)
     pack_out[...] = jnp.concatenate([total[D:, :], codes], axis=0).astype(bf16)
 
 
 def entity_kernel(
-    round_index, heads_ref, asked_ref, next_ref, ent_ref, state_ref, head_ref, tail_ref, neg_ref, *outs
+    round_index, negatives, heads_ref, asked_ref, next_ref, ent_ref, state_ref, head_ref, back_ref, other_ref, *outs
 ):
     count = ent_ref.shape[1]
-    grads = jnp.concatenate([head_ref[...], tail_ref[...], turned(neg_ref[...])], axis=1)
+    number = back_ref.shape[0] - negatives
+    back = jnp.concatenate([back_ref[:number, :], back_ref[number:, :] + other_ref[...]], axis=0)
+    grads = jnp.concatenate([head_ref[...], turned(back)], axis=1)
     high, low = halves(grads)
     named = jnp.concatenate(
         [heads_ref[round_index : round_index + 1, :], asked_ref[0:1, :], asked_ref[1:2, :]], axis=1
@@ -246,24 +249,26 @@
     outs[0][...] = rows
     outs[1][...] = state
     if len(outs) > 2:
-        pick_answer(rows.astype(bf16), next_ref, neg_ref.shape[0], outs[2])
-
-
-def lay_packs(place_ref, mine_ref, other_ref, grads, names):
-    half = mine_ref.shape[0]
-    for index in range(2 * half):
-        spot = place_ref[index]
-        at = slice(index * LANES, (index + 1) * LANES)
-        inner = lax.rem(spot, half)
-        block = jnp.where(spot < half, mine_ref[inner].astype(f32), other_ref[inner].astype(f32))
-        grads[:, at] = block.astype(bf16)
-        names[0:1, at] = (block[D : D + 1, :] * 64.0 + block[D + 1 : D + 2, :]).astype(i32)
-
-
-def need_kernel(round_index, place_ref, mine_ref, other_ref, ids_ref, others_ref, own_out, send_out, grads, names):
-    lay_packs(place_ref, mine_ref, other_ref, grads, names)
+        pick_answer(rows.astype(bf16), next_ref, negatives, outs[2])
+
+
+def lay_packs(place_ref, groups, grads, names):
+    index = 0
+    for group in groups:
+        for inner in range(group.shape[0]):
+            at = slice(index * LANES, (index + 1) * LANES)
+            block = group[place_ref[inner]]
+            grads[:, at] = block
+            codes = block[PACK - 16 :, :].astype(f32)[D - PACK + 16 :, :]
+            names[0:1, at] = (codes[0:1, :] * 64.0 + codes[1:2, :]).astype(i32)
+            index += 1
+
+
+def need_kernel(round_index, place_ref, *refs):
+    groups, (ids_ref, others_ref, own_out, send_out, grads, names) = refs[:4], refs[4:]
+    lay_packs(place_ref, groups, grads, names)
     wide = names.shape[1]
-    for ids, out in ((ids_ref, own_out), (others_ref, send_out)):
+    for ids, out in ((others_ref, send_out), (ids_ref, own_out)):
         column = as_column(ids[round_index : round_index + 1, :])
         hit = jnp.concatenate(
             [
@@ -277,10 +282,25 @@
         out[...] = jnp.transpose(dot_nt(hit, grads[...]))
 
 
-def sums_kernel(place_ref, mine_ref, other_ref, out, grads, names):
-    lay_packs(place_ref, mine_ref, other_ref, grads, names)
-    for first in range(0, out.shape[1], LANES):
-        out[:, first : first + LANES] = dot_nt(grads[...], hits(names[0:1, :], LANES, first))[:D, :]
+def sums_kernel(kinds, place_ref, *refs):
+    packs, before, refs = refs[: kinds[0]], refs[kinds[0] : sum(kinds)], refs[sum(kinds) :]
+    outs, grads, names = refs[:-2], refs[-2], refs[-1]
+    lay_packs(place_ref, packs, grads, names)
+    size = names.shape[1] // len(packs)
+    for first in range(0, outs[0].shape[1], LANES):
+        at = slice(first, first + LANES)
+        hit = hits(names[0:1, :], LANES, first)
+        parts = [
+            dot_nt(grads[:, k * size : (k + 1) * size], hit[:, k * size : (k + 1) * size])[:D, :]
+            for k in range(len(packs))
+        ]
+        if len(packs) == 4:
+            outs[0][:, at] = (parts[0] + parts[1]) + (parts[2] + parts[3])
+        elif len(packs) == 3:
+            outs[0][:, at] = parts[0] + parts[1]
+            outs[1][:, at] = parts[2]
+        else:
+            outs[0][:, at] = before[0][:, at] + (before[1][:, at] + parts[0])
 
 
 def relation_kernel(rel_ref, state_ref, *refs):
@@ -295,58 +315,30 @@
     refs[2 * ROUNDS + 1][...] = state
 
 
-def swapped(bits):
-    out = list(bits)
-    for index in range(0, len(out) - 1, 2):
-        out[index], out[index + 1] = out[index + 1], out[index]
-    return out
-
-
 class Plan:
     def __init__(self, groups, shards):
         self.total = groups * shards
         self.shards = shards
-        near = [1 << bit for bit in range(1, shards.bit_length() - 1)]
-        far = [shards << bit for bit in range(groups.bit_length() - 1)]
-        self.even = near + far
-        self.odd = swapped(near) + swapped(far)
-        self.across = [self.route(a, b) for a, b in zip(self.even, self.odd)]
-        self.core = self.route(1, 1)
-        self.within = self.across[: len(near)] + [self.core]
-
-    def route(self, even, odd):
-        return [(at, at ^ (odd if at & 1 else even)) for at in range(self.total)]
+        self.near = [1 << bit for bit in range(1, shards.bit_length() - 1)]
+        self.far = [shards << bit for bit in range(groups.bit_length() - 1)]
+        self.lead = self.near + self.far[:-2]
+
+    def route(self, mask):
+        return [(at, at ^ mask) for at in range(self.total)]
 
     def partner(self, bit):
-        mask = self.shards << bit
-        return self.route(mask, mask)
+        return self.shards << bit
+
+    def send(self, block, mask):
+        return lax.ppermute(block, BOTH, self.route(mask))
 
     def places(self, me):
-        source = jnp.arange(0, self.total, 2, dtype=i32)
-        differ = source ^ me
-        even = jnp.zeros_like(source)
-        odd = jnp.zeros_like(source)
-        for step, (one, other) in enumerate(zip(self.even, self.odd)):
-            even = even + jnp.where((differ & one) != 0, 1 << step, 0)
-            odd = odd + jnp.where((differ & other) != 0, 1 << step, 0)
-        return jnp.where((me & 1) == 0, even, odd)
-
-
-def send(block, route):
-    return lax.ppermute(block, BOTH, route)
-
-
-def doubled(block, routes):
-    for route in routes:
-        block = jnp.concatenate([block, send(block, route)], axis=0)
-    return block
-
-
-def halved(block, routes):
-    for route in reversed(routes):
-        half = block.shape[0] // 2
-        block = block[:half] + send(block[half:], route)
-    return block
+        mine = sum(((me & mask) != 0).astype(i32) << step for step, mask in enumerate(self.lead))
+        return jnp.arange(1 << len(self.lead), dtype=i32) ^ mine
+
+
+def together(*values):
+    return lax.optimization_barrier(values)
 
 
 def shards(
@@ -368,99 +360,195 @@
     negatives = neg_ids.shape[1]
     count = relation_rows.shape[0]
     wide = count + -count % LANES
-    sources = plan.total // 2
+    features = fc_weight.shape[0]
+    group = 1 << len(plan.lead)
+    send = plan.send
     me = lax.axis_index("group") * plan.shards + lax.axis_index("shard")
+    place = plan.places(me)
     ent = entity_rows.T
     ent_state = entity_state[None, :]
     rel = relation_rows.T
     rel_state = relation_state[None, :]
+    bias2 = fc_bias[None, :]
+    next_door, beyond = plan.near[0], plan.near[1:]
+
+    def asked_rows(answer, bit):
+        near = send(answer, plan.partner(bit))
+        side = send(answer[number:], plan.partner(bit) | next_door)
+        return near, side
 
     wanted = call(
         wanted_kernel, "wanted", 1, [shaped((2, LANES), i32)] * ROUNDS, (tail_ids, neg_ids)
     )
-    requested = [send(wanted[r], plan.partner(r)) for r in range(ROUNDS)]
-    rel_others = send(rel_ids, plan.core)
+    requested = [send(wanted[0], plan.partner(0))]
     answer_shape = shaped((number + negatives, D), bf16)
     (answer,) = call(
         functools.partial(answer_kernel, negatives), "answer", 1, [answer_shape], (requested[0], ent)
     )
+    rel_first, rel_later, state_later = call(
+        rows_kernel,
+        "relation_rows",
+        1,
+        [shaped((D, number)), shaped((D, number)), shaped((1, number))],
+        (rel_ids, rel, rel_state),
+        [pltpu.VMEM((D, wide), f32)],
+    )
+    near, side = asked_rows(answer, 0)
+    near, side, rel_first, rel_later, state_later = together(
+        near, side, rel_first, rel_later, state_later
+    )
+    negset = jnp.concatenate([near[number:], side], axis=0)
     taps = jnp.tile(conv_weight.reshape(FILTERS, 9).T.astype(f32), (1, WIDE // FILTERS))
     bias = jnp.tile(conv_bias[None, :], (1, WIDE // FILTERS))
-    features = fc_weight.shape[0]
     fc, band, band_t = call(
         prepare_kernel,
         "prepare",
-        5,
+        4,
         [shaped((features, D), bf16), shaped((WINDOW, WIDE), bf16), shaped((WIDE, LANES), bf16)],
         (fc_weight.T, taps),
         [pltpu.VMEM((features, LANES), f32), pltpu.VMEM((features, LANES), f32)],
+        limit=24,
     )
     fc = fc.reshape(PAIRS, WIDE, D)
-    rel_first, rel_later, state_later = call(
-        rows_kernel,
-        "relation_rows",
-        2,
-        [shaped((D, number)), shaped((D, number)), shaped((1, number))],
-        (rel_ids, rel, rel_state),
-        [pltpu.VMEM((D, wide), f32)],
-    )
+    for mask in beyond:
+        negset = jnp.concatenate([negset, send(negset, mask)], axis=0)
+    near, negset, fc, band, band_t = together(near, negset, fc, band, band_t)
+    requested.append(send(wanted[1], plan.partner(1)))
+    rel_others = send(rel_ids, 1)
+    negset = jnp.concatenate([negset, send(negset, 1)], axis=0)
     rel_inputs = (rel_first,)
-    place = plan.places(me)
-    lay = [pltpu.VMEM((PACK, sources * LANES), bf16), pltpu.VMEM((8, sources * LANES), i32)]
+
+    def lay(sources):
+        return [pltpu.VMEM((PACK, sources * LANES), bf16), pltpu.VMEM((8, sources * LANES), i32)]
 
     sums = []
     for r in range(ROUNDS):
         last = r == ROUNDS - 1
-        answered = send(answer, plan.partner(r))
-        negset = doubled(answered[number:], plan.within)
-        pack, head_grad, tail_grad, neg_part = call(
-            functools.partial(pass_kernel, r),
-            "local_pass",
-            6,
-            [
-                shaped((PACK, number), bf16),
-                shaped((D, number)),
-                shaped((D, number)),
-                shaped((negset.shape[0], D)),
-            ],
-            (head_ids, rel_ids, ent, *rel_inputs, answered[:number], negset, band, band_t, bias, fc, fc_bias[None, :]),
-            [
-                pltpu.VMEM((PIXELS, number), f32),
-                pltpu.VMEM((PAIRS, number, WIDE), f32),
-                pltpu.VMEM((PAIRS, number, WIDE), bf16),
-                pltpu.VMEM((PIXELS, number), f32),
-            ],
+        pre2, slopes = call(
+            functools.partial(forward_kernel, r),
+            "forward",
+            2.5,
+            [shaped((number, D)), shaped((PAIRS, number, WIDE))],
+            (head_ids, ent, *rel_inputs, band, bias, fc, bias2),
+            [pltpu.VMEM((PIXELS, number), f32), pltpu.VMEM((PAIRS, number, WIDE), bf16)],
+            limit=24,
         )
-        packs = doubled(pack[None], plan.across[:-1])
-        arrived = send(packs, plan.across[-1])
-        tail_back = send(tail_grad, plan.partner(r))
-        neg_back = send(halved(neg_part, plan.within), plan.partner(r))
-        if not last:
+        grad2, tail_grad, neg_part = call(
+            score_kernel,
+            "scores",
+            1,
+            [shaped((number, D), bf16), shaped((number, D)), shaped((negset.shape[0], D))],
+            (pre2, near[:number], negset),
+        )
+        if r == 0:
+            grad2, neg_part, requested[1], rel_others = together(
+                grad2, neg_part, requested[1], rel_others
+            )
+        half = neg_part.shape[0] // 2
+        arrived = send(neg_part[half:], 1)
+        pack, head_grad = call(
+            functools.partial(backward_kernel, r),
+            "backward",
+            3,
+            [shaped((PACK, number), bf16), shaped((D, number))],
+            (rel_ids, grad2, slopes, band_t, fc),
+            [pltpu.VMEM((PAIRS, number, WIDE), bf16), pltpu.VMEM((PIXELS, number), f32)],
+            limit=24,
+        )
+        pack, arrived = together(pack, arrived)
+        share = neg_part[:half] + arrived
+        packs = pack[None]
+        lead = list(plan.lead)
+        back = list(reversed(beyond))
+        for step, mask in enumerate(lead):
+            came = send(packs, mask)
+            if step < len(back):
+                half = share.shape[0] // 2
+                arrived = send(share[half:], back[step])
+                came, arrived = together(came, arrived)
+                share = share[:half] + arrived
+            elif step == len(lead) - 1:
+                own_back = jnp.concatenate([tail_grad, share[:negatives]], axis=0)
+                to_owner = send(own_back, plan.partner(r))
+                to_side = send(share[negatives:], plan.partner(r) | next_door)
+                came, to_owner, to_side = together(came, to_owner, to_side)
+            packs = jnp.concatenate([packs, came], axis=0)
+            if last and step == 0:
+                (part,) = call(
+                    functools.partial(sums_kernel, (4, 0)),
+                    "relation_sums",
+                    3,
+                    [shaped((D, wide))],
+                    (place, *groups),
+                    lay(4 * group),
+                    scalars=1,
+                )
+                packs, part = together(packs, part)
+                sums = [part, send(part, 1)]
+        one, other = plan.far[-2:]
+        across = send(packs, one)
+        along = send(packs, other)
+        out_shape = [shaped(ent.shape), shaped(ent_state.shape)]
+        outs = call(
+            functools.partial(entity_kernel, r, negatives),
+            "entity_update",
+            1.5,
+            out_shape if last else out_shape + [answer_shape],
+            (
+                head_ids,
+                requested[r],
+                requested[min(r + 1, ROUNDS - 1)],
+                ent,
+                ent_state,
+                head_grad,
+                to_owner,
+                to_side,
+            ),
+        )
+        ent, ent_state = outs[:2]
+        if last:
+            across, along, ent, ent_state, *sums = together(across, along, ent, ent_state, *sums)
+            corner = send(across, other)
+            early = call(
+                functools.partial(sums_kernel, (3, 0)),
+                "early_sums",
+                3,
+                [shaped((D, wide))] * 2,
+                (place, packs, across, along),
+                lay(3 * group),
+                scalars=1,
+            )
+            corner, *early = together(corner, *early)
+            (part,) = call(
+                functools.partial(sums_kernel, (1, 2)),
+                "late_sums",
+                1,
+                [shaped((D, wide))],
+                (place, corner, *early),
+                lay(group),
+                scalars=1,
+            )
+            sums += [part, send(part, 1)]
+        else:
+            near, side = asked_rows(outs[2], r + 1)
+            corner = send(across, other)
+            groups = (packs, across, along, corner)
+            near, side = together(near, side)
+            negset = jnp.concatenate([near[number:], side], axis=0)
+            for mask in beyond:
+                negset = jnp.concatenate([negset, send(negset, mask)], axis=0)
             own, partial = call(
                 functools.partial(need_kernel, r + 1),
                 "need",
                 1.5,
                 [shaped((PACK, number))] * 2,
-                (place, packs, arrived, rel_ids, rel_others),
-                lay,
+                (place, *groups, rel_ids, rel_others),
+                lay(4 * group),
                 scalars=1,
             )
-            rel_inputs = (own, send(partial, plan.core), rel_later, state_later)
-        out_shape = [shaped(ent.shape), shaped(ent_state.shape)]
-        outs = call(
-            functools.partial(entity_kernel, r),
-            "entity_update",
-            2,
-            out_shape if last else out_shape + [answer_shape],
-            (head_ids, requested[r], requested[min(r + 1, ROUNDS - 1)], ent, ent_state, head_grad, tail_back, neg_back),
-        )
-        ent, ent_state = outs[:2]
-        if not last:
-            answer = outs[2]
-        (part,) = call(
-            sums_kernel, "relation_sums", 3, [shaped((D, wide))], (place, packs, arrived), lay, scalars=1
-        )
-        sums += [part, send(part, plan.core)]
+            negset, own, partial = together(negset, own, partial)
+            rel_inputs = (own, send(partial, 1), rel_later, state_later)
+            negset = jnp.concatenate([negset, send(negset, 1)], axis=0)
     rel, rel_state = call(
         relation_kernel, "relation_update", 2, [shaped((D, count)), shaped((1, count))], (rel, rel_state, *sums)
     )

time: 137 us -> 117 us (0.85)
  waiting for transfers between devices: 70.4 us -> 37.2 us
  starting transfers between devices: 24 us -> 32.5 us
  local copies, waits for them, and re-layouts: 11.1 us -> 14.7 us
    ppermute x32, waiting for transfers between devices: 70.4 us -> 37.2 us  [send(): return lax.ppermute(block, BOTH, self.route(mask))]
    ppermute x32, starting transfers between devices: 24 us -> 32.5 us  [send(): return lax.ppermute(block, BOTH, self.route(mask))]
    unnamed x34 -> x39, local copies, waits for them, and re-layouts: 10.8 us -> 14.4 us
    pallas_call x12 -> x17, Pallas kernels: 28.9 us -> 30 us  [call(): pl.pallas_call(kernel, out_shape=out_shape, in_specs=[SMEM] * scalars + [...]
  transfers between devices with their start and end apart: 32 -> 32, of which waited for: 21 -> 16; matrix products, arithmetic and copies ran while one was open for 0% -> 0% of each run, Pallas kernels for 11% -> 19%
where the time goes in v3:
time: 117 us; the launch traced here: 116 us
  waiting for transfers between devices  37.2 us (32%)
  starting transfers between devices  32.5 us (28%)
  Pallas kernels  30 us (26%)
  local copies, waits for them, and re-layouts  14.7 us (13%)
    ppermute x32, waiting for transfers between devices, send(): return lax.ppermute(block, BOTH, self.route(mask))  37.2 us
    ppermute x32, starting transfers between devices, send(): return lax.ppermute(block, BOTH, self.route(mask))  32.5 us
    pallas_call x17, Pallas kernels, call(): pl.pallas_call(kernel, out_shape=out_shape, in_specs=[SMEM] * scalars + [...  30 us
    unnamed x39, local copies, waits for them, and re-layouts  14.4 us
  transfers between devices with their start and end apart: 32, of which 16 were waited for; matrix products, arithmetic and copies ran while one was open for 0% of the time, Pallas kernels for 19%

profile of v3, /device:TPU:0, one launch (start us, length us, event | category | flops | bytes accessed | tf_op | source)
XLA Modules:
  0.0 116.3 jit_solution(173517517565768189)
XLA Ops:
  2.1 3.0 %collective-permute-start = (s32[2,128]{1,0:T(2,128)S(1)}, s32[2,128]{1,0:T(2,128)S(1)}, u32[]{:S(2)}, u32[]{:S(2)}) collective-permute-start(s32[2,128]{1,0:T(2,128)S(1)} %get-tuple-element.81), channel_id=1, source_target_pairs={{0,8},{1,9},{2,10},{3,11},{4,12},{5,13},{6,14},{7,15},{8,0},{9,1},... | collective-permute-start | bytes 3080 | tf_op jit(solution)/shard_map/ppermute | solution.py:333
  7.1 2.0 %collective-permute-start.1 = (bf16[160,200]{1,0:T(8,128)(2,1)S(1)}, bf16[160,200]{1,0:T(8,128)(2,1)S(1)}, u32[]{:S(2)}, u32[]{:S(2)}) collective-permute-start(bf16[160,200]{1,0:T(8,128)(2,1)S(1)} %answer.1), channel_id=1, source_target_pairs={{0,8},{1,9},{2,10},{3,11},{4,12},{5,13},{6,14},{7,15},{8,0},{9,1},... | collective-permute-start | bytes 192008 | tf_op jit(solution)/shard_map/ppermute | solution.py:333
  11.8 2.0 %collective-permute-done.2 = bf16[32,200]{1,0:T(8,128)(2,1)S(1)} collective-permute-done((bf16[32,200]{1,0:T(8,128)(2,1)S(1)}, bf16[32,200]{1,0:T(8,128)(2,1)S(1)}, u32[]{:S(2)}, u32[]{:S(2)}) %collective-permute-start.2) | collective-permute-done | bytes 12832 | tf_op jit(solution)/shard_map/ppermute | solution.py:333
  13.8 2.7 %collective-permute-start.3 = (bf16[64,200]{1,0:T(8,128)(2,1)S(1)}, bf16[64,200]{1,0:T(8,128)(2,1)S(1)}, u32[]{:S(2)}, u32[]{:S(2)}) collective-permute-start(bf16[64,200]{1,0:T(8,128)(2,1)S(1)} %pad_maximum_fusion.9), channel_id=1, source_target_pairs={{0,4},{1,5},{2,6},{3,7},{4,0},{5,1},{6,2},{7,3},{8,12},{9,13},{10,... | collective-permute-start | bytes 76808 | tf_op jit(solution)/shard_map/ppermute | solution.py:333
  16.4 2.2 %copy-done = bf16[10368,200]{0,1:T(8,128)(2,1)S(1)} copy-done((bf16[10368,200]{0,1:T(8,128)(2,1)S(1)}, bf16[10368,200]{0,1:T(8,128)(2,1)}, u32[]{:S(2)}) %copy-start) | copy-done | bytes 4147224
  18.6 3.1 %prepare.1 = (bf16[10368,200]{1,0:T(8,128)(2,1)S(1)}, bf16[80,1152]{1,0:T(8,128)(2,1)S(1)}, bf16[1152,128]{1,0:T(8,128)(2,1)S(1)}) custom-call(bf16[200,10368]{1,0:T(8,128)(2,1)S(1)} %bitcast.19, f32[9,1152]{1,0:T(8,128)S(1)} %tile.18.taps_ref), custom_call_target="tpu_custom_call" | custom-call | flops 4000000000 | bytes 12000000 | tf_op jit(solution)/shard_map/prepare/pallas_call | solution.py:38
  21.7 2.3 %copy-done.9 = bf16[10368,200]{1,0:T(8,128)(2,1)} copy-done((bf16[10368,200]{1,0:T(8,128)(2,1)}, bf16[10368,200]{1,0:T(8,128)(2,1)S(1)}, u32[]{:S(2)}) %copy-start.9) | copy-done | bytes 4147224
  24.3 2.5 %copy-done.10 = bf16[10368,200]{1,0:T(8,128)(2,1)S(1)} copy-done((bf16[10368,200]{1,0:T(8,128)(2,1)S(1)}, bf16[10368,200]{1,0:T(8,128)(2,1)}, u32[]{:S(2)}) %copy-start.10) | copy-done | bytes 4147224
  26.8 2.6 %forward.2 = (f32[128,200]{1,0:T(8,128)S(1)}, f32[9,128,1152]{2,1,0:T(8,128)S(1)}) custom-call(s32[2,128]{1,0:T(2,128)S(1)} %copy-done.8, f32[200,1024]{1,0:T(8,128)S(1)} %bitcast.23, f32[200,128]{1,0:T(8,128)S(1)} %get-tuple-element.85.refs_0_, bf16[80,1152]{1,0:T(8,128)(2,1)S(1)} %get-tuple-element.91.refs_1_.refs_4_, f32[1,1152]{1,0:T(1,128)S(1)} %tile.20.refs_2_.refs_5_, ...), custom_call_target="tpu_custom_call" | custom-call | flops 2500000000 | bytes 7500000 | tf_op jit(solution)/shard_map/forward/pallas_call | solution.py:38
  30.5 3.0 %backward.2 = (bf16[208,128]{1,0:T(8,128)(2,1)S(1)}, f32[200,128]{1,0:T(8,128)S(1)}) custom-call(s32[2,128]{1,0:T(2,128)S(1)} %copy-done.7, bf16[128,200]{1,0:T(8,128)(2,1)S(1)} %get-tuple-element.100.grad_ref, f32[9,128,1152]{2,1,0:T(8,128)S(1)} %get-tuple-element.101.slopes, bf16[1152,128]{1,0:T(8,128)(2,1)S(1)} %get-tuple-element.102.band_t_ref, ...), custom_call_target="tpu_custom_call" | custom-call | flops 3000000000 | bytes 9000000 | tf_op jit(solution)/shard_map/backward/pallas_call | solution.py:38
  33.6 1.7 %collective-permute-start.8 = (bf16[1,208,128]{2,1,0:T(8,128)(2,1)S(1)}, bf16[1,208,128]{2,1,0:T(8,128)(2,1)S(1)}, u32[]{:S(2)}, u32[]{:S(2)}) collective-permute-start(bf16[1,208,128]{2,1,0:T(8,128)(2,1)S(1)} %bitcast.14), channel_id=1, source_target_pairs={{0,2},{1,3},{2,0},{3,1},{4,6},{5,7},{6,4},{7,5},{8,10},{9,11},{10,... | collective-permute-start | bytes 159752 | tf_op jit(solution)/shard_map/ppermute | solution.py:333
  35.7 5.6 %collective-permute-done.9 = f32[64,200]{1,0:T(8,128)S(1)} collective-permute-done((f32[64,200]{1,0:T(8,128)S(1)}, f32[64,200]{1,0:T(8,128)S(1)}, u32[]{:S(2)}, u32[]{:S(2)}) %collective-permute-start.9) | collective-permute-done | bytes 51232 | tf_op jit(solution)/shard_map/ppermute | solution.py:333
  43.7 3.5 %collective-permute-done.12.other_ref = f32[32,200]{1,0:T(8,128)S(1)} collective-permute-done((f32[32,200]{1,0:T(8,128)S(1)}, f32[32,200]{1,0:T(8,128)S(1)}, u32[]{:S(2)}, u32[]{:S(2)}) %collective-permute-start.12) | collective-permute-done | bytes 25632 | tf_op jit(solution)/shard_map/ppermute | solution.py:333
  48.1 1.7 %collective-permute-start.16 = (bf16[4,208,128]{2,1,0:T(8,128)(2,1)S(1)}, bf16[4,208,128]{2,1,0:T(8,128)(2,1)S(1)}, u32[]{:S(2)}, u32[]{:S(2)}) collective-permute-start(bf16[4,208,128]{2,1,0:T(8,128)(2,1)S(1)} %pad_maximum_fusion.refs_0_), channel_id=1, source_target_pairs={{0,8},{1,9},{2,10},{3,11},{4,12},{5,13},{6,14},{7,15},{8,0},{9,1},... | collective-permute-start | bytes 638984 | tf_op jit(solution)/shard_map/ppermute | solution.py:333
  54.4 4.1 %collective-permute-done.14 = bf16[32,200]{1,0:T(8,128)(2,1)S(1)} collective-permute-done((bf16[32,200]{1,0:T(8,128)(2,1)S(1)}, bf16[32,200]{1,0:T(8,128)(2,1)S(1)}, u32[]{:S(2)}, u32[]{:S(2)}) %collective-permute-start.14) | collective-permute-done | bytes 12832 | tf_op jit(solution)/shard_map/ppermute | solution.py:333
  60.1 3.2 %collective-permute-done.15 = bf16[64,200]{1,0:T(8,128)(2,1)S(1)} collective-permute-done((bf16[64,200]{1,0:T(8,128)(2,1)S(1)}, bf16[64,200]{1,0:T(8,128)(2,1)S(1)}, u32[]{:S(2)}, u32[]{:S(2)}) %collective-permute-start.15) | collective-permute-done | bytes 25632 | tf_op jit(solution)/shard_map/ppermute | solution.py:333
  63.3 2.2 %collective-permute-done.18.refs_3_ = bf16[4,208,128]{2,1,0:T(8,128)(2,1)S(1)} collective-permute-done((bf16[4,208,128]{2,1,0:T(8,128)(2,1)S(1)}, bf16[4,208,128]{2,1,0:T(8,128)(2,1)S(1)}, u32[]{:S(2)}, u32[]{:S(2)}) %collective-permute-start.18) | collective-permute-done | bytes 213024 | tf_op jit(solution)/shard_map/ppermute | solution.py:333
  68.5 2.5 %copy-done.12 = bf16[10368,200]{1,0:T(8,128)(2,1)S(1)} copy-done((bf16[10368,200]{1,0:T(8,128)(2,1)S(1)}, bf16[10368,200]{1,0:T(8,128)(2,1)}, u32[]{:S(2)}) %copy-start.12) | copy-done | bytes 4147224
  71.0 2.7 %forward.3 = (f32[128,200]{1,0:T(8,128)S(1)}, f32[9,128,1152]{2,1,0:T(8,128)S(1)}) custom-call(s32[2,128]{1,0:T(2,128)S(1)} %copy-done.8, f32[200,1024]{1,0:T(8,128)S(1)} %copy-done.15, f32[208,128]{1,0:T(8,128)S(1)} %get-tuple-element.121.refs_0_, f32[208,128]{1,0:T(8,128)S(1)} %collective-permute-done.19.refs_1_, ...), custom_call_target="tpu_custom_call" | custom-call | flops 2500000000 | bytes 7500000 | tf_op jit(solution)/shard_map/forward/pallas_call | solution.py:38
  74.6 2.5 %copy-done.13 = bf16[10368,200]{1,0:T(8,128)(2,1)S(1)} copy-done((bf16[10368,200]{1,0:T(8,128)(2,1)S(1)}, bf16[10368,200]{1,0:T(8,128)(2,1)}, u32[]{:S(2)}) %copy-start.13) | copy-done | bytes 4147224
  77.1 3.2 %backward.3 = (bf16[208,128]{1,0:T(8,128)(2,1)S(1)}, f32[200,128]{1,0:T(8,128)S(1)}) custom-call(s32[2,128]{1,0:T(2,128)S(1)} %copy-done.7, bf16[128,200]{1,0:T(8,128)(2,1)S(1)} %get-tuple-element.127.grad_ref, f32[9,128,1152]{2,1,0:T(8,128)S(1)} %get-tuple-element.128.slopes, bf16[1152,128]{1,0:T(8,128)(2,1)S(1)} %get-tuple-element.102.band_t_ref, ...), custom_call_target="tpu_custom_call" | custom-call | flops 3000000000 | bytes 9000000 | tf_op jit(solution)/shard_map/backward/pallas_call | solution.py:38
  82.3 3.2 %relation_sums.1.refs_0_ = f32[200,1408]{1,0:T(8,128)S(1)} custom-call(s32[4]{0:T(128)S(1)} %iota_xor_fusion.place_ref, bf16[4,208,128]{2,1,0:T(8,128)(2,1)S(1)} %pad_maximum_fusion.refs_0_, bf16[4,208,128]{2,1,0:T(8,128)(2,1)S(1)} %collective-permute-done.16.refs_1_, bf16[4,208,128]{2,1,0:T(8,128)(2,1)S(1)} %collective-permute-done.17.refs_2_, ...), custom_call_target="tpu_custom_call" | custom-call | flops 3000000000 | bytes 9000000 | tf_op jit(solution)/shard_map/relation_sums/pallas_call | solution.py:38
  85.4 2.2 %collective-permute-done.23 = f32[64,200]{1,0:T(8,128)S(1)} collective-permute-done((f32[64,200]{1,0:T(8,128)S(1)}, f32[64,200]{1,0:T(8,128)S(1)}, u32[]{:S(2)}, u32[]{:S(2)}) %collective-permute-start.23) | collective-permute-done | bytes 51232 | tf_op jit(solution)/shard_map/ppermute | solution.py:333
  88.7 3.3 %collective-permute-start.26 = (f32[32,200]{1,0:T(8,128)S(1)}, f32[32,200]{1,0:T(8,128)S(1)}, u32[]{:S(2)}, u32[]{:S(2)}) collective-permute-start(f32[32,200]{1,0:T(8,128)S(1)} %get-tuple-element.158), channel_id=1, source_target_pairs={{0,18},{1,19},{2,16},{3,17},{4,22},{5,23},{6,20},{7,21},{8,26},{9,... | collective-permute-start | bytes 76808 | tf_op jit(solution)/shard_map/ppermute | solution.py:333
  92.0 1.9 %collective-permute-done.26.other_ref = f32[32,200]{1,0:T(8,128)S(1)} collective-permute-done((f32[32,200]{1,0:T(8,128)S(1)}, f32[32,200]{1,0:T(8,128)S(1)}, u32[]{:S(2)}, u32[]{:S(2)}) %collective-permute-start.26) | collective-permute-done | bytes 25632 | tf_op jit(solution)/shard_map/ppermute | solution.py:333
  93.9 2.2 %collective-permute-done.24 = bf16[2,208,128]{2,1,0:T(8,128)(2,1)S(1)} collective-permute-done((bf16[2,208,128]{2,1,0:T(8,128)(2,1)S(1)}, bf16[2,208,128]{2,1,0:T(8,128)(2,1)S(1)}, u32[]{:S(2)}, u32[]{:S(2)}) %collective-permute-start.24) | collective-permute-done | bytes 106528 | tf_op jit(solution)/shard_map/ppermute | solution.py:333
  98.3 1.7 %entity_update.3 = (f32[200,1024]{1,0:T(8,128)}, f32[1,1024]{1,0:T(1,128)}) custom-call(s32[2,128]{1,0:T(2,128)S(1)} %copy-done.8, s32[2,128]{1,0:T(2,128)S(1)} %collective-permute-done.5.next_ref.asked_ref, s32[2,128]{1,0:T(2,128)S(1)} %collective-permute-done.5.next_ref.asked_ref, f32[200,1024]{1,0:T(8,128)S(1)} %copy-done.15, ...), custom_call_target="tpu_custom_call" | custom-call | flops 1500000000 | bytes 4500000 | tf_op jit(solution)/shard_map/entity_update/pallas_call | solution.py:38
  100.0 3.3 %collective-permute-done.27.refs_1_ = bf16[4,208,128]{2,1,0:T(8,128)(2,1)S(1)} collective-permute-done((bf16[4,208,128]{2,1,0:T(8,128)(2,1)S(1)}, bf16[4,208,128]{2,1,0:T(8,128)(2,1)S(1)}, u32[]{:S(2)}, u32[]{:S(2)}) %collective-permute-start.27) | collective-permute-done | bytes 213024 | tf_op jit(solution)/shard_map/ppermute | solution.py:333
  105.3 2.6 %early_sums.1 = (f32[200,1408]{1,0:T(8,128)S(1)}, f32[200,1408]{1,0:T(8,128)S(1)}) custom-call(s32[4]{0:T(128)S(1)} %iota_xor_fusion.place_ref, bf16[4,208,128]{2,1,0:T(8,128)(2,1)S(1)} %constant_dynamic-update-slice_fusion.refs_0_, bf16[4,208,128]{2,1,0:T(8,128)(2,1)S(1)} %collective-permute-done.27.refs_1_, ...), custom_call_target="tpu_custom_call" | custom-call | flops 3000000000 | bytes 9000000 | tf_op jit(solution)/shard_map/early_sums/pallas_call | solution.py:38
  107.8 2.0 %collective-permute-done.30.refs_0_ = bf16[4,208,128]{2,1,0:T(8,128)(2,1)S(1)} collective-permute-done((bf16[4,208,128]{2,1,0:T(8,128)(2,1)S(1)}, bf16[4,208,128]{2,1,0:T(8,128)(2,1)S(1)}, u32[]{:S(2)}, u32[]{:S(2)}) %collective-permute-start.30) | collective-permute-done | bytes 213024 | tf_op jit(solution)/shard_map/ppermute | solution.py:333
  111.2 2.8 %collective-permute-done.31.refs_3_ = f32[200,1408]{1,0:T(8,128)S(1)} collective-permute-done((f32[200,1408]{1,0:T(8,128)S(1)}, f32[200,1408]{1,0:T(8,128)S(1)}, u32[]{:S(2)}, u32[]{:S(2)}) %collective-permute-start.31) | collective-permute-done | bytes 1126432 | tf_op jit(solution)/shard_map/ppermute | solution.py:333
  114.0 1.7 %relation_update.1 = (f32[200,1387]{1,0:T(8,128)}, f32[1,1387]{1,0:T(1,128)S(1)}) custom-call(f32[200,1387]{1,0:T(8,128)S(1)} %bitcast.21, f32[1,1387]{1,0:T(1,128)S(1)} %broadcast_in_dim.15.state_ref, f32[200,1408]{1,0:T(8,128)S(1)} %relation_sums.1.refs_0_, f32[200,1408]{1,0:T(8,128)S(1)} %collective-permute-done.29.refs_1_, ...), custom_call_target="tpu_custom_call" | custom-call | flops 2000000000 | bytes 6000000 | tf_op jit(solution)/shard_map/relation_update/pallas_call | solution.py:38
  (124 shorter events, 30.1 us)
Async XLA Ops:
  2.1 4.5 %collective-permute-start = (s32[2,128]{1,0:T(2,128)S(1)}, s32[2,128]{1,0:T(2,128)S(1)}, u32[]{:S(2)}, u32[]{:S(2)}) collective-permute-start(s32[2,128]{1,0:T(2,128)S(1)} %get-tuple-element.81), channel_id=1, source_target_pairs={{0,8},{1,9},{2,10},{3,11},{4,12},{5,13},{6,14},{7,15},{8,0},{9,1},... | collective-permute-start | bytes 3080 | tf_op jit(solution)/shard_map/ppermute | solution.py:333
  5.1 24.9 %collective-permute-start.5 = (s32[2,128]{1,0:T(2,128)S(1)}, s32[2,128]{1,0:T(2,128)S(1)}, u32[]{:S(2)}, u32[]{:S(2)}) collective-permute-start(s32[2,128]{1,0:T(2,128)S(1)} %get-tuple-element.98), channel_id=1, source_target_pairs={{0,16},{1,17},{2,18},{3,19},{4,20},{5,21},{6,22},{7,23},{8,24},{9,... | collective-permute-start | bytes 3080 | tf_op jit(solution)/shard_map/ppermute | solution.py:333
  6.6 23.4 %collective-permute-start.6 = (s32[2,128]{1,0:T(2,128)S(1)}, s32[2,128]{1,0:T(2,128)S(1)}, u32[]{:S(2)}, u32[]{:S(2)}) collective-permute-start(s32[2,128]{1,0:T(2,128)S(1)} %copy-done.7), channel_id=1, source_target_pairs={{0,1},{1,0},{2,3},{3,2},{4,5},{5,4},{6,7},{7,6},{8,9},{9,8},{10,11... | collective-permute-start | bytes 3080 | tf_op jit(solution)/shard_map/ppermute | solution.py:333
  7.1 6.7 %collective-permute-start.1 = (bf16[160,200]{1,0:T(8,128)(2,1)S(1)}, bf16[160,200]{1,0:T(8,128)(2,1)S(1)}, u32[]{:S(2)}, u32[]{:S(2)}) collective-permute-start(bf16[160,200]{1,0:T(8,128)(2,1)S(1)} %answer.1), channel_id=1, source_target_pairs={{0,8},{1,9},{2,10},{3,11},{4,12},{5,13},{6,14},{7,15},{8,0},{9,1},... | collective-permute-start | bytes 192008 | tf_op jit(solution)/shard_map/ppermute | solution.py:333
  9.1 4.6 %collective-permute-start.2 = (bf16[32,200]{1,0:T(8,128)(2,1)S(1)}, bf16[32,200]{1,0:T(8,128)(2,1)S(1)}, u32[]{:S(2)}, u32[]{:S(2)}) collective-permute-start(bf16[32,200]{1,0:T(8,128)(2,1)S(1)} %slice.72), channel_id=1, source_target_pairs={{0,10},{1,11},{2,8},{3,9},{4,14},{5,15},{6,12},{7,13},{8,2},{9,3},... | collective-permute-start | bytes 38408 | tf_op jit(solution)/shard_map/ppermute | solution.py:333
  13.8 10.4 %collective-permute-start.3 = (bf16[64,200]{1,0:T(8,128)(2,1)S(1)}, bf16[64,200]{1,0:T(8,128)(2,1)S(1)}, u32[]{:S(2)}, u32[]{:S(2)}) collective-permute-start(bf16[64,200]{1,0:T(8,128)(2,1)S(1)} %pad_maximum_fusion.9), channel_id=1, source_target_pairs={{0,4},{1,5},{2,6},{3,7},{4,0},{5,1},{6,2},{7,3},{8,12},{9,13},{10,... | collective-permute-start | bytes 76808 | tf_op jit(solution)/shard_map/ppermute | solution.py:333
  24.2 5.3 %collective-permute-start.4 = (bf16[128,200]{1,0:T(8,128)(2,1)S(1)}, bf16[128,200]{1,0:T(8,128)(2,1)S(1)}, u32[]{:S(2)}, u32[]{:S(2)}) collective-permute-start(bf16[128,200]{1,0:T(8,128)(2,1)S(1)} %pad_maximum_fusion.7), channel_id=1, source_target_pairs={{0,1},{1,0},{2,3},{3,2},{4,5},{5,4},{6,7},{7,6},{8,9},{9,8},{10,11... | collective-permute-start | bytes 153608 | tf_op jit(solution)/shard_map/ppermute | solution.py:333
  30.0 3.6 %collective-permute-start.7 = (f32[128,200]{1,0:T(8,128)S(1)}, f32[128,200]{1,0:T(8,128)S(1)}, u32[]{:S(2)}, u32[]{:S(2)}) collective-permute-start(f32[128,200]{1,0:T(8,128)S(1)} %slice.57), channel_id=1, source_target_pairs={{0,1},{1,0},{2,3},{3,2},{4,5},{5,4},{6,7},{7,6},{8,9},{9,8},{10,11... | collective-permute-start | bytes 307208 | tf_op jit(solution)/shard_map/ppermute | solution.py:333
  33.6 7.7 %collective-permute-start.8 = (bf16[1,208,128]{2,1,0:T(8,128)(2,1)S(1)}, bf16[1,208,128]{2,1,0:T(8,128)(2,1)S(1)}, u32[]{:S(2)}, u32[]{:S(2)}) collective-permute-start(bf16[1,208,128]{2,1,0:T(8,128)(2,1)S(1)} %bitcast.14), channel_id=1, source_target_pairs={{0,2},{1,3},{2,0},{3,1},{4,6},{5,7},{6,4},{7,5},{8,10},{9,11},{10,... | collective-permute-start | bytes 159752 | tf_op jit(solution)/shard_map/ppermute | solution.py:333
  35.3 6.0 %collective-permute-start.9 = (f32[64,200]{1,0:T(8,128)S(1)}, f32[64,200]{1,0:T(8,128)S(1)}, u32[]{:S(2)}, u32[]{:S(2)}) collective-permute-start(f32[64,200]{1,0:T(8,128)S(1)} %slice.73), channel_id=1, source_target_pairs={{0,4},{1,5},{2,6},{3,7},{4,0},{5,1},{6,2},{7,3},{8,12},{9,13},{10,... | collective-permute-start | bytes 153608 | tf_op jit(solution)/shard_map/ppermute | solution.py:333
  41.3 6.8 %collective-permute-start.11 = (f32[160,200]{1,0:T(8,128)S(1)}, f32[160,200]{1,0:T(8,128)S(1)}, u32[]{:S(2)}, u32[]{:S(2)}) collective-permute-start(f32[160,200]{1,0:T(8,128)S(1)} %pad_maximum_fusion.1), channel_id=1, source_target_pairs={{0,8},{1,9},{2,10},{3,11},{4,12},{5,13},{6,14},{7,15},{8,0},{9,1},... | collective-permute-start | bytes 384008 | tf_op jit(solution)/shard_map/ppermute | solution.py:333
  41.9 6.2 %collective-permute-start.10 = (bf16[2,208,128]{2,1,0:T(8,128)(2,1)S(1)}, bf16[2,208,128]{2,1,0:T(8,128)(2,1)S(1)}, u32[]{:S(2)}, u32[]{:S(2)}) collective-permute-start(bf16[2,208,128]{2,1,0:T(8,128)(2,1)S(1)} %pad_maximum_fusion.5), channel_id=1, source_target_pairs={{0,4},{1,5},{2,6},{3,7},{4,0},{5,1},{6,2},{7,3},{8,12},{9,13},{10,... | collective-permute-start | bytes 319496 | tf_op jit(solution)/shard_map/ppermute | solution.py:333
  42.0 5.1 %collective-permute-start.12 = (f32[32,200]{1,0:T(8,128)S(1)}, f32[32,200]{1,0:T(8,128)S(1)}, u32[]{:S(2)}, u32[]{:S(2)}) collective-permute-start(f32[32,200]{1,0:T(8,128)S(1)} %get-tuple-element.160), channel_id=1, source_target_pairs={{0,10},{1,11},{2,8},{3,9},{4,14},{5,15},{6,12},{7,13},{8,2},{9,3},... | collective-permute-start | bytes 76808 | tf_op jit(solution)/shard_map/ppermute | solution.py:333
  48.1 11.6 %collective-permute-start.16 = (bf16[4,208,128]{2,1,0:T(8,128)(2,1)S(1)}, bf16[4,208,128]{2,1,0:T(8,128)(2,1)S(1)}, u32[]{:S(2)}, u32[]{:S(2)}) collective-permute-start(bf16[4,208,128]{2,1,0:T(8,128)(2,1)S(1)} %pad_maximum_fusion.refs_0_), channel_id=1, source_target_pairs={{0,8},{1,9},{2,10},{3,11},{4,12},{5,13},{6,14},{7,15},{8,0},{9,1},... | collective-permute-start | bytes 638984 | tf_op jit(solution)/shard_map/ppermute | solution.py:333
  51.9 6.5 %collective-permute-start.13 = (bf16[160,200]{1,0:T(8,128)(2,1)S(1)}, bf16[160,200]{1,0:T(8,128)(2,1)S(1)}, u32[]{:S(2)}, u32[]{:S(2)}) collective-permute-start(bf16[160,200]{1,0:T(8,128)(2,1)S(1)} %get-tuple-element.114), channel_id=1, source_target_pairs={{0,16},{1,17},{2,18},{3,19},{4,20},{5,21},{6,22},{7,23},{8,24},{9,... | collective-permute-start | bytes 192008 | tf_op jit(solution)/shard_map/ppermute | solution.py:333
  53.4 5.0 %collective-permute-start.14 = (bf16[32,200]{1,0:T(8,128)(2,1)S(1)}, bf16[32,200]{1,0:T(8,128)(2,1)S(1)}, u32[]{:S(2)}, u32[]{:S(2)}) collective-permute-start(bf16[32,200]{1,0:T(8,128)(2,1)S(1)} %slice.63), channel_id=1, source_target_pairs={{0,18},{1,19},{2,16},{3,17},{4,22},{5,23},{6,20},{7,21},{8,26},{9,... | collective-permute-start | bytes 38408 | tf_op jit(solution)/shard_map/ppermute | solution.py:333
  53.4 9.9 %collective-permute-start.17 = (bf16[4,208,128]{2,1,0:T(8,128)(2,1)S(1)}, bf16[4,208,128]{2,1,0:T(8,128)(2,1)S(1)}, u32[]{:S(2)}, u32[]{:S(2)}) collective-permute-start(bf16[4,208,128]{2,1,0:T(8,128)(2,1)S(1)} %pad_maximum_fusion.refs_0_), channel_id=1, source_target_pairs={{0,16},{1,17},{2,18},{3,19},{4,20},{5,21},{6,22},{7,23},{8,24},{9,... | collective-permute-start | bytes 638984 | tf_op jit(solution)/shard_map/ppermute | solution.py:333
  58.4 4.9 %collective-permute-start.15 = (bf16[64,200]{1,0:T(8,128)(2,1)S(1)}, bf16[64,200]{1,0:T(8,128)(2,1)S(1)}, u32[]{:S(2)}, u32[]{:S(2)}) collective-permute-start(bf16[64,200]{1,0:T(8,128)(2,1)S(1)} %pad_maximum_fusion.10), channel_id=1, source_target_pairs={{0,4},{1,5},{2,6},{3,7},{4,0},{5,1},{6,2},{7,3},{8,12},{9,13},{10,... | collective-permute-start | bytes 76808 | tf_op jit(solution)/shard_map/ppermute | solution.py:333
  59.7 5.8 %collective-permute-start.18 = (bf16[4,208,128]{2,1,0:T(8,128)(2,1)S(1)}, bf16[4,208,128]{2,1,0:T(8,128)(2,1)S(1)}, u32[]{:S(2)}, u32[]{:S(2)}) collective-permute-start(bf16[4,208,128]{2,1,0:T(8,128)(2,1)S(1)} %collective-permute-done.16.refs_1_), channel_id=1, source_target_pairs={{0,16},{1,17},{2,18},{3,19},{4,20},{5,21},{6,22},{7,23},{8,24},{9,... | collective-permute-start | bytes 638984 | tf_op jit(solution)/shard_map/ppermute | solution.py:333
  67.0 1.3 %collective-permute-start.20 = (bf16[128,200]{1,0:T(8,128)(2,1)S(1)}, bf16[128,200]{1,0:T(8,128)(2,1)S(1)}, u32[]{:S(2)}, u32[]{:S(2)}) collective-permute-start(bf16[128,200]{1,0:T(8,128)(2,1)S(1)} %pad_maximum_fusion.8), channel_id=1, source_target_pairs={{0,1},{1,0},{2,3},{3,2},{4,5},{5,4},{6,7},{7,6},{8,9},{9,8},{10,11... | collective-permute-start | bytes 153608 | tf_op jit(solution)/shard_map/ppermute | solution.py:333
  67.0 1.4 %collective-permute-start.19 = (f32[208,128]{1,0:T(8,128)S(1)}, f32[208,128]{1,0:T(8,128)S(1)}, u32[]{:S(2)}, u32[]{:S(2)}) collective-permute-start(f32[208,128]{1,0:T(8,128)S(1)} %get-tuple-element.122), channel_id=1, source_target_pairs={{0,1},{1,0},{2,3},{3,2},{4,5},{5,4},{6,7},{7,6},{8,9},{9,8},{10,11... | collective-permute-start | bytes 319496 | tf_op jit(solution)/shard_map/ppermute | solution.py:333
  74.2 6.2 %collective-permute-start.21 = (f32[128,200]{1,0:T(8,128)S(1)}, f32[128,200]{1,0:T(8,128)S(1)}, u32[]{:S(2)}, u32[]{:S(2)}) collective-permute-start(f32[128,200]{1,0:T(8,128)S(1)} %slice.66), channel_id=1, source_target_pairs={{0,1},{1,0},{2,3},{3,2},{4,5},{5,4},{6,7},{7,6},{8,9},{9,8},{10,11... | collective-permute-start | bytes 307208 | tf_op jit(solution)/shard_map/ppermute | solution.py:333
  80.4 7.3 %collective-permute-start.22 = (bf16[1,208,128]{2,1,0:T(8,128)(2,1)S(1)}, bf16[1,208,128]{2,1,0:T(8,128)(2,1)S(1)}, u32[]{:S(2)}, u32[]{:S(2)}) collective-permute-start(bf16[1,208,128]{2,1,0:T(8,128)(2,1)S(1)} %bitcast.17), channel_id=1, source_target_pairs={{0,2},{1,3},{2,0},{3,1},{4,6},{5,7},{6,4},{7,5},{8,10},{9,11},{10,... | collective-permute-start | bytes 159752 | tf_op jit(solution)/shard_map/ppermute | solution.py:333
  81.2 6.5 %collective-permute-start.23 = (f32[64,200]{1,0:T(8,128)S(1)}, f32[64,200]{1,0:T(8,128)S(1)}, u32[]{:S(2)}, u32[]{:S(2)}) collective-permute-start(f32[64,200]{1,0:T(8,128)S(1)} %slice.77), channel_id=1, source_target_pairs={{0,4},{1,5},{2,6},{3,7},{4,0},{5,1},{6,2},{7,3},{8,12},{9,13},{10,... | collective-permute-start | bytes 153608 | tf_op jit(solution)/shard_map/ppermute | solution.py:333
  87.7 16.1 %collective-permute-start.29 = (f32[200,1408]{1,0:T(8,128)S(1)}, f32[200,1408]{1,0:T(8,128)S(1)}, u32[]{:S(2)}, u32[]{:S(2)}) collective-permute-start(f32[200,1408]{1,0:T(8,128)S(1)} %relation_sums.1.refs_0_), channel_id=1, source_target_pairs={{0,1},{1,0},{2,3},{3,2},{4,5},{5,4},{6,7},{7,6},{8,9},{9,8},{10,11... | collective-permute-start | bytes 3379208 | tf_op jit(solution)/shard_map/ppermute | solution.py:333
  87.8 8.3 %collective-permute-start.25 = (f32[160,200]{1,0:T(8,128)S(1)}, f32[160,200]{1,0:T(8,128)S(1)}, u32[]{:S(2)}, u32[]{:S(2)}) collective-permute-start(f32[160,200]{1,0:T(8,128)S(1)} %pad_maximum_fusion.2), channel_id=1, source_target_pairs={{0,16},{1,17},{2,18},{3,19},{4,20},{5,21},{6,22},{7,23},{8,24},{9,... | collective-permute-start | bytes 384008 | tf_op jit(solution)/shard_map/ppermute | solution.py:333
  88.3 7.8 %collective-permute-start.24 = (bf16[2,208,128]{2,1,0:T(8,128)(2,1)S(1)}, bf16[2,208,128]{2,1,0:T(8,128)(2,1)S(1)}, u32[]{:S(2)}, u32[]{:S(2)}) collective-permute-start(bf16[2,208,128]{2,1,0:T(8,128)(2,1)S(1)} %pad_maximum_fusion.6), channel_id=1, source_target_pairs={{0,4},{1,5},{2,6},{3,7},{4,0},{5,1},{6,2},{7,3},{8,12},{9,13},{10,... | collective-permute-start | bytes 319496 | tf_op jit(solution)/shard_map/ppermute | solution.py:333
  88.7 5.2 %collective-permute-start.26 = (f32[32,200]{1,0:T(8,128)S(1)}, f32[32,200]{1,0:T(8,128)S(1)}, u32[]{:S(2)}, u32[]{:S(2)}) collective-permute-start(f32[32,200]{1,0:T(8,128)S(1)} %get-tuple-element.158), channel_id=1, source_target_pairs={{0,18},{1,19},{2,16},{3,17},{4,22},{5,23},{6,20},{7,21},{8,26},{9,... | collective-permute-start | bytes 76808 | tf_op jit(solution)/shard_map/ppermute | solution.py:333
  96.1 7.3 %collective-permute-start.27 = (bf16[4,208,128]{2,1,0:T(8,128)(2,1)S(1)}, bf16[4,208,128]{2,1,0:T(8,128)(2,1)S(1)}, u32[]{:S(2)}, u32[]{:S(2)}) collective-permute-start(bf16[4,208,128]{2,1,0:T(8,128)(2,1)S(1)} %constant_dynamic-update-slice_fusion.refs_0_), channel_id=1, source_target_pairs={{0,8},{1,9},{2,10},{3,11},{4,12},{5,13},{6,14},{7,15},{8,0},{9,1},... | collective-permute-start | bytes 638984 | tf_op jit(solution)/shard_map/ppermute | solution.py:333
  96.9 6.9 %collective-permute-start.28 = (bf16[4,208,128]{2,1,0:T(8,128)(2,1)S(1)}, bf16[4,208,128]{2,1,0:T(8,128)(2,1)S(1)}, u32[]{:S(2)}, u32[]{:S(2)}) collective-permute-start(bf16[4,208,128]{2,1,0:T(8,128)(2,1)S(1)} %constant_dynamic-update-slice_fusion.refs_0_), channel_id=1, source_target_pairs={{0,16},{1,17},{2,18},{3,19},{4,20},{5,21},{6,22},{7,23},{8,24},{9,... | collective-permute-start | bytes 638984 | tf_op jit(solution)/shard_map/ppermute | solution.py:333
  103.8 6.0 %collective-permute-start.30 = (bf16[4,208,128]{2,1,0:T(8,128)(2,1)S(1)}, bf16[4,208,128]{2,1,0:T(8,128)(2,1)S(1)}, u32[]{:S(2)}, u32[]{:S(2)}) collective-permute-start(bf16[4,208,128]{2,1,0:T(8,128)(2,1)S(1)} %collective-permute-done.27.refs_1_), channel_id=1, source_target_pairs={{0,16},{1,17},{2,18},{3,19},{4,20},{5,21},{6,22},{7,23},{8,24},{9,... | collective-permute-start | bytes 638984 | tf_op jit(solution)/shard_map/ppermute | solution.py:333
  111.2 2.8 %collective-permute-start.31 = (f32[200,1408]{1,0:T(8,128)S(1)}, f32[200,1408]{1,0:T(8,128)S(1)}, u32[]{:S(2)}, u32[]{:S(2)}) collective-permute-start(f32[200,1408]{1,0:T(8,128)S(1)} %late_sums.1.refs_2_), channel_id=1, source_target_pairs={{0,1},{1,0},{2,3},{3,2},{4,5},{5,4},{6,7},{7,6},{8,9},{9,8},{10,11... | collective-permute-start | bytes 3379208 | tf_op jit(solution)/shard_map/ppermute | solution.py:333
  (19 other events, 76.5 us)

commit v4 on v3

--- a/solution.py
+++ b/solution.py
@@ -18,6 +18,8 @@
 PACK = 208
 LANES = 128
 ROUNDS = 2
+LIM = 24
+LIMP = 28
 
 negative_weight = 0.03125
 learn_rate = 0.5
@@ -28,17 +30,31 @@
 BOTH = ("group", "shard")
 VMEM = pl.BlockSpec(memory_space=pltpu.VMEM)
 SMEM = pl.BlockSpec(memory_space=pltpu.SMEM)
+HBM = pl.BlockSpec(memory_space=pltpu.HBM)
 
 
 def shaped(shape, dtype=f32):
     return jax.ShapeDtypeStruct(shape, dtype)
 
 
-def call(kernel, name, micros, out_shape, args, scratch=(), scalars=0, limit=16):
+def call(kernel, name, micros, out_shape, args, scratch=(), scalars=0, limit=16, far=(), near=(), near_out=(), alias=None):
+    places = [SMEM] * scalars + [VMEM] * (len(args) - scalars)
+    args = [
+        pltpu.with_memory_space_constraint(arg, pltpu.HBM)
+        if index in far
+        else pltpu.with_memory_space_constraint(arg, pltpu.VMEM)
+        if index in near
+        else arg
+        for index, arg in enumerate(args)
+    ]
     return pl.pallas_call(
         kernel,
-        out_shape=out_shape,
-        in_specs=[SMEM] * scalars + [VMEM] * (len(args) - scalars),
+        out_shape=[
+            pltpu.VMEM(out.shape, out.dtype) if index in near_out else out
+            for index, out in enumerate(out_shape)
+        ],
+        input_output_aliases=alias or {},
+        in_specs=[HBM if index in far else spec for index, spec in enumerate(places)],
         out_specs=[VMEM] * len(out_shape),
         scratch_shapes=list(scratch),
         compiler_params=pltpu.CompilerParams(vmem_limit_bytes=limit * 1024 * 1024),
@@ -89,7 +105,16 @@
     return jnp.transpose(jnp.concatenate([values, jnp.zeros((rest, D), f32)], axis=0))
 
 
-def wanted_kernel(tails_ref, negatives_ref, *outs):
+def wanted_kernel(tails_hbm, negatives_hbm, *refs):
+    outs, (tails_ref, negatives_ref, sems) = refs[:ROUNDS], refs[ROUNDS:]
+    copies = [
+        pltpu.make_async_copy(tails_hbm, tails_ref, sems.at[0]),
+        pltpu.make_async_copy(negatives_hbm, negatives_ref, sems.at[1]),
+    ]
+    for copy in copies:
+        copy.start()
+    for copy in copies:
+        copy.wait()
     for index, out in enumerate(outs):
         out[0:1, :] = tails_ref[index : index + 1, :]
         out[1:2, :] = padded(negatives_ref[index : index + 1, :], LANES)
@@ -108,24 +133,12 @@
     pick_answer(ent_ref[...].astype(bf16), ids_ref, negatives, out)
 
 
-def prepare_kernel(fc_ref, taps_ref, fc_out, band_out, band_t_out, left, right):
-    blank = jnp.zeros((2 * LANES - D, LANES), f32)
-    for index in range(fc_ref.shape[1] // LANES):
-        at = slice(index * LANES, (index + 1) * LANES)
-        block = fc_ref[:, at].astype(f32)
-        left[at, :] = jnp.transpose(block[:LANES])
-        right[at, :] = jnp.transpose(jnp.concatenate([block[LANES:], blank], axis=0))
-    spots = SIDE * SIDE
-
-    def regroup(index, carry):
-        low = left[pl.ds(index, FILTERS, stride=spots), :]
-        high = right[pl.ds(index, FILTERS, stride=spots), :]
-        at = pl.ds(pl.multiple_of(index * FILTERS, FILTERS), FILTERS)
-        fc_out[at, :LANES] = low.astype(bf16)
-        fc_out[at, LANES:] = high[:, : D - LANES].astype(bf16)
-        return carry
-
-    lax.fori_loop(0, spots, regroup, 0, unroll=9)
+def prepare(fc_hbm, taps_ref, band_out, band_t_out, fc_ref, sems, left, right):
+    copies = []
+    for pair in range(PAIRS):
+        at = pl.ds(pair * WIDE, WIDE)
+        copies.append(pltpu.make_async_copy(fc_hbm.at[:, at], fc_ref.at[:, at], sems.at[pair]))
+        copies[-1].start()
     group = lax.broadcasted_iota(i32, (WINDOW, WIDE), 1) >> 5
     start = group + jnp.where(group >= SIDE, EMB_W - SIDE, 0)
     gap = lax.broadcasted_iota(i32, (WINDOW, WIDE), 0) - start
@@ -139,6 +152,25 @@
     band_t_out[...] = jnp.transpose(
         jnp.concatenate([band, jnp.zeros((LANES - WINDOW, WIDE), f32)], axis=0)
     ).astype(bf16)
+    for copy in copies:
+        copy.wait()
+    blank = jnp.zeros((2 * LANES - D, LANES), f32)
+    for index in range(fc_ref.shape[1] // LANES):
+        at = slice(index * LANES, (index + 1) * LANES)
+        block = fc_ref[:, at].astype(f32)
+        left[at, :] = jnp.transpose(block[:LANES])
+        right[at, :] = jnp.transpose(jnp.concatenate([block[LANES:], blank], axis=0))
+
+
+def regroup(pair, fc_out, left, right):
+    spots = SIDE * SIDE
+    each = spots // PAIRS
+    for index in range(each):
+        low = left[pl.ds(pair * each + index, FILTERS, stride=spots), :]
+        high = right[pl.ds(pair * each + index, FILTERS, stride=spots), :]
+        at = slice(index * FILTERS, (index + 1) * FILTERS)
+        fc_out[pair, at, :LANES] = low.astype(bf16)
+        fc_out[pair, at, LANES:] = high[:, : D - LANES].astype(bf16)
 
 
 def rows_kernel(ids_ref, rel_ref, state_ref, first_out, later_out, state_out, table):
@@ -168,18 +200,7 @@
     state_out[...] = jnp.sum(total, axis=0, keepdims=True)
 
 
-def forward_kernel(round_index, heads_ref, ent_ref, *refs):
-    if round_index == 0:
-        rel_rows = refs[0][...]
-        refs = refs[1:]
-    else:
-        gradient = (refs[0][...] + refs[1][...])[:D, :]
-        state = refs[3][...] + jnp.mean(gradient * gradient, axis=0, keepdims=True)
-        rel_rows = refs[2][...] - gradient * (learn_rate * lax.rsqrt(state))
-        rel_rows = rel_rows.astype(bf16).astype(f32)
-        refs = refs[4:]
-    band_ref, bias_ref, fc_ref, fcb_ref, pre2_out, slopes, picture, work = refs
-    heads = heads_ref[round_index : round_index + 1, :]
+def convolve(heads, rel_rows, ent_ref, band_ref, bias_ref, fcb_ref, fc_ref, pre2_out, slopes, picture, work, ready):
     table = ent_ref[...].astype(bf16)
     picture[:D, :] = dot(table, hits(heads, table.shape[1]))
     picture[D:, :] = rel_rows
@@ -192,8 +213,39 @@
         act = pre1 * sigma
         slopes[pair] = sigma + act * (1.0 - sigma)
         work[pair] = act.astype(bf16)
+        ready(pair)
         pre2 = pre2 + dot(work[pair], fc_ref[pair])
     pre2_out[...] = pre2 + fcb_ref[...]
+
+
+def first_kernel(
+    fc_hbm, taps_ref, heads_ref, ent_ref, rel_ref, bias_ref, fcb_ref,
+    pre2_out, slopes, fc_out, band_out, band_t_out,
+    picture, work, left, right, fc_ref, sems,
+):
+    prepare(fc_hbm, taps_ref, band_out, band_t_out, fc_ref, sems, left, right)
+
+    def ready(pair):
+        regroup(pair, fc_out, left, right)
+
+    convolve(
+        heads_ref[0:1, :], rel_ref[...], ent_ref, band_out, bias_ref, fcb_ref, fc_out,
+        pre2_out, slopes, picture, work, ready,
+    )
+
+
+def forward_kernel(
+    round_index, fc_ref, heads_ref, ent_ref, own_ref, other_ref, rows_ref, state_ref, band_ref, bias_ref, fcb_ref,
+    pre2_out, slopes, _, picture, work,
+):
+    gradient = (own_ref[...] + other_ref[...])[:D, :]
+    state = state_ref[...] + jnp.mean(gradient * gradient, axis=0, keepdims=True)
+    rel_rows = rows_ref[...] - gradient * (learn_rate * lax.rsqrt(state))
+    rel_rows = rel_rows.astype(bf16).astype(f32)
+    convolve(
+        heads_ref[round_index : round_index + 1, :], rel_rows, ent_ref, band_ref, bias_ref, fcb_ref, fc_ref,
+        pre2_out, slopes, picture, work, lambda pair: None,
+    )
 
 
 def score_kernel(pre2_ref, tail_ref, neg_ref, grad_out, tail_out, neg_out):
@@ -213,7 +265,9 @@
     neg_out[...] = dot_tn(neg_grad, query)
 
 
-def backward_kernel(round_index, relations_ref, grad_ref, slopes, band_t_ref, fc_ref, pack_out, head_out, work, total):
+def backward_kernel(
+    round_index, fc_ref, relations_ref, grad_ref, slopes, band_t_ref, pack_out, head_out, _, work, total
+):
     pre2_grad = grad_ref[...]
     total[...] = jnp.zeros_like(total)
     for pair in range(PAIRS):
@@ -321,7 +375,7 @@
         self.shards = shards
         self.near = [1 << bit for bit in range(1, shards.bit_length() - 1)]
         self.far = [shards << bit for bit in range(groups.bit_length() - 1)]
-        self.lead = self.near + self.far[:-2]
+        self.lead = self.near[::-1] + self.far[:-2]
 
     def route(self, mask):
         return [(at, at ^ mask) for at in range(self.total)]
@@ -370,7 +424,7 @@
     rel = relation_rows.T
     rel_state = relation_state[None, :]
     bias2 = fc_bias[None, :]
-    next_door, beyond = plan.near[0], plan.near[1:]
+    next_door, beyond = plan.near[-1], plan.near[:-1]
 
     def asked_rows(answer, bit):
         near = send(answer, plan.partner(bit))
@@ -378,13 +432,15 @@
         return near, side
 
     wanted = call(
-        wanted_kernel, "wanted", 1, [shaped((2, LANES), i32)] * ROUNDS, (tail_ids, neg_ids)
+        wanted_kernel,
+        "wanted",
+        1,
+        [shaped((2, LANES), i32)] * ROUNDS,
+        (tail_ids, neg_ids),
+        [pltpu.VMEM(tail_ids.shape, i32), pltpu.VMEM(neg_ids.shape, i32), pltpu.SemaphoreType.DMA((2,))],
+        far=(0, 1),
     )
     requested = [send(wanted[0], plan.partner(0))]
-    answer_shape = shaped((number + negatives, D), bf16)
-    (answer,) = call(
-        functools.partial(answer_kernel, negatives), "answer", 1, [answer_shape], (requested[0], ent)
-    )
     rel_first, rel_later, state_later = call(
         rows_kernel,
         "relation_rows",
@@ -393,30 +449,48 @@
         (rel_ids, rel, rel_state),
         [pltpu.VMEM((D, wide), f32)],
     )
+    requested[0], rel_first, rel_later, state_later = together(
+        requested[0], rel_first, rel_later, state_later
+    )
+    answer_shape = shaped((number + negatives, D), bf16)
+    (answer,) = call(
+        functools.partial(answer_kernel, negatives), "answer", 1, [answer_shape], (requested[0], ent)
+    )
     near, side = asked_rows(answer, 0)
-    near, side, rel_first, rel_later, state_later = together(
-        near, side, rel_first, rel_later, state_later
-    )
-    negset = jnp.concatenate([near[number:], side], axis=0)
     taps = jnp.tile(conv_weight.reshape(FILTERS, 9).T.astype(f32), (1, WIDE // FILTERS))
     bias = jnp.tile(conv_bias[None, :], (1, WIDE // FILTERS))
-    fc, band, band_t = call(
-        prepare_kernel,
-        "prepare",
-        4,
-        [shaped((features, D), bf16), shaped((WINDOW, WIDE), bf16), shaped((WIDE, LANES), bf16)],
-        (fc_weight.T, taps),
-        [pltpu.VMEM((features, LANES), f32), pltpu.VMEM((features, LANES), f32)],
-        limit=24,
-    )
-    fc = fc.reshape(PAIRS, WIDE, D)
+    pre2, slopes, fc, band, band_t = call(
+        first_kernel,
+        "first_forward",
+        6,
+        [
+            shaped((number, D)),
+            shaped((PAIRS, number, WIDE)),
+            shaped((PAIRS, WIDE, D), bf16),
+            shaped((WINDOW, WIDE), bf16),
+            shaped((WIDE, LANES), bf16),
+        ],
+        (fc_weight.T, taps, head_ids, ent, rel_first, bias, bias2),
+        [
+            pltpu.VMEM((PIXELS, number), f32),
+            pltpu.VMEM((PAIRS, number, WIDE), bf16),
+            pltpu.VMEM((features, LANES), f32),
+            pltpu.VMEM((features, LANES), f32),
+            pltpu.VMEM((D, features), bf16),
+            pltpu.SemaphoreType.DMA((PAIRS,)),
+        ],
+        limit=LIMP,
+        far=(0,),
+        near_out=(1, 2),
+    )
+    near, side, band = together(near, side, band)
+    negset = jnp.concatenate([near[number:], side], axis=0)
     for mask in beyond:
         negset = jnp.concatenate([negset, send(negset, mask)], axis=0)
-    near, negset, fc, band, band_t = together(near, negset, fc, band, band_t)
     requested.append(send(wanted[1], plan.partner(1)))
+    near, negset = together(near, negset)
     rel_others = send(rel_ids, 1)
     negset = jnp.concatenate([negset, send(negset, 1)], axis=0)
-    rel_inputs = (rel_first,)
 
     def lay(sources):
         return [pltpu.VMEM((PACK, sources * LANES), bf16), pltpu.VMEM((8, sources * LANES), i32)]
@@ -424,15 +498,19 @@
     sums = []
     for r in range(ROUNDS):
         last = r == ROUNDS - 1
-        pre2, slopes = call(
-            functools.partial(forward_kernel, r),
-            "forward",
-            2.5,
-            [shaped((number, D)), shaped((PAIRS, number, WIDE))],
-            (head_ids, ent, *rel_inputs, band, bias, fc, bias2),
-            [pltpu.VMEM((PIXELS, number), f32), pltpu.VMEM((PAIRS, number, WIDE), bf16)],
-            limit=24,
-        )
+        if r > 0:
+            pre2, slopes, fc = call(
+                functools.partial(forward_kernel, r),
+                "forward",
+                2.5,
+                [shaped((number, D)), shaped((PAIRS, number, WIDE)), shaped(fc.shape, bf16)],
+                (fc, head_ids, ent, *rel_inputs, band, bias, bias2),
+                [pltpu.VMEM((PIXELS, number), f32), pltpu.VMEM((PAIRS, number, WIDE), bf16)],
+                limit=LIM,
+                near=(0,),
+                near_out=(1, 2),
+                alias={0: 2},
+            )
         grad2, tail_grad, neg_part = call(
             score_kernel,
             "scores",
@@ -446,14 +524,20 @@
             )
         half = neg_part.shape[0] // 2
         arrived = send(neg_part[half:], 1)
-        pack, head_grad = call(
+        pack, head_grad, fc = call(
             functools.partial(backward_kernel, r),
             "backward",
             3,
-            [shaped((PACK, number), bf16), shaped((D, number))],
-            (rel_ids, grad2, slopes, band_t, fc),
-            [pltpu.VMEM((PAIRS, number, WIDE), bf16), pltpu.VMEM((PIXELS, number), f32)],
-            limit=24,
+            [shaped((PACK, number), bf16), shaped((D, number)), shaped(fc.shape, bf16)],
+            (fc, rel_ids, grad2, slopes, band_t),
+            [
+                pltpu.VMEM((PAIRS, number, WIDE), bf16),
+                pltpu.VMEM((PIXELS, number), f32),
+            ],
+            limit=LIM,
+            near=(0, 3),
+            near_out=(2,),
+            alias={0: 2},
         )
         pack, arrived = together(pack, arrived)
         share = neg_part[:half] + arrived
@@ -473,21 +557,21 @@
                 to_side = send(share[negatives:], plan.partner(r) | next_door)
                 came, to_owner, to_side = together(came, to_owner, to_side)
             packs = jnp.concatenate([packs, came], axis=0)
-            if last and step == 0:
-                (part,) = call(
-                    functools.partial(sums_kernel, (4, 0)),
-                    "relation_sums",
-                    3,
-                    [shaped((D, wide))],
-                    (place, *groups),
-                    lay(4 * group),
-                    scalars=1,
-                )
-                packs, part = together(packs, part)
-                sums = [part, send(part, 1)]
         one, other = plan.far[-2:]
         across = send(packs, one)
         along = send(packs, other)
+        if last:
+            (part,) = call(
+                functools.partial(sums_kernel, (4, 0)),
+                "relation_sums",
+                3,
+                [shaped((D, wide))],
+                (place, *groups),
+                lay(4 * group),
+                scalars=1,
+            )
+            across, along, part, to_owner, to_side = together(across, along, part, to_owner, to_side)
+            sums = [part, send(part, 1)]
         out_shape = [shaped(ent.shape), shaped(ent_state.shape)]
         outs = call(
             functools.partial(entity_kernel, r, negatives),
@@ -507,7 +591,6 @@
         )
         ent, ent_state = outs[:2]
         if last:
-            across, along, ent, ent_state, *sums = together(across, along, ent, ent_state, *sums)
             corner = send(across, other)
             early = call(
                 functools.partial(sums_kernel, (3, 0)),
@@ -518,7 +601,8 @@
                 lay(3 * group),
                 scalars=1,
             )
-            corner, *early = together(corner, *early)
+            corner, ent, ent_state, *rest = together(corner, ent, ent_state, *early, *sums)
+            early, sums = rest[:2], rest[2:]
             (part,) = call(
                 functools.partial(sums_kernel, (1, 2)),
                 "late_sums",

time: 117 us -> 106 us (0.906)
  local copies, waits for them, and re-layouts: 14.7 us -> 1.25 us
  starting transfers between devices: 32.5 us -> 39.4 us
  waiting for transfers between devices: 37.2 us -> 31.8 us
  Pallas kernels: 30 us -> 31.6 us
    unnamed x39 -> x26, local copies, waits for them, and re-layouts: 14.4 us -> 0.97 us
    ppermute x32, starting transfers between devices: 32.5 us -> 39.4 us  [send(): return lax.ppermute(block, BOTH, self.route(mask))]
    ppermute x32, waiting for transfers between devices: 37.2 us -> 31.8 us  [send(): return lax.ppermute(block, BOTH, self.route(mask))]
    pallas_call x17 -> x16, Pallas kernels: 30 us -> 31.6 us  [call(): pl.pallas_call(kernel, out_shape=[pltpu.VMEM(out.shape, out.dtype) if ind...]
  transfers between devices with their start and end apart: 32 -> 32, of which waited for: 16 -> 17; matrix products, arithmetic and copies ran while one was open for 0% -> 0% of each run, Pallas kernels for 19% -> 21%
where the time goes in v4:
time: 106 us
  starting transfers between devices  39.4 us (37%)
  waiting for transfers between devices  31.8 us (30%)
  Pallas kernels  31.6 us (30%)
  local copies, waits for them, and re-layouts  1.25 us (1%)
  between operations  1.08 us (1%)
    ppermute x32, starting transfers between devices, send(): return lax.ppermute(block, BOTH, self.route(mask))  39.4 us
    ppermute x32, waiting for transfers between devices, send(): return lax.ppermute(block, BOTH, self.route(mask))  31.8 us
    pallas_call x16, Pallas kernels, call(): pl.pallas_call(kernel, out_shape=[pltpu.VMEM(out.shape, out.dtype) if ind...  31.6 us
  transfers between devices with their start and end apart: 32, of which 17 were waited for; matrix products, arithmetic and copies ran while one was open for 0% of the time, Pallas kernels for 21%

profile of v4, /device:TPU:0, one launch (start us, length us, event | category | flops | bytes accessed | tf_op | source)
XLA Modules:
  0.0 106.1 jit_solution(4013413077389273285)
XLA Ops:
  1.5 3.0 %collective-permute-start = (s32[2,128]{1,0:T(2,128)S(1)}, s32[2,128]{1,0:T(2,128)S(1)}, u32[]{:S(2)}, u32[]{:S(2)}) collective-permute-start(s32[2,128]{1,0:T(2,128)S(1)} %get-tuple-element.83), channel_id=1, source_target_pairs={{0,8},{1,9},{2,10},{3,11},{4,12},{5,13},{6,14},{7,15},{8,0},{9,1},... | collective-permute-start | bytes 3080 | tf_op jit(solution)/shard_map/ppermute | solution.py:387
  6.5 2.1 %collective-permute-start.1 = (bf16[160,200]{1,0:T(8,128)(2,1)S(1)}, bf16[160,200]{1,0:T(8,128)(2,1)S(1)}, u32[]{:S(2)}, u32[]{:S(2)}) collective-permute-start(bf16[160,200]{1,0:T(8,128)(2,1)S(1)} %answer.1), channel_id=1, source_target_pairs={{0,8},{1,9},{2,10},{3,11},{4,12},{5,13},{6,14},{7,15},{8,0},{9,1},... | collective-permute-start | bytes 192008 | tf_op jit(solution)/shard_map/ppermute | solution.py:387
  8.5 2.6 %collective-permute-start.2 = (bf16[32,200]{1,0:T(8,128)(2,1)S(1)}, bf16[32,200]{1,0:T(8,128)(2,1)S(1)}, u32[]{:S(2)}, u32[]{:S(2)}) collective-permute-start(bf16[32,200]{1,0:T(8,128)(2,1)S(1)} %slice.72), channel_id=1, source_target_pairs={{0,12},{1,13},{2,14},{3,15},{4,8},{5,9},{6,10},{7,11},{8,4},{9,5},... | collective-permute-start | bytes 38408 | tf_op jit(solution)/shard_map/ppermute | solution.py:387
  11.1 6.7 %first_forward.1 = (f32[128,200]{1,0:T(8,128)S(1)}, f32[9,128,1152]{2,1,0:T(8,128)S(1)}, bf16[9,1152,200]{2,1,0:T(8,128)(2,1)S(1)}, bf16[80,1152]{1,0:T(8,128)(2,1)S(1)}, bf16[1152,128]{1,0:T(8,128)(2,1)S(1)}) custom-call(bf16[200,10368]{1,0:T(8,128)(2,1)} %bitcast.28, f32[9,1152]{1,0:T(8,128)S(1)} %tile.18.taps_ref, s32[2,128]{1,0:T(2,128)S(1)} %copy-done.5, ...), custom_call_target="tpu_custom_call" | custom-call | flops 6000000000 | bytes 18000000 | tf_op jit(solution)/shard_map/first_forward/pallas_call | solution.py:50
  17.9 1.6 %collective-permute-start.3 = (bf16[64,200]{1,0:T(8,128)(2,1)S(1)}, bf16[64,200]{1,0:T(8,128)(2,1)S(1)}, u32[]{:S(2)}, u32[]{:S(2)}) collective-permute-start(bf16[64,200]{1,0:T(8,128)(2,1)S(1)} %pad_maximum_fusion.10), channel_id=1, source_target_pairs={{0,2},{1,3},{2,0},{3,1},{4,6},{5,7},{6,4},{7,5},{8,10},{9,11},{10,... | collective-permute-start | bytes 76808 | tf_op jit(solution)/shard_map/ppermute | solution.py:387
  19.5 2.3 %collective-permute-done.3 = bf16[64,200]{1,0:T(8,128)(2,1)S(1)} collective-permute-done((bf16[64,200]{1,0:T(8,128)(2,1)S(1)}, bf16[64,200]{1,0:T(8,128)(2,1)S(1)}, u32[]{:S(2)}, u32[]{:S(2)}) %collective-permute-start.3) | collective-permute-done | bytes 25632 | tf_op jit(solution)/shard_map/ppermute | solution.py:387
  22.4 1.5 %collective-permute-start.5 = (s32[2,128]{1,0:T(2,128)S(1)}, s32[2,128]{1,0:T(2,128)S(1)}, u32[]{:S(2)}, u32[]{:S(2)}) collective-permute-start(s32[2,128]{1,0:T(2,128)S(1)} %get-tuple-element.98), channel_id=1, source_target_pairs={{0,16},{1,17},{2,18},{3,19},{4,20},{5,21},{6,22},{7,23},{8,24},{9,... | collective-permute-start | bytes 3080 | tf_op jit(solution)/shard_map/ppermute | solution.py:387
  24.5 1.5 %collective-permute-done.5.next_ref.asked_ref = s32[2,128]{1,0:T(2,128)S(1)} collective-permute-done((s32[2,128]{1,0:T(2,128)S(1)}, s32[2,128]{1,0:T(2,128)S(1)}, u32[]{:S(2)}, u32[]{:S(2)}) %collective-permute-start.5) | collective-permute-done | bytes 1056 | tf_op jit(solution)/shard_map/ppermute | solution.py:387
  26.1 3.0 %backward.2 = (bf16[208,128]{1,0:T(8,128)(2,1)S(1)}, f32[200,128]{1,0:T(8,128)S(1)}, bf16[9,1152,200]{2,1,0:T(8,128)(2,1)S(1)}) custom-call(bf16[9,1152,200]{2,1,0:T(8,128)(2,1)S(1)} %get-tuple-element.88.fc_ref, s32[2,128]{1,0:T(2,128)S(1)} %copy-done.4, bf16[128,200]{1,0:T(8,128)(2,1)S(1)} %get-tuple-element.99.grad_ref, ...), custom_call_target="tpu_custom_call", output_to_operand_aliasing={{2}: (0, {})} | custom-call | flops 3000000000 | bytes 9000000 | tf_op jit(solution)/shard_map/backward/pallas_call | solution.py:50
  29.3 1.9 %collective-permute-start.9 = (f32[64,200]{1,0:T(8,128)S(1)}, f32[64,200]{1,0:T(8,128)S(1)}, u32[]{:S(2)}, u32[]{:S(2)}) collective-permute-start(f32[64,200]{1,0:T(8,128)S(1)} %slice.73), channel_id=1, source_target_pairs={{0,2},{1,3},{2,0},{3,1},{4,6},{5,7},{6,4},{7,5},{8,10},{9,11},{10,... | collective-permute-start | bytes 153608 | tf_op jit(solution)/shard_map/ppermute | solution.py:387
  31.2 3.7 %collective-permute-done.9 = f32[64,200]{1,0:T(8,128)S(1)} collective-permute-done((f32[64,200]{1,0:T(8,128)S(1)}, f32[64,200]{1,0:T(8,128)S(1)}, u32[]{:S(2)}, u32[]{:S(2)}) %collective-permute-start.9) | collective-permute-done | bytes 51232 | tf_op jit(solution)/shard_map/ppermute | solution.py:387
  38.0 2.3 %collective-permute-start.12 = (f32[32,200]{1,0:T(8,128)S(1)}, f32[32,200]{1,0:T(8,128)S(1)}, u32[]{:S(2)}, u32[]{:S(2)}) collective-permute-start(f32[32,200]{1,0:T(8,128)S(1)} %get-tuple-element.164), channel_id=1, source_target_pairs={{0,12},{1,13},{2,14},{3,15},{4,8},{5,9},{6,10},{7,11},{8,4},{9,5},... | collective-permute-start | bytes 76808 | tf_op jit(solution)/shard_map/ppermute | solution.py:387
  40.3 3.4 %collective-permute-done.12.other_ref = f32[32,200]{1,0:T(8,128)S(1)} collective-permute-done((f32[32,200]{1,0:T(8,128)S(1)}, f32[32,200]{1,0:T(8,128)S(1)}, u32[]{:S(2)}, u32[]{:S(2)}) %collective-permute-start.12) | collective-permute-done | bytes 25632 | tf_op jit(solution)/shard_map/ppermute | solution.py:387
  47.9 2.3 %collective-permute-start.14 = (bf16[32,200]{1,0:T(8,128)(2,1)S(1)}, bf16[32,200]{1,0:T(8,128)(2,1)S(1)}, u32[]{:S(2)}, u32[]{:S(2)}) collective-permute-start(bf16[32,200]{1,0:T(8,128)(2,1)S(1)} %slice.63), channel_id=1, source_target_pairs={{0,20},{1,21},{2,22},{3,23},{4,16},{5,17},{6,18},{7,19},{8,28},{9,... | collective-permute-start | bytes 38408 | tf_op jit(solution)/shard_map/ppermute | solution.py:387
  50.2 1.6 %collective-permute-start.17 = (bf16[4,208,128]{2,1,0:T(8,128)(2,1)S(1)}, bf16[4,208,128]{2,1,0:T(8,128)(2,1)S(1)}, u32[]{:S(2)}, u32[]{:S(2)}) collective-permute-start(bf16[4,208,128]{2,1,0:T(8,128)(2,1)S(1)} %pad_maximum_fusion.refs_0_), channel_id=1, source_target_pairs={{0,16},{1,17},{2,18},{3,19},{4,20},{5,21},{6,22},{7,23},{8,24},{9,... | collective-permute-start | bytes 638984 | tf_op jit(solution)/shard_map/ppermute | solution.py:387
  51.7 1.7 %collective-permute-done.14 = bf16[32,200]{1,0:T(8,128)(2,1)S(1)} collective-permute-done((bf16[32,200]{1,0:T(8,128)(2,1)S(1)}, bf16[32,200]{1,0:T(8,128)(2,1)S(1)}, u32[]{:S(2)}, u32[]{:S(2)}) %collective-permute-start.14) | collective-permute-done | bytes 12832 | tf_op jit(solution)/shard_map/ppermute | solution.py:387
  55.4 2.0 %collective-permute-done.15 = bf16[64,200]{1,0:T(8,128)(2,1)S(1)} collective-permute-done((bf16[64,200]{1,0:T(8,128)(2,1)S(1)}, bf16[64,200]{1,0:T(8,128)(2,1)S(1)}, u32[]{:S(2)}, u32[]{:S(2)}) %collective-permute-start.15) | collective-permute-done | bytes 25632 | tf_op jit(solution)/shard_map/ppermute | solution.py:387
  58.2 2.6 %collective-permute-done.18.refs_3_ = bf16[4,208,128]{2,1,0:T(8,128)(2,1)S(1)} collective-permute-done((bf16[4,208,128]{2,1,0:T(8,128)(2,1)S(1)}, bf16[4,208,128]{2,1,0:T(8,128)(2,1)S(1)}, u32[]{:S(2)}, u32[]{:S(2)}) %collective-permute-start.18) | collective-permute-done | bytes 213024 | tf_op jit(solution)/shard_map/ppermute | solution.py:387
  63.7 2.9 %forward.1 = (f32[128,200]{1,0:T(8,128)S(1)}, f32[9,128,1152]{2,1,0:T(8,128)S(1)}, bf16[9,1152,200]{2,1,0:T(8,128)(2,1)S(1)}) custom-call(bf16[9,1152,200]{2,1,0:T(8,128)(2,1)S(1)} %copy-done.7, s32[2,128]{1,0:T(2,128)S(1)} %copy-done.5, f32[200,1024]{1,0:T(8,128)S(1)} %copy-done.9, ...), custom_call_target="tpu_custom_call", output_to_operand_aliasing={{2}: (0, {})} | custom-call | flops 2500000000 | bytes 7500000 | tf_op jit(solution)/shard_map/forward/pallas_call | solution.py:50
  67.4 3.0 %backward.3 = (bf16[208,128]{1,0:T(8,128)(2,1)S(1)}, f32[200,128]{1,0:T(8,128)S(1)}, bf16[9,1152,200]{2,1,0:T(8,128)(2,1)S(1)}) custom-call(bf16[9,1152,200]{2,1,0:T(8,128)(2,1)S(1)} %get-tuple-element.127.fc_ref, s32[2,128]{1,0:T(2,128)S(1)} %copy-done.4, bf16[128,200]{1,0:T(8,128)(2,1)S(1)} %get-tuple-element.130.grad_ref, ...), custom_call_target="tpu_custom_call", output_to_operand_aliasing={{2}: (0, {})} | custom-call | flops 3000000000 | bytes 9000000 | tf_op jit(solution)/shard_map/backward/pallas_call | solution.py:50
  70.5 1.8 %collective-permute-start.22 = (bf16[1,208,128]{2,1,0:T(8,128)(2,1)S(1)}, bf16[1,208,128]{2,1,0:T(8,128)(2,1)S(1)}, u32[]{:S(2)}, u32[]{:S(2)}) collective-permute-start(bf16[1,208,128]{2,1,0:T(8,128)(2,1)S(1)} %bitcast.13), channel_id=1, source_target_pairs={{0,4},{1,5},{2,6},{3,7},{4,0},{5,1},{6,2},{7,3},{8,12},{9,13},{10,... | collective-permute-start | bytes 159752 | tf_op jit(solution)/shard_map/ppermute | solution.py:387
  73.8 3.3 %collective-permute-done.23 = f32[64,200]{1,0:T(8,128)S(1)} collective-permute-done((f32[64,200]{1,0:T(8,128)S(1)}, f32[64,200]{1,0:T(8,128)S(1)}, u32[]{:S(2)}, u32[]{:S(2)}) %collective-permute-start.23) | collective-permute-done | bytes 51232 | tf_op jit(solution)/shard_map/ppermute | solution.py:387
  78.7 2.6 %collective-permute-start.26 = (f32[32,200]{1,0:T(8,128)S(1)}, f32[32,200]{1,0:T(8,128)S(1)}, u32[]{:S(2)}, u32[]{:S(2)}) collective-permute-start(f32[32,200]{1,0:T(8,128)S(1)} %get-tuple-element.162), channel_id=1, source_target_pairs={{0,20},{1,21},{2,22},{3,23},{4,16},{5,17},{6,18},{7,19},{8,28},{9,... | collective-permute-start | bytes 76808 | tf_op jit(solution)/shard_map/ppermute | solution.py:387
  81.3 3.1 %collective-permute-done.26.other_ref = f32[32,200]{1,0:T(8,128)S(1)} collective-permute-done((f32[32,200]{1,0:T(8,128)S(1)}, f32[32,200]{1,0:T(8,128)S(1)}, u32[]{:S(2)}, u32[]{:S(2)}) %collective-permute-start.26) | collective-permute-done | bytes 25632 | tf_op jit(solution)/shard_map/ppermute | solution.py:387
  84.4 1.6 %collective-permute-start.27 = (bf16[4,208,128]{2,1,0:T(8,128)(2,1)S(1)}, bf16[4,208,128]{2,1,0:T(8,128)(2,1)S(1)}, u32[]{:S(2)}, u32[]{:S(2)}) collective-permute-start(bf16[4,208,128]{2,1,0:T(8,128)(2,1)S(1)} %pad_maximum_fusion.1.refs_0_), channel_id=1, source_target_pairs={{0,8},{1,9},{2,10},{3,11},{4,12},{5,13},{6,14},{7,15},{8,0},{9,1},... | collective-permute-start | bytes 638984 | tf_op jit(solution)/shard_map/ppermute | solution.py:387
  87.6 3.2 %relation_sums.1.refs_0_ = f32[200,1408]{1,0:T(8,128)S(1)} custom-call(s32[4]{0:T(128)S(1)} %iota_xor_fusion.place_ref, bf16[4,208,128]{2,1,0:T(8,128)(2,1)S(1)} %pad_maximum_fusion.refs_0_, bf16[4,208,128]{2,1,0:T(8,128)(2,1)S(1)} %collective-permute-done.16.refs_1_, bf16[4,208,128]{2,1,0:T(8,128)(2,1)S(1)} %collective-permute-done.17.refs_2_, ...), custom_call_target="tpu_custom_call" | custom-call | flops 3000000000 | bytes 9000000 | tf_op jit(solution)/shard_map/relation_sums/pallas_call | solution.py:50
  91.9 1.5 %collective-permute-start.29 = (bf16[4,208,128]{2,1,0:T(8,128)(2,1)S(1)}, bf16[4,208,128]{2,1,0:T(8,128)(2,1)S(1)}, u32[]{:S(2)}, u32[]{:S(2)}) collective-permute-start(bf16[4,208,128]{2,1,0:T(8,128)(2,1)S(1)} %collective-permute-done.27.refs_1_), channel_id=1, source_target_pairs={{0,16},{1,17},{2,18},{3,19},{4,20},{5,21},{6,22},{7,23},{8,24},{9,... | collective-permute-start | bytes 638984 | tf_op jit(solution)/shard_map/ppermute | solution.py:387
  93.4 1.7 %entity_update.3 = (f32[200,1024]{1,0:T(8,128)}, f32[1,1024]{1,0:T(1,128)}) custom-call(s32[2,128]{1,0:T(2,128)S(1)} %copy-done.5, s32[2,128]{1,0:T(2,128)S(1)} %collective-permute-done.5.next_ref.asked_ref, s32[2,128]{1,0:T(2,128)S(1)} %collective-permute-done.5.next_ref.asked_ref, f32[200,1024]{1,0:T(8,128)S(1)} %copy-done.9, ...), custom_call_target="tpu_custom_call" | custom-call | flops 1500000000 | bytes 4500000 | tf_op jit(solution)/shard_map/entity_update/pallas_call | solution.py:50
  95.1 2.6 %early_sums.1 = (f32[200,1408]{1,0:T(8,128)S(1)}, f32[200,1408]{1,0:T(8,128)S(1)}) custom-call(s32[4]{0:T(128)S(1)} %iota_xor_fusion.place_ref, bf16[4,208,128]{2,1,0:T(8,128)(2,1)S(1)} %pad_maximum_fusion.1.refs_0_, bf16[4,208,128]{2,1,0:T(8,128)(2,1)S(1)} %collective-permute-done.27.refs_1_, bf16[4,208,128]{2,1,0:T(8,128)(2,1)S(1)} %collective-permute-done.28.refs_2_), custom_call_target="tpu_custom_call" | custom-call | flops 3000000000 | bytes 9000000 | tf_op jit(solution)/shard_map/early_sums/pallas_call | solution.py:50
  97.7 1.9 %collective-permute-done.29.refs_0_ = bf16[4,208,128]{2,1,0:T(8,128)(2,1)S(1)} collective-permute-done((bf16[4,208,128]{2,1,0:T(8,128)(2,1)S(1)}, bf16[4,208,128]{2,1,0:T(8,128)(2,1)S(1)}, u32[]{:S(2)}, u32[]{:S(2)}) %collective-permute-start.29) | collective-permute-done | bytes 213024 | tf_op jit(solution)/shard_map/ppermute | solution.py:387
  101.0 2.8 %collective-permute-done.31.refs_3_ = f32[200,1408]{1,0:T(8,128)S(1)} collective-permute-done((f32[200,1408]{1,0:T(8,128)S(1)}, f32[200,1408]{1,0:T(8,128)S(1)}, u32[]{:S(2)}, u32[]{:S(2)}) %collective-permute-start.31) | collective-permute-done | bytes 1126432 | tf_op jit(solution)/shard_map/ppermute | solution.py:387
  103.7 1.7 %relation_update.1 = (f32[200,1387]{1,0:T(8,128)}, f32[1,1387]{1,0:T(1,128)S(1)}) custom-call(f32[200,1387]{1,0:T(8,128)S(1)} %bitcast.20, f32[1,1387]{1,0:T(1,128)S(1)} %broadcast_in_dim.15.state_ref, f32[200,1408]{1,0:T(8,128)S(1)} %relation_sums.1.refs_0_, f32[200,1408]{1,0:T(8,128)S(1)} %collective-permute-done.30.refs_1_, ...), custom_call_target="tpu_custom_call" | custom-call | flops 2000000000 | bytes 6000000 | tf_op jit(solution)/shard_map/relation_update/pallas_call | solution.py:50
  (110 shorter events, 25.6 us)
Async XLA Ops:
  1.5 4.6 %collective-permute-start = (s32[2,128]{1,0:T(2,128)S(1)}, s32[2,128]{1,0:T(2,128)S(1)}, u32[]{:S(2)}, u32[]{:S(2)}) collective-permute-start(s32[2,128]{1,0:T(2,128)S(1)} %get-tuple-element.83), channel_id=1, source_target_pairs={{0,8},{1,9},{2,10},{3,11},{4,12},{5,13},{6,14},{7,15},{8,0},{9,1},... | collective-permute-start | bytes 3080 | tf_op jit(solution)/shard_map/ppermute | solution.py:387
  6.5 11.4 %collective-permute-start.1 = (bf16[160,200]{1,0:T(8,128)(2,1)S(1)}, bf16[160,200]{1,0:T(8,128)(2,1)S(1)}, u32[]{:S(2)}, u32[]{:S(2)}) collective-permute-start(bf16[160,200]{1,0:T(8,128)(2,1)S(1)} %answer.1), channel_id=1, source_target_pairs={{0,8},{1,9},{2,10},{3,11},{4,12},{5,13},{6,14},{7,15},{8,0},{9,1},... | collective-permute-start | bytes 192008 | tf_op jit(solution)/shard_map/ppermute | solution.py:387
  8.5 9.3 %collective-permute-start.2 = (bf16[32,200]{1,0:T(8,128)(2,1)S(1)}, bf16[32,200]{1,0:T(8,128)(2,1)S(1)}, u32[]{:S(2)}, u32[]{:S(2)}) collective-permute-start(bf16[32,200]{1,0:T(8,128)(2,1)S(1)} %slice.72), channel_id=1, source_target_pairs={{0,12},{1,13},{2,14},{3,15},{4,8},{5,9},{6,10},{7,11},{8,4},{9,5},... | collective-permute-start | bytes 38408 | tf_op jit(solution)/shard_map/ppermute | solution.py:387
  17.9 4.0 %collective-permute-start.3 = (bf16[64,200]{1,0:T(8,128)(2,1)S(1)}, bf16[64,200]{1,0:T(8,128)(2,1)S(1)}, u32[]{:S(2)}, u32[]{:S(2)}) collective-permute-start(bf16[64,200]{1,0:T(8,128)(2,1)S(1)} %pad_maximum_fusion.10), channel_id=1, source_target_pairs={{0,2},{1,3},{2,0},{3,1},{4,6},{5,7},{6,4},{7,5},{8,10},{9,11},{10,... | collective-permute-start | bytes 76808 | tf_op jit(solution)/shard_map/ppermute | solution.py:387
  21.9 2.1 %collective-permute-start.4 = (bf16[128,200]{1,0:T(8,128)(2,1)S(1)}, bf16[128,200]{1,0:T(8,128)(2,1)S(1)}, u32[]{:S(2)}, u32[]{:S(2)}) collective-permute-start(bf16[128,200]{1,0:T(8,128)(2,1)S(1)} %pad_maximum_fusion.8), channel_id=1, source_target_pairs={{0,1},{1,0},{2,3},{3,2},{4,5},{5,4},{6,7},{7,6},{8,9},{9,8},{10,11... | collective-permute-start | bytes 153608 | tf_op jit(solution)/shard_map/ppermute | solution.py:387
  21.9 4.1 %collective-permute-start.6 = (s32[2,128]{1,0:T(2,128)S(1)}, s32[2,128]{1,0:T(2,128)S(1)}, u32[]{:S(2)}, u32[]{:S(2)}) collective-permute-start(s32[2,128]{1,0:T(2,128)S(1)} %copy-done.4), channel_id=1, source_target_pairs={{0,1},{1,0},{2,3},{3,2},{4,5},{5,4},{6,7},{7,6},{8,9},{9,8},{10,11... | collective-permute-start | bytes 3080 | tf_op jit(solution)/shard_map/ppermute | solution.py:387
  22.4 3.6 %collective-permute-start.5 = (s32[2,128]{1,0:T(2,128)S(1)}, s32[2,128]{1,0:T(2,128)S(1)}, u32[]{:S(2)}, u32[]{:S(2)}) collective-permute-start(s32[2,128]{1,0:T(2,128)S(1)} %get-tuple-element.98), channel_id=1, source_target_pairs={{0,16},{1,17},{2,18},{3,19},{4,20},{5,21},{6,22},{7,23},{8,24},{9,... | collective-permute-start | bytes 3080 | tf_op jit(solution)/shard_map/ppermute | solution.py:387
  26.0 3.1 %collective-permute-start.7 = (f32[128,200]{1,0:T(8,128)S(1)}, f32[128,200]{1,0:T(8,128)S(1)}, u32[]{:S(2)}, u32[]{:S(2)}) collective-permute-start(f32[128,200]{1,0:T(8,128)S(1)} %slice.57), channel_id=1, source_target_pairs={{0,1},{1,0},{2,3},{3,2},{4,5},{5,4},{6,7},{7,6},{8,9},{9,8},{10,11... | collective-permute-start | bytes 307208 | tf_op jit(solution)/shard_map/ppermute | solution.py:387
  29.1 6.2 %collective-permute-start.8 = (bf16[1,208,128]{2,1,0:T(8,128)(2,1)S(1)}, bf16[1,208,128]{2,1,0:T(8,128)(2,1)S(1)}, u32[]{:S(2)}, u32[]{:S(2)}) collective-permute-start(bf16[1,208,128]{2,1,0:T(8,128)(2,1)S(1)} %bitcast.16), channel_id=1, source_target_pairs={{0,4},{1,5},{2,6},{3,7},{4,0},{5,1},{6,2},{7,3},{8,12},{9,13},{10,... | collective-permute-start | bytes 159752 | tf_op jit(solution)/shard_map/ppermute | solution.py:387
  29.3 5.6 %collective-permute-start.9 = (f32[64,200]{1,0:T(8,128)S(1)}, f32[64,200]{1,0:T(8,128)S(1)}, u32[]{:S(2)}, u32[]{:S(2)}) collective-permute-start(f32[64,200]{1,0:T(8,128)S(1)} %slice.73), channel_id=1, source_target_pairs={{0,2},{1,3},{2,0},{3,1},{4,6},{5,7},{6,4},{7,5},{8,10},{9,11},{10,... | collective-permute-start | bytes 153608 | tf_op jit(solution)/shard_map/ppermute | solution.py:387
  35.3 8.4 %collective-permute-start.11 = (f32[160,200]{1,0:T(8,128)S(1)}, f32[160,200]{1,0:T(8,128)S(1)}, u32[]{:S(2)}, u32[]{:S(2)}) collective-permute-start(f32[160,200]{1,0:T(8,128)S(1)} %pad_maximum_fusion.2), channel_id=1, source_target_pairs={{0,8},{1,9},{2,10},{3,11},{4,12},{5,13},{6,14},{7,15},{8,0},{9,1},... | collective-permute-start | bytes 384008 | tf_op jit(solution)/shard_map/ppermute | solution.py:387
  36.8 6.9 %collective-permute-start.10 = (bf16[2,208,128]{2,1,0:T(8,128)(2,1)S(1)}, bf16[2,208,128]{2,1,0:T(8,128)(2,1)S(1)}, u32[]{:S(2)}, u32[]{:S(2)}) collective-permute-start(bf16[2,208,128]{2,1,0:T(8,128)(2,1)S(1)} %pad_maximum_fusion.6), channel_id=1, source_target_pairs={{0,2},{1,3},{2,0},{3,1},{4,6},{5,7},{6,4},{7,5},{8,10},{9,11},{10,... | collective-permute-start | bytes 319496 | tf_op jit(solution)/shard_map/ppermute | solution.py:387
  38.0 5.7 %collective-permute-start.12 = (f32[32,200]{1,0:T(8,128)S(1)}, f32[32,200]{1,0:T(8,128)S(1)}, u32[]{:S(2)}, u32[]{:S(2)}) collective-permute-start(f32[32,200]{1,0:T(8,128)S(1)} %get-tuple-element.164), channel_id=1, source_target_pairs={{0,12},{1,13},{2,14},{3,15},{4,8},{5,9},{6,10},{7,11},{8,4},{9,5},... | collective-permute-start | bytes 76808 | tf_op jit(solution)/shard_map/ppermute | solution.py:387
  43.8 11.2 %collective-permute-start.16 = (bf16[4,208,128]{2,1,0:T(8,128)(2,1)S(1)}, bf16[4,208,128]{2,1,0:T(8,128)(2,1)S(1)}, u32[]{:S(2)}, u32[]{:S(2)}) collective-permute-start(bf16[4,208,128]{2,1,0:T(8,128)(2,1)S(1)} %pad_maximum_fusion.refs_0_), channel_id=1, source_target_pairs={{0,8},{1,9},{2,10},{3,11},{4,12},{5,13},{6,14},{7,15},{8,0},{9,1},... | collective-permute-start | bytes 638984 | tf_op jit(solution)/shard_map/ppermute | solution.py:387
  46.4 7.1 %collective-permute-start.13 = (bf16[160,200]{1,0:T(8,128)(2,1)S(1)}, bf16[160,200]{1,0:T(8,128)(2,1)S(1)}, u32[]{:S(2)}, u32[]{:S(2)}) collective-permute-start(bf16[160,200]{1,0:T(8,128)(2,1)S(1)} %get-tuple-element.115), channel_id=1, source_target_pairs={{0,16},{1,17},{2,18},{3,19},{4,20},{5,21},{6,22},{7,23},{8,24},{9,... | collective-permute-start | bytes 192008 | tf_op jit(solution)/shard_map/ppermute | solution.py:387
  47.9 5.5 %collective-permute-start.14 = (bf16[32,200]{1,0:T(8,128)(2,1)S(1)}, bf16[32,200]{1,0:T(8,128)(2,1)S(1)}, u32[]{:S(2)}, u32[]{:S(2)}) collective-permute-start(bf16[32,200]{1,0:T(8,128)(2,1)S(1)} %slice.63), channel_id=1, source_target_pairs={{0,20},{1,21},{2,22},{3,23},{4,16},{5,17},{6,18},{7,19},{8,28},{9,... | collective-permute-start | bytes 38408 | tf_op jit(solution)/shard_map/ppermute | solution.py:387
  50.2 8.0 %collective-permute-start.17 = (bf16[4,208,128]{2,1,0:T(8,128)(2,1)S(1)}, bf16[4,208,128]{2,1,0:T(8,128)(2,1)S(1)}, u32[]{:S(2)}, u32[]{:S(2)}) collective-permute-start(bf16[4,208,128]{2,1,0:T(8,128)(2,1)S(1)} %pad_maximum_fusion.refs_0_), channel_id=1, source_target_pairs={{0,16},{1,17},{2,18},{3,19},{4,20},{5,21},{6,22},{7,23},{8,24},{9,... | collective-permute-start | bytes 638984 | tf_op jit(solution)/shard_map/ppermute | solution.py:387
  53.5 4.0 %collective-permute-start.15 = (bf16[64,200]{1,0:T(8,128)(2,1)S(1)}, bf16[64,200]{1,0:T(8,128)(2,1)S(1)}, u32[]{:S(2)}, u32[]{:S(2)}) collective-permute-start(bf16[64,200]{1,0:T(8,128)(2,1)S(1)} %pad_maximum_fusion.11), channel_id=1, source_target_pairs={{0,2},{1,3},{2,0},{3,1},{4,6},{5,7},{6,4},{7,5},{8,10},{9,11},{10,... | collective-permute-start | bytes 76808 | tf_op jit(solution)/shard_map/ppermute | solution.py:387
  54.9 5.8 %collective-permute-start.18 = (bf16[4,208,128]{2,1,0:T(8,128)(2,1)S(1)}, bf16[4,208,128]{2,1,0:T(8,128)(2,1)S(1)}, u32[]{:S(2)}, u32[]{:S(2)}) collective-permute-start(bf16[4,208,128]{2,1,0:T(8,128)(2,1)S(1)} %collective-permute-done.16.refs_1_), channel_id=1, source_target_pairs={{0,16},{1,17},{2,18},{3,19},{4,20},{5,21},{6,22},{7,23},{8,24},{9,... | collective-permute-start | bytes 638984 | tf_op jit(solution)/shard_map/ppermute | solution.py:387
  62.2 1.3 %collective-permute-start.20 = (bf16[128,200]{1,0:T(8,128)(2,1)S(1)}, bf16[128,200]{1,0:T(8,128)(2,1)S(1)}, u32[]{:S(2)}, u32[]{:S(2)}) collective-permute-start(bf16[128,200]{1,0:T(8,128)(2,1)S(1)} %pad_maximum_fusion.9), channel_id=1, source_target_pairs={{0,1},{1,0},{2,3},{3,2},{4,5},{5,4},{6,7},{7,6},{8,9},{9,8},{10,11... | collective-permute-start | bytes 153608 | tf_op jit(solution)/shard_map/ppermute | solution.py:387
  62.2 1.4 %collective-permute-start.19 = (f32[208,128]{1,0:T(8,128)S(1)}, f32[208,128]{1,0:T(8,128)S(1)}, u32[]{:S(2)}, u32[]{:S(2)}) collective-permute-start(f32[208,128]{1,0:T(8,128)S(1)} %get-tuple-element.123), channel_id=1, source_target_pairs={{0,1},{1,0},{2,3},{3,2},{4,5},{5,4},{6,7},{7,6},{8,9},{9,8},{10,11... | collective-permute-start | bytes 319496 | tf_op jit(solution)/shard_map/ppermute | solution.py:387
  67.0 3.5 %collective-permute-start.21 = (f32[128,200]{1,0:T(8,128)S(1)}, f32[128,200]{1,0:T(8,128)S(1)}, u32[]{:S(2)}, u32[]{:S(2)}) collective-permute-start(f32[128,200]{1,0:T(8,128)S(1)} %slice.66), channel_id=1, source_target_pairs={{0,1},{1,0},{2,3},{3,2},{4,5},{5,4},{6,7},{7,6},{8,9},{9,8},{10,11... | collective-permute-start | bytes 307208 | tf_op jit(solution)/shard_map/ppermute | solution.py:387
  70.5 6.6 %collective-permute-start.22 = (bf16[1,208,128]{2,1,0:T(8,128)(2,1)S(1)}, bf16[1,208,128]{2,1,0:T(8,128)(2,1)S(1)}, u32[]{:S(2)}, u32[]{:S(2)}) collective-permute-start(bf16[1,208,128]{2,1,0:T(8,128)(2,1)S(1)} %bitcast.13), channel_id=1, source_target_pairs={{0,4},{1,5},{2,6},{3,7},{4,0},{5,1},{6,2},{7,3},{8,12},{9,13},{10,... | collective-permute-start | bytes 159752 | tf_op jit(solution)/shard_map/ppermute | solution.py:387
  72.4 4.7 %collective-permute-start.23 = (f32[64,200]{1,0:T(8,128)S(1)}, f32[64,200]{1,0:T(8,128)S(1)}, u32[]{:S(2)}, u32[]{:S(2)}) collective-permute-start(f32[64,200]{1,0:T(8,128)S(1)} %slice.77), channel_id=1, source_target_pairs={{0,2},{1,3},{2,0},{3,1},{4,6},{5,7},{6,4},{7,5},{8,10},{9,11},{10,... | collective-permute-start | bytes 153608 | tf_op jit(solution)/shard_map/ppermute | solution.py:387
  77.1 7.3 %collective-permute-start.25 = (f32[160,200]{1,0:T(8,128)S(1)}, f32[160,200]{1,0:T(8,128)S(1)}, u32[]{:S(2)}, u32[]{:S(2)}) collective-permute-start(f32[160,200]{1,0:T(8,128)S(1)} %pad_maximum_fusion.3), channel_id=1, source_target_pairs={{0,16},{1,17},{2,18},{3,19},{4,20},{5,21},{6,22},{7,23},{8,24},{9,... | collective-permute-start | bytes 384008 | tf_op jit(solution)/shard_map/ppermute | solution.py:387
  77.8 6.6 %collective-permute-start.24 = (bf16[2,208,128]{2,1,0:T(8,128)(2,1)S(1)}, bf16[2,208,128]{2,1,0:T(8,128)(2,1)S(1)}, u32[]{:S(2)}, u32[]{:S(2)}) collective-permute-start(bf16[2,208,128]{2,1,0:T(8,128)(2,1)S(1)} %pad_maximum_fusion.7), channel_id=1, source_target_pairs={{0,2},{1,3},{2,0},{3,1},{4,6},{5,7},{6,4},{7,5},{8,10},{9,11},{10,... | collective-permute-start | bytes 319496 | tf_op jit(solution)/shard_map/ppermute | solution.py:387
  78.7 5.7 %collective-permute-start.26 = (f32[32,200]{1,0:T(8,128)S(1)}, f32[32,200]{1,0:T(8,128)S(1)}, u32[]{:S(2)}, u32[]{:S(2)}) collective-permute-start(f32[32,200]{1,0:T(8,128)S(1)} %get-tuple-element.162), channel_id=1, source_target_pairs={{0,20},{1,21},{2,22},{3,23},{4,16},{5,17},{6,18},{7,19},{8,28},{9,... | collective-permute-start | bytes 76808 | tf_op jit(solution)/shard_map/ppermute | solution.py:387
  84.4 6.3 %collective-permute-start.27 = (bf16[4,208,128]{2,1,0:T(8,128)(2,1)S(1)}, bf16[4,208,128]{2,1,0:T(8,128)(2,1)S(1)}, u32[]{:S(2)}, u32[]{:S(2)}) collective-permute-start(bf16[4,208,128]{2,1,0:T(8,128)(2,1)S(1)} %pad_maximum_fusion.1.refs_0_), channel_id=1, source_target_pairs={{0,8},{1,9},{2,10},{3,11},{4,12},{5,13},{6,14},{7,15},{8,0},{9,1},... | collective-permute-start | bytes 638984 | tf_op jit(solution)/shard_map/ppermute | solution.py:387
  86.0 5.8 %collective-permute-start.28 = (bf16[4,208,128]{2,1,0:T(8,128)(2,1)S(1)}, bf16[4,208,128]{2,1,0:T(8,128)(2,1)S(1)}, u32[]{:S(2)}, u32[]{:S(2)}) collective-permute-start(bf16[4,208,128]{2,1,0:T(8,128)(2,1)S(1)} %pad_maximum_fusion.1.refs_0_), channel_id=1, source_target_pairs={{0,16},{1,17},{2,18},{3,19},{4,20},{5,21},{6,22},{7,23},{8,24},{9,... | collective-permute-start | bytes 638984 | tf_op jit(solution)/shard_map/ppermute | solution.py:387
  91.9 7.7 %collective-permute-start.30 = (f32[200,1408]{1,0:T(8,128)S(1)}, f32[200,1408]{1,0:T(8,128)S(1)}, u32[]{:S(2)}, u32[]{:S(2)}) collective-permute-start(f32[200,1408]{1,0:T(8,128)S(1)} %relation_sums.1.refs_0_), channel_id=1, source_target_pairs={{0,1},{1,0},{2,3},{3,2},{4,5},{5,4},{6,7},{7,6},{8,9},{9,8},{10,11... | collective-permute-start | bytes 3379208 | tf_op jit(solution)/shard_map/ppermute | solution.py:387
  91.9 7.7 %collective-permute-start.29 = (bf16[4,208,128]{2,1,0:T(8,128)(2,1)S(1)}, bf16[4,208,128]{2,1,0:T(8,128)(2,1)S(1)}, u32[]{:S(2)}, u32[]{:S(2)}) collective-permute-start(bf16[4,208,128]{2,1,0:T(8,128)(2,1)S(1)} %collective-permute-done.27.refs_1_), channel_id=1, source_target_pairs={{0,16},{1,17},{2,18},{3,19},{4,20},{5,21},{6,22},{7,23},{8,24},{9,... | collective-permute-start | bytes 638984 | tf_op jit(solution)/shard_map/ppermute | solution.py:387
  100.9 2.8 %collective-permute-start.31 = (f32[200,1408]{1,0:T(8,128)S(1)}, f32[200,1408]{1,0:T(8,128)S(1)}, u32[]{:S(2)}, u32[]{:S(2)}) collective-permute-start(f32[200,1408]{1,0:T(8,128)S(1)} %late_sums.1.refs_2_), channel_id=1, source_target_pairs={{0,1},{1,0},{2,3},{3,2},{4,5},{5,4},{6,7},{7,6},{8,9},{9,8},{10,11... | collective-permute-start | bytes 3379208 | tf_op jit(solution)/shard_map/ppermute | solution.py:387
  (13 other events, 74.3 us)

commit v5 on v4

--- a/solution.py
+++ b/solution.py
@@ -59,7 +59,7 @@
         scratch_shapes=list(scratch),
         compiler_params=pltpu.CompilerParams(vmem_limit_bytes=limit * 1024 * 1024),
         cost_estimate=pl.CostEstimate(
-            flops=int(micros * 1e9), bytes_accessed=int(micros * 3e6), transcendentals=0
+            flops=int(micros * 3e9), bytes_accessed=int(micros * 9e6), transcendentals=0
         ),
         name=name,
     )(*args)
@@ -236,7 +236,7 @@
 
 def forward_kernel(
     round_index, fc_ref, heads_ref, ent_ref, own_ref, other_ref, rows_ref, state_ref, band_ref, bias_ref, fcb_ref,
-    pre2_out, slopes, _, picture, work,
+    pre2_out, slopes, fc_same, ent_same, picture, work,
 ):
     gradient = (own_ref[...] + other_ref[...])[:D, :]
     state = state_ref[...] + jnp.mean(gradient * gradient, axis=0, keepdims=True)
@@ -290,7 +290,8 @@
 ):
     count = ent_ref.shape[1]
     number = back_ref.shape[0] - negatives
-    back = jnp.concatenate([back_ref[:number, :], back_ref[number:, :] + other_ref[...]], axis=0)
+    back = back_ref[...].astype(f32)
+    back = jnp.concatenate([back[:number, :], back[number:, :] + other_ref[...].astype(f32)], axis=0)
     grads = jnp.concatenate([head_ref[...], turned(back)], axis=1)
     high, low = halves(grads)
     named = jnp.concatenate(
@@ -366,7 +367,7 @@
         state = state + jnp.mean(gradient * gradient, axis=0, keepdims=True)
         rows = rows - gradient * (learn_rate * lax.rsqrt(state))
     refs[2 * ROUNDS][...] = rows
-    refs[2 * ROUNDS + 1][...] = state
+    refs[2 * ROUNDS + 1][...] = state[0]
 
 
 class Plan:
@@ -499,17 +500,22 @@
     for r in range(ROUNDS):
         last = r == ROUNDS - 1
         if r > 0:
-            pre2, slopes, fc = call(
+            pre2, slopes, fc, ent = call(
                 functools.partial(forward_kernel, r),
                 "forward",
                 2.5,
-                [shaped((number, D)), shaped((PAIRS, number, WIDE)), shaped(fc.shape, bf16)],
+                [
+                    shaped((number, D)),
+                    shaped((PAIRS, number, WIDE)),
+                    shaped(fc.shape, bf16),
+                    shaped(ent.shape),
+                ],
                 (fc, head_ids, ent, *rel_inputs, band, bias, bias2),
                 [pltpu.VMEM((PIXELS, number), f32), pltpu.VMEM((PAIRS, number, WIDE), bf16)],
                 limit=LIM,
-                near=(0,),
-                near_out=(1, 2),
-                alias={0: 2},
+                near=(0, 2),
+                near_out=(1, 2, 3),
+                alias={0: 2, 2: 3},
             )
         grad2, tail_grad, neg_part = call(
             score_kernel,
@@ -519,9 +525,7 @@
             (pre2, near[:number], negset),
         )
         if r == 0:
-            grad2, neg_part, requested[1], rel_others = together(
-                grad2, neg_part, requested[1], rel_others
-            )
+            grad2, neg_part, rel_others = together(grad2, neg_part, rel_others)
         half = neg_part.shape[0] // 2
         arrived = send(neg_part[half:], 1)
         pack, head_grad, fc = call(
@@ -543,35 +547,47 @@
         share = neg_part[:half] + arrived
         packs = pack[None]
         lead = list(plan.lead)
+        if last:
+            before = call(
+                functools.partial(sums_kernel, (3, 0)),
+                "early_sums",
+                3,
+                [shaped((D, wide))] * 2,
+                (place, *groups[:3]),
+                lay(3 * group),
+                scalars=1,
+            )
         back = list(reversed(beyond))
         for step, mask in enumerate(lead):
             came = send(packs, mask)
             if step < len(back):
                 half = share.shape[0] // 2
                 arrived = send(share[half:], back[step])
-                came, arrived = together(came, arrived)
+                if last:
+                    came, arrived, *before = together(came, arrived, *before)
+                    (part,) = call(
+                        functools.partial(sums_kernel, (1, 2)),
+                        "late_sums",
+                        1,
+                        [shaped((D, wide))],
+                        (place, groups[3], *before),
+                        lay(group),
+                        scalars=1,
+                    )
+                else:
+                    came, arrived, requested[1] = together(came, arrived, requested[1])
                 share = share[:half] + arrived
             elif step == len(lead) - 1:
-                own_back = jnp.concatenate([tail_grad, share[:negatives]], axis=0)
+                own_back = jnp.concatenate([tail_grad, share[:negatives]], axis=0).astype(bf16)
+                side_back = share[negatives:].astype(bf16)
                 to_owner = send(own_back, plan.partner(r))
-                to_side = send(share[negatives:], plan.partner(r) | next_door)
-                came, to_owner, to_side = together(came, to_owner, to_side)
+                to_side = send(side_back, plan.partner(r) | next_door)
+                if last:
+                    came, to_owner, to_side, part = together(came, to_owner, to_side, part)
             packs = jnp.concatenate([packs, came], axis=0)
         one, other = plan.far[-2:]
         across = send(packs, one)
         along = send(packs, other)
-        if last:
-            (part,) = call(
-                functools.partial(sums_kernel, (4, 0)),
-                "relation_sums",
-                3,
-                [shaped((D, wide))],
-                (place, *groups),
-                lay(4 * group),
-                scalars=1,
-            )
-            across, along, part, to_owner, to_side = together(across, along, part, to_owner, to_side)
-            sums = [part, send(part, 1)]
         out_shape = [shaped(ent.shape), shaped(ent_state.shape)]
         outs = call(
             functools.partial(entity_kernel, r, negatives),
@@ -588,9 +604,13 @@
                 to_owner,
                 to_side,
             ),
+            near=(3,) if last else (),
+            near_out=() if last else (0,),
         )
         ent, ent_state = outs[:2]
         if last:
+            across, along, ent, ent_state, part = together(across, along, ent, ent_state, part)
+            sums = [part, send(part, 1)]
             corner = send(across, other)
             early = call(
                 functools.partial(sums_kernel, (3, 0)),
@@ -601,8 +621,7 @@
                 lay(3 * group),
                 scalars=1,
             )
-            corner, ent, ent_state, *rest = together(corner, ent, ent_state, *early, *sums)
-            early, sums = rest[:2], rest[2:]
+            corner, *early = together(corner, *early)
             (part,) = call(
                 functools.partial(sums_kernel, (1, 2)),
                 "late_sums",
@@ -634,9 +653,9 @@
             rel_inputs = (own, send(partial, 1), rel_later, state_later)
             negset = jnp.concatenate([negset, send(negset, 1)], axis=0)
     rel, rel_state = call(
-        relation_kernel, "relation_update", 2, [shaped((D, count)), shaped((1, count))], (rel, rel_state, *sums)
-    )
-    return (ent.T, ent_state.reshape(-1), rel.T, rel_state.reshape(-1))
+        relation_kernel, "relation_update", 2, [shaped((D, count)), shaped((count,))], (rel, rel_state, *sums)
+    )
+    return (ent.T, ent_state.reshape(-1), rel.T, rel_state)
 
 
 def solution(mesh):

time: 106 us -> 101 us (0.953)
  waiting for transfers between devices: 31.8 us -> 27 us
    ppermute x32, waiting for transfers between devices: 31.8 us -> 27 us  [send(): return lax.ppermute(block, BOTH, self.route(mask))]
    pallas_call x16 -> x17, Pallas kernels: 31.6 us -> 32.4 us  [call(): pl.pallas_call(kernel, out_shape=[pltpu.VMEM(out.shape, out.dtype) if ind...]
  transfers between devices with their start and end apart: 32 -> 32, of which waited for: 17 -> 18; matrix products, arithmetic and copies ran while one was open for 0% -> 0% of each run, Pallas kernels for 21% -> 25%
where the time goes in v5:
time: 101 us
  starting transfers between devices  39.4 us (39%)
  Pallas kernels  32.4 us (32%)
  waiting for transfers between devices  27 us (27%)
  between operations  1.11 us (1%)
    ppermute x32, starting transfers between devices, send(): return lax.ppermute(block, BOTH, self.route(mask))  39.4 us
    pallas_call x17, Pallas kernels, call(): pl.pallas_call(kernel, out_shape=[pltpu.VMEM(out.shape, out.dtype) if ind...  32.4 us
    ppermute x32, waiting for transfers between devices, send(): return lax.ppermute(block, BOTH, self.route(mask))  27 us
  transfers between devices with their start and end apart: 32, of which 18 were waited for; matrix products, arithmetic and copies ran while one was open for 0% of the time, Pallas kernels for 25%

profile of v5, /device:TPU:0, one launch (start us, length us, event | category | flops | bytes accessed | tf_op | source)
XLA Modules:
  0.0 100.6 jit_solution(5168619899839400192)
XLA Ops:
  1.5 3.0 %collective-permute-start = (s32[2,128]{1,0:T(2,128)S(1)}, s32[2,128]{1,0:T(2,128)S(1)}, u32[]{:S(2)}, u32[]{:S(2)}) collective-permute-start(s32[2,128]{1,0:T(2,128)S(1)} %get-tuple-element.82), channel_id=1, source_target_pairs={{0,8},{1,9},{2,10},{3,11},{4,12},{5,13},{6,14},{7,15},{8,0},{9,1},... | collective-permute-start | bytes 3080 | tf_op jit(solution)/shard_map/ppermute | solution.py:388
  6.5 2.1 %collective-permute-start.1 = (bf16[160,200]{1,0:T(8,128)(2,1)S(1)}, bf16[160,200]{1,0:T(8,128)(2,1)S(1)}, u32[]{:S(2)}, u32[]{:S(2)}) collective-permute-start(bf16[160,200]{1,0:T(8,128)(2,1)S(1)} %answer.1), channel_id=1, source_target_pairs={{0,8},{1,9},{2,10},{3,11},{4,12},{5,13},{6,14},{7,15},{8,0},{9,1},... | collective-permute-start | bytes 192008 | tf_op jit(solution)/shard_map/ppermute | solution.py:388
  8.5 2.6 %collective-permute-start.2 = (bf16[32,200]{1,0:T(8,128)(2,1)S(1)}, bf16[32,200]{1,0:T(8,128)(2,1)S(1)}, u32[]{:S(2)}, u32[]{:S(2)}) collective-permute-start(bf16[32,200]{1,0:T(8,128)(2,1)S(1)} %slice.76), channel_id=1, source_target_pairs={{0,12},{1,13},{2,14},{3,15},{4,8},{5,9},{6,10},{7,11},{8,4},{9,5},... | collective-permute-start | bytes 38408 | tf_op jit(solution)/shard_map/ppermute | solution.py:388
  11.1 6.7 %first_forward.1 = (f32[128,200]{1,0:T(8,128)S(1)}, f32[9,128,1152]{2,1,0:T(8,128)S(1)}, bf16[9,1152,200]{2,1,0:T(8,128)(2,1)S(1)}, bf16[80,1152]{1,0:T(8,128)(2,1)S(1)}, bf16[1152,128]{1,0:T(8,128)(2,1)S(1)}) custom-call(bf16[200,10368]{1,0:T(8,128)(2,1)} %bitcast.30, f32[9,1152]{1,0:T(8,128)S(1)} %tile.18.taps_ref, s32[2,128]{1,0:T(2,128)S(1)} %copy-done.5, ...), custom_call_target="tpu_custom_call" | custom-call | flops 17999998976 | bytes 54000000 | tf_op jit(solution)/shard_map/first_forward/pallas_call | solution.py:50
  17.9 1.6 %collective-permute-start.3 = (bf16[64,200]{1,0:T(8,128)(2,1)S(1)}, bf16[64,200]{1,0:T(8,128)(2,1)S(1)}, u32[]{:S(2)}, u32[]{:S(2)}) collective-permute-start(bf16[64,200]{1,0:T(8,128)(2,1)S(1)} %pad_maximum_fusion.10), channel_id=1, source_target_pairs={{0,2},{1,3},{2,0},{3,1},{4,6},{5,7},{6,4},{7,5},{8,10},{9,11},{10,... | collective-permute-start | bytes 76808 | tf_op jit(solution)/shard_map/ppermute | solution.py:388
  19.5 2.3 %collective-permute-done.3 = bf16[64,200]{1,0:T(8,128)(2,1)S(1)} collective-permute-done((bf16[64,200]{1,0:T(8,128)(2,1)S(1)}, bf16[64,200]{1,0:T(8,128)(2,1)S(1)}, u32[]{:S(2)}, u32[]{:S(2)}) %collective-permute-start.3) | collective-permute-done | bytes 25632 | tf_op jit(solution)/shard_map/ppermute | solution.py:388
  24.0 3.0 %backward.2 = (bf16[208,128]{1,0:T(8,128)(2,1)S(1)}, f32[200,128]{1,0:T(8,128)S(1)}, bf16[9,1152,200]{2,1,0:T(8,128)(2,1)S(1)}) custom-call(bf16[9,1152,200]{2,1,0:T(8,128)(2,1)S(1)} %get-tuple-element.87.fc_ref, s32[2,128]{1,0:T(2,128)S(1)} %copy-done.4, bf16[128,200]{1,0:T(8,128)(2,1)S(1)} %get-tuple-element.97.grad_ref, ...), custom_call_target="tpu_custom_call", output_to_operand_aliasing={{2}: (0, {})} | custom-call | flops 8999999488 | bytes 27000000 | tf_op jit(solution)/shard_map/backward/pallas_call | solution.py:50
  27.1 1.9 %collective-permute-start.8 = (f32[64,200]{1,0:T(8,128)S(1)}, f32[64,200]{1,0:T(8,128)S(1)}, u32[]{:S(2)}, u32[]{:S(2)}) collective-permute-start(f32[64,200]{1,0:T(8,128)S(1)} %slice.77), channel_id=1, source_target_pairs={{0,2},{1,3},{2,0},{3,1},{4,6},{5,7},{6,4},{7,5},{8,10},{9,11},{10,... | collective-permute-start | bytes 153608 | tf_op jit(solution)/shard_map/ppermute | solution.py:388
  30.6 2.0 %collective-permute-done.9.next_ref.asked_ref = s32[2,128]{1,0:T(2,128)S(1)} collective-permute-done((s32[2,128]{1,0:T(2,128)S(1)}, s32[2,128]{1,0:T(2,128)S(1)}, u32[]{:S(2)}, u32[]{:S(2)}) %collective-permute-start.9) | collective-permute-done | bytes 1056 | tf_op jit(solution)/shard_map/ppermute | solution.py:388
  34.3 1.6 %collective-permute-start.10 = (bf16[160,200]{1,0:T(8,128)(2,1)S(1)}, bf16[160,200]{1,0:T(8,128)(2,1)S(1)}, u32[]{:S(2)}, u32[]{:S(2)}) collective-permute-start(bf16[160,200]{1,0:T(8,128)(2,1)S(1)} %pad_maximum_fusion.6), channel_id=1, source_target_pairs={{0,8},{1,9},{2,10},{3,11},{4,12},{5,13},{6,14},{7,15},{8,0},{9,1},... | collective-permute-start | bytes 192008 | tf_op jit(solution)/shard_map/ppermute | solution.py:388
  35.9 2.1 %collective-permute-start.11 = (bf16[32,200]{1,0:T(8,128)(2,1)S(1)}, bf16[32,200]{1,0:T(8,128)(2,1)S(1)}, u32[]{:S(2)}, u32[]{:S(2)}) collective-permute-start(bf16[32,200]{1,0:T(8,128)(2,1)S(1)} %get-tuple-element.162), channel_id=1, source_target_pairs={{0,12},{1,13},{2,14},{3,15},{4,8},{5,9},{6,10},{7,11},{8,4},{9,5},... | collective-permute-start | bytes 38408 | tf_op jit(solution)/shard_map/ppermute | solution.py:388
  38.0 1.6 %collective-permute-start.16 = (bf16[4,208,128]{2,1,0:T(8,128)(2,1)S(1)}, bf16[4,208,128]{2,1,0:T(8,128)(2,1)S(1)}, u32[]{:S(2)}, u32[]{:S(2)}) collective-permute-start(bf16[4,208,128]{2,1,0:T(8,128)(2,1)S(1)} %pad_maximum_fusion.refs_0_), channel_id=1, source_target_pairs={{0,8},{1,9},{2,10},{3,11},{4,12},{5,13},{6,14},{7,15},{8,0},{9,1},... | collective-permute-start | bytes 638984 | tf_op jit(solution)/shard_map/ppermute | solution.py:388
  39.6 1.9 %collective-permute-done.11.other_ref = bf16[32,200]{1,0:T(8,128)(2,1)S(1)} collective-permute-done((bf16[32,200]{1,0:T(8,128)(2,1)S(1)}, bf16[32,200]{1,0:T(8,128)(2,1)S(1)}, u32[]{:S(2)}, u32[]{:S(2)}) %collective-permute-start.11) | collective-permute-done | bytes 12832 | tf_op jit(solution)/shard_map/ppermute | solution.py:388
  42.7 1.6 %collective-permute-start.12 = (bf16[160,200]{1,0:T(8,128)(2,1)S(1)}, bf16[160,200]{1,0:T(8,128)(2,1)S(1)}, u32[]{:S(2)}, u32[]{:S(2)}) collective-permute-start(bf16[160,200]{1,0:T(8,128)(2,1)S(1)} %get-tuple-element.111), channel_id=1, source_target_pairs={{0,16},{1,17},{2,18},{3,19},{4,20},{5,21},{6,22},{7,23},{8,24},{9,... | collective-permute-start | bytes 192008 | tf_op jit(solution)/shard_map/ppermute | solution.py:388
  44.2 2.0 %collective-permute-start.13 = (bf16[32,200]{1,0:T(8,128)(2,1)S(1)}, bf16[32,200]{1,0:T(8,128)(2,1)S(1)}, u32[]{:S(2)}, u32[]{:S(2)}) collective-permute-start(bf16[32,200]{1,0:T(8,128)(2,1)S(1)} %slice.67), channel_id=1, source_target_pairs={{0,20},{1,21},{2,22},{3,23},{4,16},{5,17},{6,18},{7,19},{8,28},{9,... | collective-permute-start | bytes 38408 | tf_op jit(solution)/shard_map/ppermute | solution.py:388
  46.3 1.6 %collective-permute-start.17 = (bf16[4,208,128]{2,1,0:T(8,128)(2,1)S(1)}, bf16[4,208,128]{2,1,0:T(8,128)(2,1)S(1)}, u32[]{:S(2)}, u32[]{:S(2)}) collective-permute-start(bf16[4,208,128]{2,1,0:T(8,128)(2,1)S(1)} %pad_maximum_fusion.refs_0_), channel_id=1, source_target_pairs={{0,16},{1,17},{2,18},{3,19},{4,20},{5,21},{6,22},{7,23},{8,24},{9,... | collective-permute-start | bytes 638984 | tf_op jit(solution)/shard_map/ppermute | solution.py:388
  47.8 2.0 %collective-permute-done.13 = bf16[32,200]{1,0:T(8,128)(2,1)S(1)} collective-permute-done((bf16[32,200]{1,0:T(8,128)(2,1)S(1)}, bf16[32,200]{1,0:T(8,128)(2,1)S(1)}, u32[]{:S(2)}, u32[]{:S(2)}) %collective-permute-start.13) | collective-permute-done | bytes 12832 | tf_op jit(solution)/shard_map/ppermute | solution.py:388
  51.2 2.7 %collective-permute-done.14 = bf16[64,200]{1,0:T(8,128)(2,1)S(1)} collective-permute-done((bf16[64,200]{1,0:T(8,128)(2,1)S(1)}, bf16[64,200]{1,0:T(8,128)(2,1)S(1)}, u32[]{:S(2)}, u32[]{:S(2)}) %collective-permute-start.14) | collective-permute-done | bytes 25632 | tf_op jit(solution)/shard_map/ppermute | solution.py:388
  54.2 2.3 %collective-permute-done.18.refs_3_.refs_0_ = bf16[4,208,128]{2,1,0:T(8,128)(2,1)S(1)} collective-permute-done((bf16[4,208,128]{2,1,0:T(8,128)(2,1)S(1)}, bf16[4,208,128]{2,1,0:T(8,128)(2,1)S(1)}, u32[]{:S(2)}, u32[]{:S(2)}) %collective-permute-start.18) | collective-permute-done | bytes 213024 | tf_op jit(solution)/shard_map/ppermute | solution.py:388
  59.4 2.9 %forward.1 = (f32[128,200]{1,0:T(8,128)S(1)}, f32[9,128,1152]{2,1,0:T(8,128)S(1)}, bf16[9,1152,200]{2,1,0:T(8,128)(2,1)S(1)}, f32[200,1024]{1,0:T(8,128)S(1)}) custom-call(bf16[9,1152,200]{2,1,0:T(8,128)(2,1)S(1)} %bitcast.28, s32[2,128]{1,0:T(2,128)S(1)} %copy-done.5, ...), custom_call_target="tpu_custom_call", output_to_operand_aliasing={{2}: (0, {}), {3}: (2, {})} | custom-call | flops 7500000256 | bytes 22500000 | tf_op jit(solution)/shard_map/forward/pallas_call | solution.py:50
  63.3 3.0 %backward.3 = (bf16[208,128]{1,0:T(8,128)(2,1)S(1)}, f32[200,128]{1,0:T(8,128)S(1)}, bf16[9,1152,200]{2,1,0:T(8,128)(2,1)S(1)}) custom-call(bf16[9,1152,200]{2,1,0:T(8,128)(2,1)S(1)} %get-tuple-element.123.fc_ref, s32[2,128]{1,0:T(2,128)S(1)} %copy-done.4, bf16[128,200]{1,0:T(8,128)(2,1)S(1)} %get-tuple-element.126.grad_ref, ...), custom_call_target="tpu_custom_call", output_to_operand_aliasing={{2}: (0, {})} | custom-call | flops 8999999488 | bytes 27000000 | tf_op jit(solution)/shard_map/backward/pallas_call | solution.py:50
  66.3 2.5 %collective-permute-start.22 = (bf16[1,208,128]{2,1,0:T(8,128)(2,1)S(1)}, bf16[1,208,128]{2,1,0:T(8,128)(2,1)S(1)}, u32[]{:S(2)}, u32[]{:S(2)}) collective-permute-start(bf16[1,208,128]{2,1,0:T(8,128)(2,1)S(1)} %bitcast.13), channel_id=1, source_target_pairs={{0,4},{1,5},{2,6},{3,7},{4,0},{5,1},{6,2},{7,3},{8,12},{9,13},{10,... | collective-permute-start | bytes 159752 | tf_op jit(solution)/shard_map/ppermute | solution.py:388
  69.9 2.6 %early_sums.2 = (f32[200,1408]{1,0:T(8,128)S(1)}, f32[200,1408]{1,0:T(8,128)S(1)}) custom-call(s32[4]{0:T(128)S(1)} %iota_xor_fusion.place_ref, bf16[4,208,128]{2,1,0:T(8,128)(2,1)S(1)} %pad_maximum_fusion.refs_0_, bf16[4,208,128]{2,1,0:T(8,128)(2,1)S(1)} %collective-permute-done.16.refs_1_, bf16[4,208,128]{2,1,0:T(8,128)(2,1)S(1)} %collective-permute-done.17.refs_2_), custom_call_target="tpu_custom_call" | custom-call | flops 8999999488 | bytes 27000000 | tf_op jit(solution)/shard_map/early_sums/pallas_call | solution.py:50
  75.0 2.6 %collective-permute-start.26 = (bf16[32,200]{1,0:T(8,128)(2,1)S(1)}, bf16[32,200]{1,0:T(8,128)(2,1)S(1)}, u32[]{:S(2)}, u32[]{:S(2)}) collective-permute-start(bf16[32,200]{1,0:T(8,128)(2,1)S(1)} %get-tuple-element.160), channel_id=1, source_target_pairs={{0,20},{1,21},{2,22},{3,23},{4,16},{5,17},{6,18},{7,19},{8,28},{9,... | collective-permute-start | bytes 38408 | tf_op jit(solution)/shard_map/ppermute | solution.py:388
  79.0 1.6 %collective-permute-done.26.other_ref = bf16[32,200]{1,0:T(8,128)(2,1)S(1)} collective-permute-done((bf16[32,200]{1,0:T(8,128)(2,1)S(1)}, bf16[32,200]{1,0:T(8,128)(2,1)S(1)}, u32[]{:S(2)}, u32[]{:S(2)}) %collective-permute-start.26) | collective-permute-done | bytes 12832 | tf_op jit(solution)/shard_map/ppermute | solution.py:388
  82.7 1.7 %entity_update.3 = (f32[200,1024]{1,0:T(8,128)}, f32[1,1024]{1,0:T(1,128)}) custom-call(s32[2,128]{1,0:T(2,128)S(1)} %copy-done.5, s32[2,128]{1,0:T(2,128)S(1)} %collective-permute-done.9.next_ref.asked_ref, s32[2,128]{1,0:T(2,128)S(1)} %collective-permute-done.9.next_ref.asked_ref, f32[200,1024]{1,0:T(8,128)S(1)} %get-tuple-element.140.ent_ref, ...), custom_call_target="tpu_custom_call" | custom-call | flops 4499999744 | bytes 13500000 | tf_op jit(solution)/shard_map/entity_update/pallas_call | solution.py:50
  84.4 2.1 %collective-permute-done.27.refs_1_ = bf16[4,208,128]{2,1,0:T(8,128)(2,1)S(1)} collective-permute-done((bf16[4,208,128]{2,1,0:T(8,128)(2,1)S(1)}, bf16[4,208,128]{2,1,0:T(8,128)(2,1)S(1)}, u32[]{:S(2)}, u32[]{:S(2)}) %collective-permute-start.27) | collective-permute-done | bytes 213024 | tf_op jit(solution)/shard_map/ppermute | solution.py:388
  87.0 1.5 %collective-permute-start.30 = (bf16[4,208,128]{2,1,0:T(8,128)(2,1)S(1)}, bf16[4,208,128]{2,1,0:T(8,128)(2,1)S(1)}, u32[]{:S(2)}, u32[]{:S(2)}) collective-permute-start(bf16[4,208,128]{2,1,0:T(8,128)(2,1)S(1)} %collective-permute-done.27.refs_1_), channel_id=1, source_target_pairs={{0,16},{1,17},{2,18},{3,19},{4,20},{5,21},{6,22},{7,23},{8,24},{9,... | collective-permute-start | bytes 638984 | tf_op jit(solution)/shard_map/ppermute | solution.py:388
  88.5 2.6 %early_sums.3 = (f32[200,1408]{1,0:T(8,128)S(1)}, f32[200,1408]{1,0:T(8,128)S(1)}) custom-call(s32[4]{0:T(128)S(1)} %iota_xor_fusion.place_ref, bf16[4,208,128]{2,1,0:T(8,128)(2,1)S(1)} %pad_maximum_fusion.1.refs_0_, bf16[4,208,128]{2,1,0:T(8,128)(2,1)S(1)} %collective-permute-done.27.refs_1_, bf16[4,208,128]{2,1,0:T(8,128)(2,1)S(1)} %collective-permute-done.28.refs_2_), custom_call_target="tpu_custom_call" | custom-call | flops 8999999488 | bytes 27000000 | tf_op jit(solution)/shard_map/early_sums/pallas_call | solution.py:50
  91.1 3.6 %collective-permute-done.30.refs_0_ = bf16[4,208,128]{2,1,0:T(8,128)(2,1)S(1)} collective-permute-done((bf16[4,208,128]{2,1,0:T(8,128)(2,1)S(1)}, bf16[4,208,128]{2,1,0:T(8,128)(2,1)S(1)}, u32[]{:S(2)}, u32[]{:S(2)}) %collective-permute-start.30) | collective-permute-done | bytes 213024 | tf_op jit(solution)/shard_map/ppermute | solution.py:388
  96.1 2.7 %collective-permute-done.31.refs_3_ = f32[200,1408]{1,0:T(8,128)S(1)} collective-permute-done((f32[200,1408]{1,0:T(8,128)S(1)}, f32[200,1408]{1,0:T(8,128)S(1)}, u32[]{:S(2)}, u32[]{:S(2)}) %collective-permute-start.31) | collective-permute-done | bytes 1126432 | tf_op jit(solution)/shard_map/ppermute | solution.py:388
  98.9 1.7 %relation_update.1 = (f32[200,1387]{1,0:T(8,128)}, f32[1387]{0:T(1024)}) custom-call(f32[200,1387]{1,0:T(8,128)S(1)} %bitcast.20, f32[1,1387]{1,0:T(1,128)S(1)} %broadcast_in_dim.15.state_ref, f32[200,1408]{1,0:T(8,128)S(1)} %late_sums.2.refs_0_, f32[200,1408]{1,0:T(8,128)S(1)} %collective-permute-done.29.refs_1_, f32[200,1408]{1,0:T(8,128)S(1)} %late_sums.3.refs_2_, ...), custom_call_target="tpu_custom_call" | custom-call | flops 6000000000 | bytes 18000000 | tf_op jit(solution)/shard_map/relation_update/pallas_call | solution.py:50
  (119 shorter events, 23.7 us)
Async XLA Ops:
  1.5 4.6 %collective-permute-start = (s32[2,128]{1,0:T(2,128)S(1)}, s32[2,128]{1,0:T(2,128)S(1)}, u32[]{:S(2)}, u32[]{:S(2)}) collective-permute-start(s32[2,128]{1,0:T(2,128)S(1)} %get-tuple-element.82), channel_id=1, source_target_pairs={{0,8},{1,9},{2,10},{3,11},{4,12},{5,13},{6,14},{7,15},{8,0},{9,1},... | collective-permute-start | bytes 3080 | tf_op jit(solution)/shard_map/ppermute | solution.py:388
  6.5 11.4 %collective-permute-start.1 = (bf16[160,200]{1,0:T(8,128)(2,1)S(1)}, bf16[160,200]{1,0:T(8,128)(2,1)S(1)}, u32[]{:S(2)}, u32[]{:S(2)}) collective-permute-start(bf16[160,200]{1,0:T(8,128)(2,1)S(1)} %answer.1), channel_id=1, source_target_pairs={{0,8},{1,9},{2,10},{3,11},{4,12},{5,13},{6,14},{7,15},{8,0},{9,1},... | collective-permute-start | bytes 192008 | tf_op jit(solution)/shard_map/ppermute | solution.py:388
  8.5 9.3 %collective-permute-start.2 = (bf16[32,200]{1,0:T(8,128)(2,1)S(1)}, bf16[32,200]{1,0:T(8,128)(2,1)S(1)}, u32[]{:S(2)}, u32[]{:S(2)}) collective-permute-start(bf16[32,200]{1,0:T(8,128)(2,1)S(1)} %slice.76), channel_id=1, source_target_pairs={{0,12},{1,13},{2,14},{3,15},{4,8},{5,9},{6,10},{7,11},{8,4},{9,5},... | collective-permute-start | bytes 38408 | tf_op jit(solution)/shard_map/ppermute | solution.py:388
  17.9 4.0 %collective-permute-start.3 = (bf16[64,200]{1,0:T(8,128)(2,1)S(1)}, bf16[64,200]{1,0:T(8,128)(2,1)S(1)}, u32[]{:S(2)}, u32[]{:S(2)}) collective-permute-start(bf16[64,200]{1,0:T(8,128)(2,1)S(1)} %pad_maximum_fusion.10), channel_id=1, source_target_pairs={{0,2},{1,3},{2,0},{3,1},{4,6},{5,7},{6,4},{7,5},{8,10},{9,11},{10,... | collective-permute-start | bytes 76808 | tf_op jit(solution)/shard_map/ppermute | solution.py:388
  21.9 1.3 %collective-permute-start.4 = (bf16[128,200]{1,0:T(8,128)(2,1)S(1)}, bf16[128,200]{1,0:T(8,128)(2,1)S(1)}, u32[]{:S(2)}, u32[]{:S(2)}) collective-permute-start(bf16[128,200]{1,0:T(8,128)(2,1)S(1)} %pad_maximum_fusion.8), channel_id=1, source_target_pairs={{0,1},{1,0},{2,3},{3,2},{4,5},{5,4},{6,7},{7,6},{8,9},{9,8},{10,11... | collective-permute-start | bytes 153608 | tf_op jit(solution)/shard_map/ppermute | solution.py:388
  22.0 1.7 %collective-permute-start.5 = (s32[2,128]{1,0:T(2,128)S(1)}, s32[2,128]{1,0:T(2,128)S(1)}, u32[]{:S(2)}, u32[]{:S(2)}) collective-permute-start(s32[2,128]{1,0:T(2,128)S(1)} %copy-done.4), channel_id=1, source_target_pairs={{0,1},{1,0},{2,3},{3,2},{4,5},{5,4},{6,7},{7,6},{8,9},{9,8},{10,11... | collective-permute-start | bytes 3080 | tf_op jit(solution)/shard_map/ppermute | solution.py:388
  23.7 3.2 %collective-permute-start.6 = (f32[128,200]{1,0:T(8,128)S(1)}, f32[128,200]{1,0:T(8,128)S(1)}, u32[]{:S(2)}, u32[]{:S(2)}) collective-permute-start(f32[128,200]{1,0:T(8,128)S(1)} %slice.61), channel_id=1, source_target_pairs={{0,1},{1,0},{2,3},{3,2},{4,5},{5,4},{6,7},{7,6},{8,9},{9,8},{10,11... | collective-permute-start | bytes 307208 | tf_op jit(solution)/shard_map/ppermute | solution.py:388
  27.0 5.8 %collective-permute-start.7 = (bf16[1,208,128]{2,1,0:T(8,128)(2,1)S(1)}, bf16[1,208,128]{2,1,0:T(8,128)(2,1)S(1)}, u32[]{:S(2)}, u32[]{:S(2)}) collective-permute-start(bf16[1,208,128]{2,1,0:T(8,128)(2,1)S(1)} %bitcast.16), channel_id=1, source_target_pairs={{0,4},{1,5},{2,6},{3,7},{4,0},{5,1},{6,2},{7,3},{8,12},{9,13},{10,... | collective-permute-start | bytes 159752 | tf_op jit(solution)/shard_map/ppermute | solution.py:388
  27.1 5.5 %collective-permute-start.8 = (f32[64,200]{1,0:T(8,128)S(1)}, f32[64,200]{1,0:T(8,128)S(1)}, u32[]{:S(2)}, u32[]{:S(2)}) collective-permute-start(f32[64,200]{1,0:T(8,128)S(1)} %slice.77), channel_id=1, source_target_pairs={{0,2},{1,3},{2,0},{3,1},{4,6},{5,7},{6,4},{7,5},{8,10},{9,11},{10,... | collective-permute-start | bytes 153608 | tf_op jit(solution)/shard_map/ppermute | solution.py:388
  29.1 3.6 %collective-permute-start.9 = (s32[2,128]{1,0:T(2,128)S(1)}, s32[2,128]{1,0:T(2,128)S(1)}, u32[]{:S(2)}, u32[]{:S(2)}) collective-permute-start(s32[2,128]{1,0:T(2,128)S(1)} %get-tuple-element.105), channel_id=1, source_target_pairs={{0,16},{1,17},{2,18},{3,19},{4,20},{5,21},{6,22},{7,23},{8,24},{9,... | collective-permute-start | bytes 3080 | tf_op jit(solution)/shard_map/ppermute | solution.py:388
  32.9 5.1 %collective-permute-start.15 = (bf16[2,208,128]{2,1,0:T(8,128)(2,1)S(1)}, bf16[2,208,128]{2,1,0:T(8,128)(2,1)S(1)}, u32[]{:S(2)}, u32[]{:S(2)}) collective-permute-start(bf16[2,208,128]{2,1,0:T(8,128)(2,1)S(1)} %pad_maximum_fusion.4), channel_id=1, source_target_pairs={{0,2},{1,3},{2,0},{3,1},{4,6},{5,7},{6,4},{7,5},{8,10},{9,11},{10,... | collective-permute-start | bytes 319496 | tf_op jit(solution)/shard_map/ppermute | solution.py:388
  34.3 7.2 %collective-permute-start.10 = (bf16[160,200]{1,0:T(8,128)(2,1)S(1)}, bf16[160,200]{1,0:T(8,128)(2,1)S(1)}, u32[]{:S(2)}, u32[]{:S(2)}) collective-permute-start(bf16[160,200]{1,0:T(8,128)(2,1)S(1)} %pad_maximum_fusion.6), channel_id=1, source_target_pairs={{0,8},{1,9},{2,10},{3,11},{4,12},{5,13},{6,14},{7,15},{8,0},{9,1},... | collective-permute-start | bytes 192008 | tf_op jit(solution)/shard_map/ppermute | solution.py:388
  35.9 5.6 %collective-permute-start.11 = (bf16[32,200]{1,0:T(8,128)(2,1)S(1)}, bf16[32,200]{1,0:T(8,128)(2,1)S(1)}, u32[]{:S(2)}, u32[]{:S(2)}) collective-permute-start(bf16[32,200]{1,0:T(8,128)(2,1)S(1)} %get-tuple-element.162), channel_id=1, source_target_pairs={{0,12},{1,13},{2,14},{3,15},{4,8},{5,9},{6,10},{7,11},{8,4},{9,5},... | collective-permute-start | bytes 38408 | tf_op jit(solution)/shard_map/ppermute | solution.py:388
  38.0 12.6 %collective-permute-start.16 = (bf16[4,208,128]{2,1,0:T(8,128)(2,1)S(1)}, bf16[4,208,128]{2,1,0:T(8,128)(2,1)S(1)}, u32[]{:S(2)}, u32[]{:S(2)}) collective-permute-start(bf16[4,208,128]{2,1,0:T(8,128)(2,1)S(1)} %pad_maximum_fusion.refs_0_), channel_id=1, source_target_pairs={{0,8},{1,9},{2,10},{3,11},{4,12},{5,13},{6,14},{7,15},{8,0},{9,1},... | collective-permute-start | bytes 638984 | tf_op jit(solution)/shard_map/ppermute | solution.py:388
  42.7 7.2 %collective-permute-start.12 = (bf16[160,200]{1,0:T(8,128)(2,1)S(1)}, bf16[160,200]{1,0:T(8,128)(2,1)S(1)}, u32[]{:S(2)}, u32[]{:S(2)}) collective-permute-start(bf16[160,200]{1,0:T(8,128)(2,1)S(1)} %get-tuple-element.111), channel_id=1, source_target_pairs={{0,16},{1,17},{2,18},{3,19},{4,20},{5,21},{6,22},{7,23},{8,24},{9,... | collective-permute-start | bytes 192008 | tf_op jit(solution)/shard_map/ppermute | solution.py:388
  44.2 5.6 %collective-permute-start.13 = (bf16[32,200]{1,0:T(8,128)(2,1)S(1)}, bf16[32,200]{1,0:T(8,128)(2,1)S(1)}, u32[]{:S(2)}, u32[]{:S(2)}) collective-permute-start(bf16[32,200]{1,0:T(8,128)(2,1)S(1)} %slice.67), channel_id=1, source_target_pairs={{0,20},{1,21},{2,22},{3,23},{4,16},{5,17},{6,18},{7,19},{8,28},{9,... | collective-permute-start | bytes 38408 | tf_op jit(solution)/shard_map/ppermute | solution.py:388
  46.3 7.9 %collective-permute-start.17 = (bf16[4,208,128]{2,1,0:T(8,128)(2,1)S(1)}, bf16[4,208,128]{2,1,0:T(8,128)(2,1)S(1)}, u32[]{:S(2)}, u32[]{:S(2)}) collective-permute-start(bf16[4,208,128]{2,1,0:T(8,128)(2,1)S(1)} %pad_maximum_fusion.refs_0_), channel_id=1, source_target_pairs={{0,16},{1,17},{2,18},{3,19},{4,20},{5,21},{6,22},{7,23},{8,24},{9,... | collective-permute-start | bytes 638984 | tf_op jit(solution)/shard_map/ppermute | solution.py:388
  49.9 4.0 %collective-permute-start.14 = (bf16[64,200]{1,0:T(8,128)(2,1)S(1)}, bf16[64,200]{1,0:T(8,128)(2,1)S(1)}, u32[]{:S(2)}, u32[]{:S(2)}) collective-permute-start(bf16[64,200]{1,0:T(8,128)(2,1)S(1)} %pad_maximum_fusion.11), channel_id=1, source_target_pairs={{0,2},{1,3},{2,0},{3,1},{4,6},{5,7},{6,4},{7,5},{8,10},{9,11},{10,... | collective-permute-start | bytes 76808 | tf_op jit(solution)/shard_map/ppermute | solution.py:388
  50.7 5.8 %collective-permute-start.18 = (bf16[4,208,128]{2,1,0:T(8,128)(2,1)S(1)}, bf16[4,208,128]{2,1,0:T(8,128)(2,1)S(1)}, u32[]{:S(2)}, u32[]{:S(2)}) collective-permute-start(bf16[4,208,128]{2,1,0:T(8,128)(2,1)S(1)} %collective-permute-done.16.refs_1_), channel_id=1, source_target_pairs={{0,16},{1,17},{2,18},{3,19},{4,20},{5,21},{6,22},{7,23},{8,24},{9,... | collective-permute-start | bytes 638984 | tf_op jit(solution)/shard_map/ppermute | solution.py:388
  57.9 1.3 %collective-permute-start.20 = (bf16[128,200]{1,0:T(8,128)(2,1)S(1)}, bf16[128,200]{1,0:T(8,128)(2,1)S(1)}, u32[]{:S(2)}, u32[]{:S(2)}) collective-permute-start(bf16[128,200]{1,0:T(8,128)(2,1)S(1)} %pad_maximum_fusion.9), channel_id=1, source_target_pairs={{0,1},{1,0},{2,3},{3,2},{4,5},{5,4},{6,7},{7,6},{8,9},{9,8},{10,11... | collective-permute-start | bytes 153608 | tf_op jit(solution)/shard_map/ppermute | solution.py:388
  58.0 1.4 %collective-permute-start.19 = (f32[208,128]{1,0:T(8,128)S(1)}, f32[208,128]{1,0:T(8,128)S(1)}, u32[]{:S(2)}, u32[]{:S(2)}) collective-permute-start(f32[208,128]{1,0:T(8,128)S(1)} %get-tuple-element.119), channel_id=1, source_target_pairs={{0,1},{1,0},{2,3},{3,2},{4,5},{5,4},{6,7},{7,6},{8,9},{9,8},{10,11... | collective-permute-start | bytes 319496 | tf_op jit(solution)/shard_map/ppermute | solution.py:388
  62.8 3.5 %collective-permute-start.21 = (f32[128,200]{1,0:T(8,128)S(1)}, f32[128,200]{1,0:T(8,128)S(1)}, u32[]{:S(2)}, u32[]{:S(2)}) collective-permute-start(f32[128,200]{1,0:T(8,128)S(1)} %slice.70), channel_id=1, source_target_pairs={{0,1},{1,0},{2,3},{3,2},{4,5},{5,4},{6,7},{7,6},{8,9},{9,8},{10,11... | collective-permute-start | bytes 307208 | tf_op jit(solution)/shard_map/ppermute | solution.py:388
  66.3 7.0 %collective-permute-start.22 = (bf16[1,208,128]{2,1,0:T(8,128)(2,1)S(1)}, bf16[1,208,128]{2,1,0:T(8,128)(2,1)S(1)}, u32[]{:S(2)}, u32[]{:S(2)}) collective-permute-start(bf16[1,208,128]{2,1,0:T(8,128)(2,1)S(1)} %bitcast.13), channel_id=1, source_target_pairs={{0,4},{1,5},{2,6},{3,7},{4,0},{5,1},{6,2},{7,3},{8,12},{9,13},{10,... | collective-permute-start | bytes 159752 | tf_op jit(solution)/shard_map/ppermute | solution.py:388
  68.8 4.5 %collective-permute-start.23 = (f32[64,200]{1,0:T(8,128)S(1)}, f32[64,200]{1,0:T(8,128)S(1)}, u32[]{:S(2)}, u32[]{:S(2)}) collective-permute-start(f32[64,200]{1,0:T(8,128)S(1)} %slice.81), channel_id=1, source_target_pairs={{0,2},{1,3},{2,0},{3,1},{4,6},{5,7},{6,4},{7,5},{8,10},{9,11},{10,... | collective-permute-start | bytes 153608 | tf_op jit(solution)/shard_map/ppermute | solution.py:388
  73.3 7.3 %collective-permute-start.24 = (bf16[2,208,128]{2,1,0:T(8,128)(2,1)S(1)}, bf16[2,208,128]{2,1,0:T(8,128)(2,1)S(1)}, u32[]{:S(2)}, u32[]{:S(2)}) collective-permute-start(bf16[2,208,128]{2,1,0:T(8,128)(2,1)S(1)} %pad_maximum_fusion.5), channel_id=1, source_target_pairs={{0,2},{1,3},{2,0},{3,1},{4,6},{5,7},{6,4},{7,5},{8,10},{9,11},{10,... | collective-permute-start | bytes 319496 | tf_op jit(solution)/shard_map/ppermute | solution.py:388
  74.4 6.1 %collective-permute-start.25 = (bf16[160,200]{1,0:T(8,128)(2,1)S(1)}, bf16[160,200]{1,0:T(8,128)(2,1)S(1)}, u32[]{:S(2)}, u32[]{:S(2)}) collective-permute-start(bf16[160,200]{1,0:T(8,128)(2,1)S(1)} %pad_maximum_fusion.7), channel_id=1, source_target_pairs={{0,16},{1,17},{2,18},{3,19},{4,20},{5,21},{6,22},{7,23},{8,24},{9,... | collective-permute-start | bytes 192008 | tf_op jit(solution)/shard_map/ppermute | solution.py:388
  75.0 5.5 %collective-permute-start.26 = (bf16[32,200]{1,0:T(8,128)(2,1)S(1)}, bf16[32,200]{1,0:T(8,128)(2,1)S(1)}, u32[]{:S(2)}, u32[]{:S(2)}) collective-permute-start(bf16[32,200]{1,0:T(8,128)(2,1)S(1)} %get-tuple-element.160), channel_id=1, source_target_pairs={{0,20},{1,21},{2,22},{3,23},{4,16},{5,17},{6,18},{7,19},{8,28},{9,... | collective-permute-start | bytes 38408 | tf_op jit(solution)/shard_map/ppermute | solution.py:388
  80.6 5.9 %collective-permute-start.27 = (bf16[4,208,128]{2,1,0:T(8,128)(2,1)S(1)}, bf16[4,208,128]{2,1,0:T(8,128)(2,1)S(1)}, u32[]{:S(2)}, u32[]{:S(2)}) collective-permute-start(bf16[4,208,128]{2,1,0:T(8,128)(2,1)S(1)} %pad_maximum_fusion.1.refs_0_), channel_id=1, source_target_pairs={{0,8},{1,9},{2,10},{3,11},{4,12},{5,13},{6,14},{7,15},{8,0},{9,1},... | collective-permute-start | bytes 638984 | tf_op jit(solution)/shard_map/ppermute | solution.py:388
  81.2 5.8 %collective-permute-start.28 = (bf16[4,208,128]{2,1,0:T(8,128)(2,1)S(1)}, bf16[4,208,128]{2,1,0:T(8,128)(2,1)S(1)}, u32[]{:S(2)}, u32[]{:S(2)}) collective-permute-start(bf16[4,208,128]{2,1,0:T(8,128)(2,1)S(1)} %pad_maximum_fusion.1.refs_0_), channel_id=1, source_target_pairs={{0,16},{1,17},{2,18},{3,19},{4,20},{5,21},{6,22},{7,23},{8,24},{9,... | collective-permute-start | bytes 638984 | tf_op jit(solution)/shard_map/ppermute | solution.py:388
  87.0 9.1 %collective-permute-start.29 = (f32[200,1408]{1,0:T(8,128)S(1)}, f32[200,1408]{1,0:T(8,128)S(1)}, u32[]{:S(2)}, u32[]{:S(2)}) collective-permute-start(f32[200,1408]{1,0:T(8,128)S(1)} %late_sums.2.refs_0_), channel_id=1, source_target_pairs={{0,1},{1,0},{2,3},{3,2},{4,5},{5,4},{6,7},{7,6},{8,9},{9,8},{10,11... | collective-permute-start | bytes 3379208 | tf_op jit(solution)/shard_map/ppermute | solution.py:388
  87.0 7.7 %collective-permute-start.30 = (bf16[4,208,128]{2,1,0:T(8,128)(2,1)S(1)}, bf16[4,208,128]{2,1,0:T(8,128)(2,1)S(1)}, u32[]{:S(2)}, u32[]{:S(2)}) collective-permute-start(bf16[4,208,128]{2,1,0:T(8,128)(2,1)S(1)} %collective-permute-done.27.refs_1_), channel_id=1, source_target_pairs={{0,16},{1,17},{2,18},{3,19},{4,20},{5,21},{6,22},{7,23},{8,24},{9,... | collective-permute-start | bytes 638984 | tf_op jit(solution)/shard_map/ppermute | solution.py:388
  96.0 2.8 %collective-permute-start.31 = (f32[200,1408]{1,0:T(8,128)S(1)}, f32[200,1408]{1,0:T(8,128)S(1)}, u32[]{:S(2)}, u32[]{:S(2)}) collective-permute-start(f32[200,1408]{1,0:T(8,128)S(1)} %late_sums.3.refs_2_), channel_id=1, source_target_pairs={{0,1},{1,0},{2,3},{3,2},{4,5},{5,4},{6,7},{7,6},{8,9},{9,8},{10,11... | collective-permute-start | bytes 3379208 | tf_op jit(solution)/shard_map/ppermute | solution.py:388
  (16 other events, 85.1 us)

commit v6 on v5

--- a/solution.py
+++ b/solution.py
@@ -583,11 +583,13 @@
                 to_owner = send(own_back, plan.partner(r))
                 to_side = send(side_back, plan.partner(r) | next_door)
                 if last:
-                    came, to_owner, to_side, part = together(came, to_owner, to_side, part)
+                    came, part = together(came, part)
             packs = jnp.concatenate([packs, came], axis=0)
         one, other = plan.far[-2:]
         across = send(packs, one)
         along = send(packs, other)
+        if last:
+            across, along, to_owner, to_side = together(across, along, to_owner, to_side)
         out_shape = [shaped(ent.shape), shaped(ent_state.shape)]
         outs = call(
             functools.partial(entity_kernel, r, negatives),
@@ -609,8 +611,7 @@
         )
         ent, ent_state = outs[:2]
         if last:
-            across, along, ent, ent_state, part = together(across, along, ent, ent_state, part)
-            sums = [part, send(part, 1)]
+            across, along, part = together(across, along, part)
             corner = send(across, other)
             early = call(
                 functools.partial(sums_kernel, (3, 0)),
@@ -621,7 +622,8 @@
                 lay(3 * group),
                 scalars=1,
             )
-            corner, *early = together(corner, *early)
+            corner, part, ent, ent_state, *early = together(corner, part, ent, ent_state, *early)
+            sums = [part, send(part, 1)]
             (part,) = call(
                 functools.partial(sums_kernel, (1, 2)),
                 "late_sums",

time: 101 us -> 98.6 us (0.976)
  waiting for transfers between devices: 27 us -> 25.7 us
    ppermute x32, waiting for transfers between devices: 27 us -> 25.7 us  [send(): return lax.ppermute(block, BOTH, self.route(mask))]
where the time goes in v6:
time: 98.6 us; the launch traced here: 98.4 us
  starting transfers between devices  38.5 us (39%)
  Pallas kernels  32.4 us (33%)
  waiting for transfers between devices  25.7 us (26%)
  between operations  1.1 us (1%)
    ppermute x32, starting transfers between devices, send(): return lax.ppermute(block, BOTH, self.route(mask))  38.5 us
    pallas_call x17, Pallas kernels, call(): pl.pallas_call(kernel, out_shape=[pltpu.VMEM(out.shape, out.dtype) if ind...  32.4 us
    ppermute x32, waiting for transfers between devices, send(): return lax.ppermute(block, BOTH, self.route(mask))  25.7 us
  transfers between devices with their start and end apart: 32, of which 18 were waited for; matrix products, arithmetic and copies ran while one was open for 0% of the time, Pallas kernels for 25%

profile of v6, /device:TPU:0, one launch (start us, length us, event | category | flops | bytes accessed | tf_op | source)
XLA Modules:
  0.0 98.4 jit_solution(647625606554099112)
XLA Ops:
  1.5 3.0 %collective-permute-start = (s32[2,128]{1,0:T(2,128)S(1)}, s32[2,128]{1,0:T(2,128)S(1)}, u32[]{:S(2)}, u32[]{:S(2)}) collective-permute-start(s32[2,128]{1,0:T(2,128)S(1)} %get-tuple-element.85), channel_id=1, source_target_pairs={{0,8},{1,9},{2,10},{3,11},{4,12},{5,13},{6,14},{7,15},{8,0},{9,1},... | collective-permute-start | bytes 3080 | tf_op jit(solution)/shard_map/ppermute | solution.py:388
  6.5 2.1 %collective-permute-start.1 = (bf16[160,200]{1,0:T(8,128)(2,1)S(1)}, bf16[160,200]{1,0:T(8,128)(2,1)S(1)}, u32[]{:S(2)}, u32[]{:S(2)}) collective-permute-start(bf16[160,200]{1,0:T(8,128)(2,1)S(1)} %answer.1), channel_id=1, source_target_pairs={{0,8},{1,9},{2,10},{3,11},{4,12},{5,13},{6,14},{7,15},{8,0},{9,1},... | collective-permute-start | bytes 192008 | tf_op jit(solution)/shard_map/ppermute | solution.py:388
  8.5 2.6 %collective-permute-start.2 = (bf16[32,200]{1,0:T(8,128)(2,1)S(1)}, bf16[32,200]{1,0:T(8,128)(2,1)S(1)}, u32[]{:S(2)}, u32[]{:S(2)}) collective-permute-start(bf16[32,200]{1,0:T(8,128)(2,1)S(1)} %slice.76), channel_id=1, source_target_pairs={{0,12},{1,13},{2,14},{3,15},{4,8},{5,9},{6,10},{7,11},{8,4},{9,5},... | collective-permute-start | bytes 38408 | tf_op jit(solution)/shard_map/ppermute | solution.py:388
  11.1 6.7 %first_forward.1 = (f32[128,200]{1,0:T(8,128)S(1)}, f32[9,128,1152]{2,1,0:T(8,128)S(1)}, bf16[9,1152,200]{2,1,0:T(8,128)(2,1)S(1)}, bf16[80,1152]{1,0:T(8,128)(2,1)S(1)}, bf16[1152,128]{1,0:T(8,128)(2,1)S(1)}) custom-call(bf16[200,10368]{1,0:T(8,128)(2,1)} %bitcast.30, f32[9,1152]{1,0:T(8,128)S(1)} %tile.18.taps_ref, s32[2,128]{1,0:T(2,128)S(1)} %copy-done.5, ...), custom_call_target="tpu_custom_call" | custom-call | flops 17999998976 | bytes 54000000 | tf_op jit(solution)/shard_map/first_forward/pallas_call | solution.py:50
  17.9 1.6 %collective-permute-start.3 = (bf16[64,200]{1,0:T(8,128)(2,1)S(1)}, bf16[64,200]{1,0:T(8,128)(2,1)S(1)}, u32[]{:S(2)}, u32[]{:S(2)}) collective-permute-start(bf16[64,200]{1,0:T(8,128)(2,1)S(1)} %pad_maximum_fusion.10), channel_id=1, source_target_pairs={{0,2},{1,3},{2,0},{3,1},{4,6},{5,7},{6,4},{7,5},{8,10},{9,11},{10,... | collective-permute-start | bytes 76808 | tf_op jit(solution)/shard_map/ppermute | solution.py:388
  19.5 2.3 %collective-permute-done.3 = bf16[64,200]{1,0:T(8,128)(2,1)S(1)} collective-permute-done((bf16[64,200]{1,0:T(8,128)(2,1)S(1)}, bf16[64,200]{1,0:T(8,128)(2,1)S(1)}, u32[]{:S(2)}, u32[]{:S(2)}) %collective-permute-start.3) | collective-permute-done | bytes 25632 | tf_op jit(solution)/shard_map/ppermute | solution.py:388
  24.0 3.0 %backward.2 = (bf16[208,128]{1,0:T(8,128)(2,1)S(1)}, f32[200,128]{1,0:T(8,128)S(1)}, bf16[9,1152,200]{2,1,0:T(8,128)(2,1)S(1)}) custom-call(bf16[9,1152,200]{2,1,0:T(8,128)(2,1)S(1)} %get-tuple-element.90.fc_ref, s32[2,128]{1,0:T(2,128)S(1)} %copy-done.4, bf16[128,200]{1,0:T(8,128)(2,1)S(1)} %get-tuple-element.100.grad_ref, ...), custom_call_target="tpu_custom_call", output_to_operand_aliasing={{2}: (0, {})} | custom-call | flops 8999999488 | bytes 27000000 | tf_op jit(solution)/shard_map/backward/pallas_call | solution.py:50
  27.1 1.9 %collective-permute-start.8 = (f32[64,200]{1,0:T(8,128)S(1)}, f32[64,200]{1,0:T(8,128)S(1)}, u32[]{:S(2)}, u32[]{:S(2)}) collective-permute-start(f32[64,200]{1,0:T(8,128)S(1)} %slice.77), channel_id=1, source_target_pairs={{0,2},{1,3},{2,0},{3,1},{4,6},{5,7},{6,4},{7,5},{8,10},{9,11},{10,... | collective-permute-start | bytes 153608 | tf_op jit(solution)/shard_map/ppermute | solution.py:388
  29.1 1.5 %collective-permute-start.9 = (s32[2,128]{1,0:T(2,128)S(1)}, s32[2,128]{1,0:T(2,128)S(1)}, u32[]{:S(2)}, u32[]{:S(2)}) collective-permute-start(s32[2,128]{1,0:T(2,128)S(1)} %get-tuple-element.108), channel_id=1, source_target_pairs={{0,16},{1,17},{2,18},{3,19},{4,20},{5,21},{6,22},{7,23},{8,24},{9,... | collective-permute-start | bytes 3080 | tf_op jit(solution)/shard_map/ppermute | solution.py:388
  30.6 2.0 %collective-permute-done.9.next_ref.asked_ref = s32[2,128]{1,0:T(2,128)S(1)} collective-permute-done((s32[2,128]{1,0:T(2,128)S(1)}, s32[2,128]{1,0:T(2,128)S(1)}, u32[]{:S(2)}, u32[]{:S(2)}) %collective-permute-start.9) | collective-permute-done | bytes 1056 | tf_op jit(solution)/shard_map/ppermute | solution.py:388
  32.9 1.4 %collective-permute-start.15 = (bf16[2,208,128]{2,1,0:T(8,128)(2,1)S(1)}, bf16[2,208,128]{2,1,0:T(8,128)(2,1)S(1)}, u32[]{:S(2)}, u32[]{:S(2)}) collective-permute-start(bf16[2,208,128]{2,1,0:T(8,128)(2,1)S(1)} %pad_maximum_fusion.4), channel_id=1, source_target_pairs={{0,2},{1,3},{2,0},{3,1},{4,6},{5,7},{6,4},{7,5},{8,10},{9,11},{10,... | collective-permute-start | bytes 319496 | tf_op jit(solution)/shard_map/ppermute | solution.py:388
  34.3 1.6 %collective-permute-start.10 = (bf16[160,200]{1,0:T(8,128)(2,1)S(1)}, bf16[160,200]{1,0:T(8,128)(2,1)S(1)}, u32[]{:S(2)}, u32[]{:S(2)}) collective-permute-start(bf16[160,200]{1,0:T(8,128)(2,1)S(1)} %pad_maximum_fusion.6), channel_id=1, source_target_pairs={{0,8},{1,9},{2,10},{3,11},{4,12},{5,13},{6,14},{7,15},{8,0},{9,1},... | collective-permute-start | bytes 192008 | tf_op jit(solution)/shard_map/ppermute | solution.py:388
  35.9 2.1 %collective-permute-start.11 = (bf16[32,200]{1,0:T(8,128)(2,1)S(1)}, bf16[32,200]{1,0:T(8,128)(2,1)S(1)}, u32[]{:S(2)}, u32[]{:S(2)}) collective-permute-start(bf16[32,200]{1,0:T(8,128)(2,1)S(1)} %get-tuple-element.168), channel_id=1, source_target_pairs={{0,12},{1,13},{2,14},{3,15},{4,8},{5,9},{6,10},{7,11},{8,4},{9,5},... | collective-permute-start | bytes 38408 | tf_op jit(solution)/shard_map/ppermute | solution.py:388
  38.0 1.6 %collective-permute-start.16 = (bf16[4,208,128]{2,1,0:T(8,128)(2,1)S(1)}, bf16[4,208,128]{2,1,0:T(8,128)(2,1)S(1)}, u32[]{:S(2)}, u32[]{:S(2)}) collective-permute-start(bf16[4,208,128]{2,1,0:T(8,128)(2,1)S(1)} %pad_maximum_fusion.refs_0_), channel_id=1, source_target_pairs={{0,8},{1,9},{2,10},{3,11},{4,12},{5,13},{6,14},{7,15},{8,0},{9,1},... | collective-permute-start | bytes 638984 | tf_op jit(solution)/shard_map/ppermute | solution.py:388
  39.6 1.9 %collective-permute-done.11.other_ref = bf16[32,200]{1,0:T(8,128)(2,1)S(1)} collective-permute-done((bf16[32,200]{1,0:T(8,128)(2,1)S(1)}, bf16[32,200]{1,0:T(8,128)(2,1)S(1)}, u32[]{:S(2)}, u32[]{:S(2)}) %collective-permute-start.11) | collective-permute-done | bytes 12832 | tf_op jit(solution)/shard_map/ppermute | solution.py:388
  42.7 1.6 %collective-permute-start.12 = (bf16[160,200]{1,0:T(8,128)(2,1)S(1)}, bf16[160,200]{1,0:T(8,128)(2,1)S(1)}, u32[]{:S(2)}, u32[]{:S(2)}) collective-permute-start(bf16[160,200]{1,0:T(8,128)(2,1)S(1)} %get-tuple-element.114), channel_id=1, source_target_pairs={{0,16},{1,17},{2,18},{3,19},{4,20},{5,21},{6,22},{7,23},{8,24},{9,... | collective-permute-start | bytes 192008 | tf_op jit(solution)/shard_map/ppermute | solution.py:388
  44.2 2.0 %collective-permute-start.13 = (bf16[32,200]{1,0:T(8,128)(2,1)S(1)}, bf16[32,200]{1,0:T(8,128)(2,1)S(1)}, u32[]{:S(2)}, u32[]{:S(2)}) collective-permute-start(bf16[32,200]{1,0:T(8,128)(2,1)S(1)} %slice.67), channel_id=1, source_target_pairs={{0,20},{1,21},{2,22},{3,23},{4,16},{5,17},{6,18},{7,19},{8,28},{9,... | collective-permute-start | bytes 38408 | tf_op jit(solution)/shard_map/ppermute | solution.py:388
  46.3 1.6 %collective-permute-start.17 = (bf16[4,208,128]{2,1,0:T(8,128)(2,1)S(1)}, bf16[4,208,128]{2,1,0:T(8,128)(2,1)S(1)}, u32[]{:S(2)}, u32[]{:S(2)}) collective-permute-start(bf16[4,208,128]{2,1,0:T(8,128)(2,1)S(1)} %pad_maximum_fusion.refs_0_), channel_id=1, source_target_pairs={{0,16},{1,17},{2,18},{3,19},{4,20},{5,21},{6,22},{7,23},{8,24},{9,... | collective-permute-start | bytes 638984 | tf_op jit(solution)/shard_map/ppermute | solution.py:388
  47.8 2.0 %collective-permute-done.13 = bf16[32,200]{1,0:T(8,128)(2,1)S(1)} collective-permute-done((bf16[32,200]{1,0:T(8,128)(2,1)S(1)}, bf16[32,200]{1,0:T(8,128)(2,1)S(1)}, u32[]{:S(2)}, u32[]{:S(2)}) %collective-permute-start.13) | collective-permute-done | bytes 12832 | tf_op jit(solution)/shard_map/ppermute | solution.py:388
  51.2 2.7 %collective-permute-done.14 = bf16[64,200]{1,0:T(8,128)(2,1)S(1)} collective-permute-done((bf16[64,200]{1,0:T(8,128)(2,1)S(1)}, bf16[64,200]{1,0:T(8,128)(2,1)S(1)}, u32[]{:S(2)}, u32[]{:S(2)}) %collective-permute-start.14) | collective-permute-done | bytes 25632 | tf_op jit(solution)/shard_map/ppermute | solution.py:388
  54.2 2.3 %collective-permute-done.18.refs_3_.refs_0_ = bf16[4,208,128]{2,1,0:T(8,128)(2,1)S(1)} collective-permute-done((bf16[4,208,128]{2,1,0:T(8,128)(2,1)S(1)}, bf16[4,208,128]{2,1,0:T(8,128)(2,1)S(1)}, u32[]{:S(2)}, u32[]{:S(2)}) %collective-permute-start.18) | collective-permute-done | bytes 213024 | tf_op jit(solution)/shard_map/ppermute | solution.py:388
  59.4 2.9 %forward.1 = (f32[128,200]{1,0:T(8,128)S(1)}, f32[9,128,1152]{2,1,0:T(8,128)S(1)}, bf16[9,1152,200]{2,1,0:T(8,128)(2,1)S(1)}, f32[200,1024]{1,0:T(8,128)S(1)}) custom-call(bf16[9,1152,200]{2,1,0:T(8,128)(2,1)S(1)} %bitcast.28, s32[2,128]{1,0:T(2,128)S(1)} %copy-done.5, ...), custom_call_target="tpu_custom_call", output_to_operand_aliasing={{2}: (0, {}), {3}: (2, {})} | custom-call | flops 7500000256 | bytes 22500000 | tf_op jit(solution)/shard_map/forward/pallas_call | solution.py:50
  63.3 3.0 %backward.3 = (bf16[208,128]{1,0:T(8,128)(2,1)S(1)}, f32[200,128]{1,0:T(8,128)S(1)}, bf16[9,1152,200]{2,1,0:T(8,128)(2,1)S(1)}) custom-call(bf16[9,1152,200]{2,1,0:T(8,128)(2,1)S(1)} %get-tuple-element.126.fc_ref, s32[2,128]{1,0:T(2,128)S(1)} %copy-done.4, bf16[128,200]{1,0:T(8,128)(2,1)S(1)} %get-tuple-element.129.grad_ref, ...), custom_call_target="tpu_custom_call", output_to_operand_aliasing={{2}: (0, {})} | custom-call | flops 8999999488 | bytes 27000000 | tf_op jit(solution)/shard_map/backward/pallas_call | solution.py:50
  66.3 2.5 %collective-permute-start.22 = (bf16[1,208,128]{2,1,0:T(8,128)(2,1)S(1)}, bf16[1,208,128]{2,1,0:T(8,128)(2,1)S(1)}, u32[]{:S(2)}, u32[]{:S(2)}) collective-permute-start(bf16[1,208,128]{2,1,0:T(8,128)(2,1)S(1)} %bitcast.16), channel_id=1, source_target_pairs={{0,4},{1,5},{2,6},{3,7},{4,0},{5,1},{6,2},{7,3},{8,12},{9,13},{10,... | collective-permute-start | bytes 159752 | tf_op jit(solution)/shard_map/ppermute | solution.py:388
  69.9 2.6 %early_sums.2 = (f32[200,1408]{1,0:T(8,128)S(1)}, f32[200,1408]{1,0:T(8,128)S(1)}) custom-call(s32[4]{0:T(128)S(1)} %iota_xor_fusion.place_ref, bf16[4,208,128]{2,1,0:T(8,128)(2,1)S(1)} %pad_maximum_fusion.refs_0_, bf16[4,208,128]{2,1,0:T(8,128)(2,1)S(1)} %collective-permute-done.16.refs_1_, bf16[4,208,128]{2,1,0:T(8,128)(2,1)S(1)} %collective-permute-done.17.refs_2_), custom_call_target="tpu_custom_call" | custom-call | flops 8999999488 | bytes 27000000 | tf_op jit(solution)/shard_map/early_sums/pallas_call | solution.py:50
  75.8 2.3 %collective-permute-done.24 = bf16[2,208,128]{2,1,0:T(8,128)(2,1)S(1)} collective-permute-done((bf16[2,208,128]{2,1,0:T(8,128)(2,1)S(1)}, bf16[2,208,128]{2,1,0:T(8,128)(2,1)S(1)}, u32[]{:S(2)}, u32[]{:S(2)}) %collective-permute-start.24) | collective-permute-done | bytes 106528 | tf_op jit(solution)/shard_map/ppermute | solution.py:388
  82.1 4.3 %collective-permute-done.28.other_ref = bf16[32,200]{1,0:T(8,128)(2,1)S(1)} collective-permute-done((bf16[32,200]{1,0:T(8,128)(2,1)S(1)}, bf16[32,200]{1,0:T(8,128)(2,1)S(1)}, u32[]{:S(2)}, u32[]{:S(2)}) %collective-permute-start.28) | collective-permute-done | bytes 12832 | tf_op jit(solution)/shard_map/ppermute | solution.py:388
  86.4 1.5 %collective-permute-start.29 = (bf16[4,208,128]{2,1,0:T(8,128)(2,1)S(1)}, bf16[4,208,128]{2,1,0:T(8,128)(2,1)S(1)}, u32[]{:S(2)}, u32[]{:S(2)}) collective-permute-start(bf16[4,208,128]{2,1,0:T(8,128)(2,1)S(1)} %collective-permute-done.25.refs_1_), channel_id=1, source_target_pairs={{0,16},{1,17},{2,18},{3,19},{4,20},{5,21},{6,22},{7,23},{8,24},{9,... | collective-permute-start | bytes 638984 | tf_op jit(solution)/shard_map/ppermute | solution.py:388
  87.8 2.6 %early_sums.3 = (f32[200,1408]{1,0:T(8,128)S(1)}, f32[200,1408]{1,0:T(8,128)S(1)}) custom-call(s32[4]{0:T(128)S(1)} %iota_xor_fusion.place_ref, bf16[4,208,128]{2,1,0:T(8,128)(2,1)S(1)} %pad_maximum_fusion.1.refs_0_, bf16[4,208,128]{2,1,0:T(8,128)(2,1)S(1)} %collective-permute-done.25.refs_1_, bf16[4,208,128]{2,1,0:T(8,128)(2,1)S(1)} %collective-permute-done.26.refs_2_), custom_call_target="tpu_custom_call" | custom-call | flops 8999999488 | bytes 27000000 | tf_op jit(solution)/shard_map/early_sums/pallas_call | solution.py:50
  90.4 1.7 %entity_update.3 = (f32[200,1024]{1,0:T(8,128)}, f32[1,1024]{1,0:T(1,128)}) custom-call(s32[2,128]{1,0:T(2,128)S(1)} %copy-done.5, s32[2,128]{1,0:T(2,128)S(1)} %collective-permute-done.9.next_ref.asked_ref, s32[2,128]{1,0:T(2,128)S(1)} %collective-permute-done.9.next_ref.asked_ref, f32[200,1024]{1,0:T(8,128)S(1)} %get-tuple-element.148.ent_ref, ...), custom_call_target="tpu_custom_call" | custom-call | flops 4499999744 | bytes 13500000 | tf_op jit(solution)/shard_map/entity_update/pallas_call | solution.py:50
  95.1 1.6 %collective-permute-done.31.refs_3_ = f32[200,1408]{1,0:T(8,128)S(1)} collective-permute-done((f32[200,1408]{1,0:T(8,128)S(1)}, f32[200,1408]{1,0:T(8,128)S(1)}, u32[]{:S(2)}, u32[]{:S(2)}) %collective-permute-start.31) | collective-permute-done | bytes 1126432 | tf_op jit(solution)/shard_map/ppermute | solution.py:388
  96.7 1.7 %relation_update.1 = (f32[200,1387]{1,0:T(8,128)}, f32[1387]{0:T(1024)}) custom-call(f32[200,1387]{1,0:T(8,128)S(1)} %bitcast.20, f32[1,1387]{1,0:T(1,128)S(1)} %broadcast_in_dim.15.state_ref, f32[200,1408]{1,0:T(8,128)S(1)} %late_sums.2.refs_0_, f32[200,1408]{1,0:T(8,128)S(1)} %collective-permute-done.30.refs_1_, f32[200,1408]{1,0:T(8,128)S(1)} %late_sums.3.refs_2_, ...), custom_call_target="tpu_custom_call" | custom-call | flops 6000000000 | bytes 18000000 | tf_op jit(solution)/shard_map/relation_update/pallas_call | solution.py:50
  (119 shorter events, 23.1 us)
Async XLA Ops:
  1.5 4.6 %collective-permute-start = (s32[2,128]{1,0:T(2,128)S(1)}, s32[2,128]{1,0:T(2,128)S(1)}, u32[]{:S(2)}, u32[]{:S(2)}) collective-permute-start(s32[2,128]{1,0:T(2,128)S(1)} %get-tuple-element.85), channel_id=1, source_target_pairs={{0,8},{1,9},{2,10},{3,11},{4,12},{5,13},{6,14},{7,15},{8,0},{9,1},... | collective-permute-start | bytes 3080 | tf_op jit(solution)/shard_map/ppermute | solution.py:388
  6.5 11.4 %collective-permute-start.1 = (bf16[160,200]{1,0:T(8,128)(2,1)S(1)}, bf16[160,200]{1,0:T(8,128)(2,1)S(1)}, u32[]{:S(2)}, u32[]{:S(2)}) collective-permute-start(bf16[160,200]{1,0:T(8,128)(2,1)S(1)} %answer.1), channel_id=1, source_target_pairs={{0,8},{1,9},{2,10},{3,11},{4,12},{5,13},{6,14},{7,15},{8,0},{9,1},... | collective-permute-start | bytes 192008 | tf_op jit(solution)/shard_map/ppermute | solution.py:388
  8.5 9.3 %collective-permute-start.2 = (bf16[32,200]{1,0:T(8,128)(2,1)S(1)}, bf16[32,200]{1,0:T(8,128)(2,1)S(1)}, u32[]{:S(2)}, u32[]{:S(2)}) collective-permute-start(bf16[32,200]{1,0:T(8,128)(2,1)S(1)} %slice.76), channel_id=1, source_target_pairs={{0,12},{1,13},{2,14},{3,15},{4,8},{5,9},{6,10},{7,11},{8,4},{9,5},... | collective-permute-start | bytes 38408 | tf_op jit(solution)/shard_map/ppermute | solution.py:388
  17.9 4.0 %collective-permute-start.3 = (bf16[64,200]{1,0:T(8,128)(2,1)S(1)}, bf16[64,200]{1,0:T(8,128)(2,1)S(1)}, u32[]{:S(2)}, u32[]{:S(2)}) collective-permute-start(bf16[64,200]{1,0:T(8,128)(2,1)S(1)} %pad_maximum_fusion.10), channel_id=1, source_target_pairs={{0,2},{1,3},{2,0},{3,1},{4,6},{5,7},{6,4},{7,5},{8,10},{9,11},{10,... | collective-permute-start | bytes 76808 | tf_op jit(solution)/shard_map/ppermute | solution.py:388
  21.9 1.3 %collective-permute-start.4 = (bf16[128,200]{1,0:T(8,128)(2,1)S(1)}, bf16[128,200]{1,0:T(8,128)(2,1)S(1)}, u32[]{:S(2)}, u32[]{:S(2)}) collective-permute-start(bf16[128,200]{1,0:T(8,128)(2,1)S(1)} %pad_maximum_fusion.8), channel_id=1, source_target_pairs={{0,1},{1,0},{2,3},{3,2},{4,5},{5,4},{6,7},{7,6},{8,9},{9,8},{10,11... | collective-permute-start | bytes 153608 | tf_op jit(solution)/shard_map/ppermute | solution.py:388
  22.0 1.7 %collective-permute-start.5 = (s32[2,128]{1,0:T(2,128)S(1)}, s32[2,128]{1,0:T(2,128)S(1)}, u32[]{:S(2)}, u32[]{:S(2)}) collective-permute-start(s32[2,128]{1,0:T(2,128)S(1)} %copy-done.4), channel_id=1, source_target_pairs={{0,1},{1,0},{2,3},{3,2},{4,5},{5,4},{6,7},{7,6},{8,9},{9,8},{10,11... | collective-permute-start | bytes 3080 | tf_op jit(solution)/shard_map/ppermute | solution.py:388
  23.7 3.2 %collective-permute-start.6 = (f32[128,200]{1,0:T(8,128)S(1)}, f32[128,200]{1,0:T(8,128)S(1)}, u32[]{:S(2)}, u32[]{:S(2)}) collective-permute-start(f32[128,200]{1,0:T(8,128)S(1)} %slice.61), channel_id=1, source_target_pairs={{0,1},{1,0},{2,3},{3,2},{4,5},{5,4},{6,7},{7,6},{8,9},{9,8},{10,11... | collective-permute-start | bytes 307208 | tf_op jit(solution)/shard_map/ppermute | solution.py:388
  27.0 5.8 %collective-permute-start.7 = (bf16[1,208,128]{2,1,0:T(8,128)(2,1)S(1)}, bf16[1,208,128]{2,1,0:T(8,128)(2,1)S(1)}, u32[]{:S(2)}, u32[]{:S(2)}) collective-permute-start(bf16[1,208,128]{2,1,0:T(8,128)(2,1)S(1)} %bitcast.13), channel_id=1, source_target_pairs={{0,4},{1,5},{2,6},{3,7},{4,0},{5,1},{6,2},{7,3},{8,12},{9,13},{10,... | collective-permute-start | bytes 159752 | tf_op jit(solution)/shard_map/ppermute | solution.py:388
  27.1 5.5 %collective-permute-start.8 = (f32[64,200]{1,0:T(8,128)S(1)}, f32[64,200]{1,0:T(8,128)S(1)}, u32[]{:S(2)}, u32[]{:S(2)}) collective-permute-start(f32[64,200]{1,0:T(8,128)S(1)} %slice.77), channel_id=1, source_target_pairs={{0,2},{1,3},{2,0},{3,1},{4,6},{5,7},{6,4},{7,5},{8,10},{9,11},{10,... | collective-permute-start | bytes 153608 | tf_op jit(solution)/shard_map/ppermute | solution.py:388
  29.1 3.6 %collective-permute-start.9 = (s32[2,128]{1,0:T(2,128)S(1)}, s32[2,128]{1,0:T(2,128)S(1)}, u32[]{:S(2)}, u32[]{:S(2)}) collective-permute-start(s32[2,128]{1,0:T(2,128)S(1)} %get-tuple-element.108), channel_id=1, source_target_pairs={{0,16},{1,17},{2,18},{3,19},{4,20},{5,21},{6,22},{7,23},{8,24},{9,... | collective-permute-start | bytes 3080 | tf_op jit(solution)/shard_map/ppermute | solution.py:388
  32.9 5.1 %collective-permute-start.15 = (bf16[2,208,128]{2,1,0:T(8,128)(2,1)S(1)}, bf16[2,208,128]{2,1,0:T(8,128)(2,1)S(1)}, u32[]{:S(2)}, u32[]{:S(2)}) collective-permute-start(bf16[2,208,128]{2,1,0:T(8,128)(2,1)S(1)} %pad_maximum_fusion.4), channel_id=1, source_target_pairs={{0,2},{1,3},{2,0},{3,1},{4,6},{5,7},{6,4},{7,5},{8,10},{9,11},{10,... | collective-permute-start | bytes 319496 | tf_op jit(solution)/shard_map/ppermute | solution.py:388
  34.3 7.2 %collective-permute-start.10 = (bf16[160,200]{1,0:T(8,128)(2,1)S(1)}, bf16[160,200]{1,0:T(8,128)(2,1)S(1)}, u32[]{:S(2)}, u32[]{:S(2)}) collective-permute-start(bf16[160,200]{1,0:T(8,128)(2,1)S(1)} %pad_maximum_fusion.6), channel_id=1, source_target_pairs={{0,8},{1,9},{2,10},{3,11},{4,12},{5,13},{6,14},{7,15},{8,0},{9,1},... | collective-permute-start | bytes 192008 | tf_op jit(solution)/shard_map/ppermute | solution.py:388
  35.9 5.6 %collective-permute-start.11 = (bf16[32,200]{1,0:T(8,128)(2,1)S(1)}, bf16[32,200]{1,0:T(8,128)(2,1)S(1)}, u32[]{:S(2)}, u32[]{:S(2)}) collective-permute-start(bf16[32,200]{1,0:T(8,128)(2,1)S(1)} %get-tuple-element.168), channel_id=1, source_target_pairs={{0,12},{1,13},{2,14},{3,15},{4,8},{5,9},{6,10},{7,11},{8,4},{9,5},... | collective-permute-start | bytes 38408 | tf_op jit(solution)/shard_map/ppermute | solution.py:388
  38.0 12.6 %collective-permute-start.16 = (bf16[4,208,128]{2,1,0:T(8,128)(2,1)S(1)}, bf16[4,208,128]{2,1,0:T(8,128)(2,1)S(1)}, u32[]{:S(2)}, u32[]{:S(2)}) collective-permute-start(bf16[4,208,128]{2,1,0:T(8,128)(2,1)S(1)} %pad_maximum_fusion.refs_0_), channel_id=1, source_target_pairs={{0,8},{1,9},{2,10},{3,11},{4,12},{5,13},{6,14},{7,15},{8,0},{9,1},... | collective-permute-start | bytes 638984 | tf_op jit(solution)/shard_map/ppermute | solution.py:388
  42.7 7.2 %collective-permute-start.12 = (bf16[160,200]{1,0:T(8,128)(2,1)S(1)}, bf16[160,200]{1,0:T(8,128)(2,1)S(1)}, u32[]{:S(2)}, u32[]{:S(2)}) collective-permute-start(bf16[160,200]{1,0:T(8,128)(2,1)S(1)} %get-tuple-element.114), channel_id=1, source_target_pairs={{0,16},{1,17},{2,18},{3,19},{4,20},{5,21},{6,22},{7,23},{8,24},{9,... | collective-permute-start | bytes 192008 | tf_op jit(solution)/shard_map/ppermute | solution.py:388
  44.2 5.6 %collective-permute-start.13 = (bf16[32,200]{1,0:T(8,128)(2,1)S(1)}, bf16[32,200]{1,0:T(8,128)(2,1)S(1)}, u32[]{:S(2)}, u32[]{:S(2)}) collective-permute-start(bf16[32,200]{1,0:T(8,128)(2,1)S(1)} %slice.67), channel_id=1, source_target_pairs={{0,20},{1,21},{2,22},{3,23},{4,16},{5,17},{6,18},{7,19},{8,28},{9,... | collective-permute-start | bytes 38408 | tf_op jit(solution)/shard_map/ppermute | solution.py:388
  46.3 7.9 %collective-permute-start.17 = (bf16[4,208,128]{2,1,0:T(8,128)(2,1)S(1)}, bf16[4,208,128]{2,1,0:T(8,128)(2,1)S(1)}, u32[]{:S(2)}, u32[]{:S(2)}) collective-permute-start(bf16[4,208,128]{2,1,0:T(8,128)(2,1)S(1)} %pad_maximum_fusion.refs_0_), channel_id=1, source_target_pairs={{0,16},{1,17},{2,18},{3,19},{4,20},{5,21},{6,22},{7,23},{8,24},{9,... | collective-permute-start | bytes 638984 | tf_op jit(solution)/shard_map/ppermute | solution.py:388
  49.9 4.0 %collective-permute-start.14 = (bf16[64,200]{1,0:T(8,128)(2,1)S(1)}, bf16[64,200]{1,0:T(8,128)(2,1)S(1)}, u32[]{:S(2)}, u32[]{:S(2)}) collective-permute-start(bf16[64,200]{1,0:T(8,128)(2,1)S(1)} %pad_maximum_fusion.11), channel_id=1, source_target_pairs={{0,2},{1,3},{2,0},{3,1},{4,6},{5,7},{6,4},{7,5},{8,10},{9,11},{10,... | collective-permute-start | bytes 76808 | tf_op jit(solution)/shard_map/ppermute | solution.py:388
  50.7 5.8 %collective-permute-start.18 = (bf16[4,208,128]{2,1,0:T(8,128)(2,1)S(1)}, bf16[4,208,128]{2,1,0:T(8,128)(2,1)S(1)}, u32[]{:S(2)}, u32[]{:S(2)}) collective-permute-start(bf16[4,208,128]{2,1,0:T(8,128)(2,1)S(1)} %collective-permute-done.16.refs_1_), channel_id=1, source_target_pairs={{0,16},{1,17},{2,18},{3,19},{4,20},{5,21},{6,22},{7,23},{8,24},{9,... | collective-permute-start | bytes 638984 | tf_op jit(solution)/shard_map/ppermute | solution.py:388
  57.9 1.3 %collective-permute-start.20 = (bf16[128,200]{1,0:T(8,128)(2,1)S(1)}, bf16[128,200]{1,0:T(8,128)(2,1)S(1)}, u32[]{:S(2)}, u32[]{:S(2)}) collective-permute-start(bf16[128,200]{1,0:T(8,128)(2,1)S(1)} %pad_maximum_fusion.9), channel_id=1, source_target_pairs={{0,1},{1,0},{2,3},{3,2},{4,5},{5,4},{6,7},{7,6},{8,9},{9,8},{10,11... | collective-permute-start | bytes 153608 | tf_op jit(solution)/shard_map/ppermute | solution.py:388
  58.0 1.4 %collective-permute-start.19 = (f32[208,128]{1,0:T(8,128)S(1)}, f32[208,128]{1,0:T(8,128)S(1)}, u32[]{:S(2)}, u32[]{:S(2)}) collective-permute-start(f32[208,128]{1,0:T(8,128)S(1)} %get-tuple-element.122), channel_id=1, source_target_pairs={{0,1},{1,0},{2,3},{3,2},{4,5},{5,4},{6,7},{7,6},{8,9},{9,8},{10,11... | collective-permute-start | bytes 319496 | tf_op jit(solution)/shard_map/ppermute | solution.py:388
  62.8 3.5 %collective-permute-start.21 = (f32[128,200]{1,0:T(8,128)S(1)}, f32[128,200]{1,0:T(8,128)S(1)}, u32[]{:S(2)}, u32[]{:S(2)}) collective-permute-start(f32[128,200]{1,0:T(8,128)S(1)} %slice.70), channel_id=1, source_target_pairs={{0,1},{1,0},{2,3},{3,2},{4,5},{5,4},{6,7},{7,6},{8,9},{9,8},{10,11... | collective-permute-start | bytes 307208 | tf_op jit(solution)/shard_map/ppermute | solution.py:388
  66.3 7.0 %collective-permute-start.22 = (bf16[1,208,128]{2,1,0:T(8,128)(2,1)S(1)}, bf16[1,208,128]{2,1,0:T(8,128)(2,1)S(1)}, u32[]{:S(2)}, u32[]{:S(2)}) collective-permute-start(bf16[1,208,128]{2,1,0:T(8,128)(2,1)S(1)} %bitcast.16), channel_id=1, source_target_pairs={{0,4},{1,5},{2,6},{3,7},{4,0},{5,1},{6,2},{7,3},{8,12},{9,13},{10,... | collective-permute-start | bytes 159752 | tf_op jit(solution)/shard_map/ppermute | solution.py:388
  68.8 4.5 %collective-permute-start.23 = (f32[64,200]{1,0:T(8,128)S(1)}, f32[64,200]{1,0:T(8,128)S(1)}, u32[]{:S(2)}, u32[]{:S(2)}) collective-permute-start(f32[64,200]{1,0:T(8,128)S(1)} %slice.81), channel_id=1, source_target_pairs={{0,2},{1,3},{2,0},{3,1},{4,6},{5,7},{6,4},{7,5},{8,10},{9,11},{10,... | collective-permute-start | bytes 153608 | tf_op jit(solution)/shard_map/ppermute | solution.py:388
  73.3 4.8 %collective-permute-start.24 = (bf16[2,208,128]{2,1,0:T(8,128)(2,1)S(1)}, bf16[2,208,128]{2,1,0:T(8,128)(2,1)S(1)}, u32[]{:S(2)}, u32[]{:S(2)}) collective-permute-start(bf16[2,208,128]{2,1,0:T(8,128)(2,1)S(1)} %pad_maximum_fusion.5), channel_id=1, source_target_pairs={{0,2},{1,3},{2,0},{3,1},{4,6},{5,7},{6,4},{7,5},{8,10},{9,11},{10,... | collective-permute-start | bytes 319496 | tf_op jit(solution)/shard_map/ppermute | solution.py:388
  78.1 8.3 %collective-permute-start.25 = (bf16[4,208,128]{2,1,0:T(8,128)(2,1)S(1)}, bf16[4,208,128]{2,1,0:T(8,128)(2,1)S(1)}, u32[]{:S(2)}, u32[]{:S(2)}) collective-permute-start(bf16[4,208,128]{2,1,0:T(8,128)(2,1)S(1)} %pad_maximum_fusion.1.refs_0_), channel_id=1, source_target_pairs={{0,8},{1,9},{2,10},{3,11},{4,12},{5,13},{6,14},{7,15},{8,0},{9,1},... | collective-permute-start | bytes 638984 | tf_op jit(solution)/shard_map/ppermute | solution.py:388
  78.6 7.8 %collective-permute-start.26 = (bf16[4,208,128]{2,1,0:T(8,128)(2,1)S(1)}, bf16[4,208,128]{2,1,0:T(8,128)(2,1)S(1)}, u32[]{:S(2)}, u32[]{:S(2)}) collective-permute-start(bf16[4,208,128]{2,1,0:T(8,128)(2,1)S(1)} %pad_maximum_fusion.1.refs_0_), channel_id=1, source_target_pairs={{0,16},{1,17},{2,18},{3,19},{4,20},{5,21},{6,22},{7,23},{8,24},{9,... | collective-permute-start | bytes 638984 | tf_op jit(solution)/shard_map/ppermute | solution.py:388
  80.0 6.3 %collective-permute-start.27 = (bf16[160,200]{1,0:T(8,128)(2,1)S(1)}, bf16[160,200]{1,0:T(8,128)(2,1)S(1)}, u32[]{:S(2)}, u32[]{:S(2)}) collective-permute-start(bf16[160,200]{1,0:T(8,128)(2,1)S(1)} %pad_maximum_fusion.7), channel_id=1, source_target_pairs={{0,16},{1,17},{2,18},{3,19},{4,20},{5,21},{6,22},{7,23},{8,24},{9,... | collective-permute-start | bytes 192008 | tf_op jit(solution)/shard_map/ppermute | solution.py:388
  80.7 5.6 %collective-permute-start.28 = (bf16[32,200]{1,0:T(8,128)(2,1)S(1)}, bf16[32,200]{1,0:T(8,128)(2,1)S(1)}, u32[]{:S(2)}, u32[]{:S(2)}) collective-permute-start(bf16[32,200]{1,0:T(8,128)(2,1)S(1)} %get-tuple-element.166), channel_id=1, source_target_pairs={{0,20},{1,21},{2,22},{3,23},{4,16},{5,17},{6,18},{7,19},{8,28},{9,... | collective-permute-start | bytes 38408 | tf_op jit(solution)/shard_map/ppermute | solution.py:388
  86.4 5.9 %collective-permute-start.29 = (bf16[4,208,128]{2,1,0:T(8,128)(2,1)S(1)}, bf16[4,208,128]{2,1,0:T(8,128)(2,1)S(1)}, u32[]{:S(2)}, u32[]{:S(2)}) collective-permute-start(bf16[4,208,128]{2,1,0:T(8,128)(2,1)S(1)} %collective-permute-done.25.refs_1_), channel_id=1, source_target_pairs={{0,16},{1,17},{2,18},{3,19},{4,20},{5,21},{6,22},{7,23},{8,24},{9,... | collective-permute-start | bytes 638984 | tf_op jit(solution)/shard_map/ppermute | solution.py:388
  92.3 2.8 %collective-permute-start.30 = (f32[200,1408]{1,0:T(8,128)S(1)}, f32[200,1408]{1,0:T(8,128)S(1)}, u32[]{:S(2)}, u32[]{:S(2)}) collective-permute-start(f32[200,1408]{1,0:T(8,128)S(1)} %late_sums.2.refs_0_), channel_id=1, source_target_pairs={{0,1},{1,0},{2,3},{3,2},{4,5},{5,4},{6,7},{7,6},{8,9},{9,8},{10,11... | collective-permute-start | bytes 3379208 | tf_op jit(solution)/shard_map/ppermute | solution.py:388
  93.7 3.0 %collective-permute-start.31 = (f32[200,1408]{1,0:T(8,128)S(1)}, f32[200,1408]{1,0:T(8,128)S(1)}, u32[]{:S(2)}, u32[]{:S(2)}) collective-permute-start(f32[200,1408]{1,0:T(8,128)S(1)} %late_sums.3.refs_2_), channel_id=1, source_target_pairs={{0,1},{1,0},{2,3},{3,2},{4,5},{5,4},{6,7},{7,6},{8,9},{9,8},{10,11... | collective-permute-start | bytes 3379208 | tf_op jit(solution)/shard_map/ppermute | solution.py:388
  (16 other events, 85.1 us)

commit v7 on v6

--- a/solution.py
+++ b/solution.py
@@ -588,8 +588,6 @@
         one, other = plan.far[-2:]
         across = send(packs, one)
         along = send(packs, other)
-        if last:
-            across, along, to_owner, to_side = together(across, along, to_owner, to_side)
         out_shape = [shaped(ent.shape), shaped(ent_state.shape)]
         outs = call(
             functools.partial(entity_kernel, r, negatives),

time: 98.6 us -> 97.7 us (level)
  transfers between devices with their start and end apart: 32 -> 32, of which waited for: 18 -> 19; matrix products, arithmetic and copies ran while one was open for 0% -> 0% of each run, Pallas kernels for 25% -> 25%
where the time goes in v7:
time: 97.7 us; the launch traced here: 97.5 us
  starting transfers between devices  38.3 us (39%)
  Pallas kernels  32.4 us (33%)
  waiting for transfers between devices  25 us (26%)
  between operations  1.11 us (1%)
    ppermute x32, starting transfers between devices, send(): return lax.ppermute(block, BOTH, self.route(mask))  38.3 us
    pallas_call x17, Pallas kernels, call(): pl.pallas_call(kernel, out_shape=[pltpu.VMEM(out.shape, out.dtype) if ind...  32.4 us
    ppermute x32, waiting for transfers between devices, send(): return lax.ppermute(block, BOTH, self.route(mask))  25 us
  transfers between devices with their start and end apart: 32, of which 19 were waited for; matrix products, arithmetic and copies ran while one was open for 0% of the time, Pallas kernels for 25%

profile of v7, /device:TPU:0, one launch (start us, length us, event | category | flops | bytes accessed | tf_op | source)
XLA Modules:
  0.0 97.5 jit_solution(17492782953589826058)
XLA Ops:
  1.5 3.0 %collective-permute-start = (s32[2,128]{1,0:T(2,128)S(1)}, s32[2,128]{1,0:T(2,128)S(1)}, u32[]{:S(2)}, u32[]{:S(2)}) collective-permute-start(s32[2,128]{1,0:T(2,128)S(1)} %get-tuple-element.81), channel_id=1, source_target_pairs={{0,8},{1,9},{2,10},{3,11},{4,12},{5,13},{6,14},{7,15},{8,0},{9,1},... | collective-permute-start | bytes 3080 | tf_op jit(solution)/shard_map/ppermute | solution.py:388
  6.5 2.1 %collective-permute-start.1 = (bf16[160,200]{1,0:T(8,128)(2,1)S(1)}, bf16[160,200]{1,0:T(8,128)(2,1)S(1)}, u32[]{:S(2)}, u32[]{:S(2)}) collective-permute-start(bf16[160,200]{1,0:T(8,128)(2,1)S(1)} %answer.1), channel_id=1, source_target_pairs={{0,8},{1,9},{2,10},{3,11},{4,12},{5,13},{6,14},{7,15},{8,0},{9,1},... | collective-permute-start | bytes 192008 | tf_op jit(solution)/shard_map/ppermute | solution.py:388
  8.5 2.6 %collective-permute-start.2 = (bf16[32,200]{1,0:T(8,128)(2,1)S(1)}, bf16[32,200]{1,0:T(8,128)(2,1)S(1)}, u32[]{:S(2)}, u32[]{:S(2)}) collective-permute-start(bf16[32,200]{1,0:T(8,128)(2,1)S(1)} %slice.76), channel_id=1, source_target_pairs={{0,12},{1,13},{2,14},{3,15},{4,8},{5,9},{6,10},{7,11},{8,4},{9,5},... | collective-permute-start | bytes 38408 | tf_op jit(solution)/shard_map/ppermute | solution.py:388
  11.1 6.7 %first_forward.1 = (f32[128,200]{1,0:T(8,128)S(1)}, f32[9,128,1152]{2,1,0:T(8,128)S(1)}, bf16[9,1152,200]{2,1,0:T(8,128)(2,1)S(1)}, bf16[80,1152]{1,0:T(8,128)(2,1)S(1)}, bf16[1152,128]{1,0:T(8,128)(2,1)S(1)}) custom-call(bf16[200,10368]{1,0:T(8,128)(2,1)} %bitcast.30, f32[9,1152]{1,0:T(8,128)S(1)} %tile.18.taps_ref, s32[2,128]{1,0:T(2,128)S(1)} %copy-done.5, ...), custom_call_target="tpu_custom_call" | custom-call | flops 17999998976 | bytes 54000000 | tf_op jit(solution)/shard_map/first_forward/pallas_call | solution.py:50
  17.9 1.6 %collective-permute-start.3 = (bf16[64,200]{1,0:T(8,128)(2,1)S(1)}, bf16[64,200]{1,0:T(8,128)(2,1)S(1)}, u32[]{:S(2)}, u32[]{:S(2)}) collective-permute-start(bf16[64,200]{1,0:T(8,128)(2,1)S(1)} %pad_maximum_fusion.10), channel_id=1, source_target_pairs={{0,2},{1,3},{2,0},{3,1},{4,6},{5,7},{6,4},{7,5},{8,10},{9,11},{10,... | collective-permute-start | bytes 76808 | tf_op jit(solution)/shard_map/ppermute | solution.py:388
  19.5 2.3 %collective-permute-done.3 = bf16[64,200]{1,0:T(8,128)(2,1)S(1)} collective-permute-done((bf16[64,200]{1,0:T(8,128)(2,1)S(1)}, bf16[64,200]{1,0:T(8,128)(2,1)S(1)}, u32[]{:S(2)}, u32[]{:S(2)}) %collective-permute-start.3) | collective-permute-done | bytes 25632 | tf_op jit(solution)/shard_map/ppermute | solution.py:388
  24.0 3.0 %backward.2 = (bf16[208,128]{1,0:T(8,128)(2,1)S(1)}, f32[200,128]{1,0:T(8,128)S(1)}, bf16[9,1152,200]{2,1,0:T(8,128)(2,1)S(1)}) custom-call(bf16[9,1152,200]{2,1,0:T(8,128)(2,1)S(1)} %get-tuple-element.86.fc_ref, s32[2,128]{1,0:T(2,128)S(1)} %copy-done.4, bf16[128,200]{1,0:T(8,128)(2,1)S(1)} %get-tuple-element.96.grad_ref, ...), custom_call_target="tpu_custom_call", output_to_operand_aliasing={{2}: (0, {})} | custom-call | flops 8999999488 | bytes 27000000 | tf_op jit(solution)/shard_map/backward/pallas_call | solution.py:50
  27.1 1.9 %collective-permute-start.8 = (f32[64,200]{1,0:T(8,128)S(1)}, f32[64,200]{1,0:T(8,128)S(1)}, u32[]{:S(2)}, u32[]{:S(2)}) collective-permute-start(f32[64,200]{1,0:T(8,128)S(1)} %slice.77), channel_id=1, source_target_pairs={{0,2},{1,3},{2,0},{3,1},{4,6},{5,7},{6,4},{7,5},{8,10},{9,11},{10,... | collective-permute-start | bytes 153608 | tf_op jit(solution)/shard_map/ppermute | solution.py:388
  29.1 1.5 %collective-permute-start.9 = (s32[2,128]{1,0:T(2,128)S(1)}, s32[2,128]{1,0:T(2,128)S(1)}, u32[]{:S(2)}, u32[]{:S(2)}) collective-permute-start(s32[2,128]{1,0:T(2,128)S(1)} %get-tuple-element.104), channel_id=1, source_target_pairs={{0,16},{1,17},{2,18},{3,19},{4,20},{5,21},{6,22},{7,23},{8,24},{9,... | collective-permute-start | bytes 3080 | tf_op jit(solution)/shard_map/ppermute | solution.py:388
  30.6 2.0 %collective-permute-done.9.next_ref.asked_ref = s32[2,128]{1,0:T(2,128)S(1)} collective-permute-done((s32[2,128]{1,0:T(2,128)S(1)}, s32[2,128]{1,0:T(2,128)S(1)}, u32[]{:S(2)}, u32[]{:S(2)}) %collective-permute-start.9) | collective-permute-done | bytes 1056 | tf_op jit(solution)/shard_map/ppermute | solution.py:388
  32.9 1.4 %collective-permute-start.15 = (bf16[2,208,128]{2,1,0:T(8,128)(2,1)S(1)}, bf16[2,208,128]{2,1,0:T(8,128)(2,1)S(1)}, u32[]{:S(2)}, u32[]{:S(2)}) collective-permute-start(bf16[2,208,128]{2,1,0:T(8,128)(2,1)S(1)} %pad_maximum_fusion.4), channel_id=1, source_target_pairs={{0,2},{1,3},{2,0},{3,1},{4,6},{5,7},{6,4},{7,5},{8,10},{9,11},{10,... | collective-permute-start | bytes 319496 | tf_op jit(solution)/shard_map/ppermute | solution.py:388
  34.3 1.6 %collective-permute-start.10 = (bf16[160,200]{1,0:T(8,128)(2,1)S(1)}, bf16[160,200]{1,0:T(8,128)(2,1)S(1)}, u32[]{:S(2)}, u32[]{:S(2)}) collective-permute-start(bf16[160,200]{1,0:T(8,128)(2,1)S(1)} %pad_maximum_fusion.6), channel_id=1, source_target_pairs={{0,8},{1,9},{2,10},{3,11},{4,12},{5,13},{6,14},{7,15},{8,0},{9,1},... | collective-permute-start | bytes 192008 | tf_op jit(solution)/shard_map/ppermute | solution.py:388
  35.9 2.1 %collective-permute-start.11 = (bf16[32,200]{1,0:T(8,128)(2,1)S(1)}, bf16[32,200]{1,0:T(8,128)(2,1)S(1)}, u32[]{:S(2)}, u32[]{:S(2)}) collective-permute-start(bf16[32,200]{1,0:T(8,128)(2,1)S(1)} %get-tuple-element.160), channel_id=1, source_target_pairs={{0,12},{1,13},{2,14},{3,15},{4,8},{5,9},{6,10},{7,11},{8,4},{9,5},... | collective-permute-start | bytes 38408 | tf_op jit(solution)/shard_map/ppermute | solution.py:388
  38.0 1.6 %collective-permute-start.16 = (bf16[4,208,128]{2,1,0:T(8,128)(2,1)S(1)}, bf16[4,208,128]{2,1,0:T(8,128)(2,1)S(1)}, u32[]{:S(2)}, u32[]{:S(2)}) collective-permute-start(bf16[4,208,128]{2,1,0:T(8,128)(2,1)S(1)} %pad_maximum_fusion.refs_0_), channel_id=1, source_target_pairs={{0,8},{1,9},{2,10},{3,11},{4,12},{5,13},{6,14},{7,15},{8,0},{9,1},... | collective-permute-start | bytes 638984 | tf_op jit(solution)/shard_map/ppermute | solution.py:388
  39.6 1.9 %collective-permute-done.11.other_ref = bf16[32,200]{1,0:T(8,128)(2,1)S(1)} collective-permute-done((bf16[32,200]{1,0:T(8,128)(2,1)S(1)}, bf16[32,200]{1,0:T(8,128)(2,1)S(1)}, u32[]{:S(2)}, u32[]{:S(2)}) %collective-permute-start.11) | collective-permute-done | bytes 12832 | tf_op jit(solution)/shard_map/ppermute | solution.py:388
  42.7 1.6 %collective-permute-start.12 = (bf16[160,200]{1,0:T(8,128)(2,1)S(1)}, bf16[160,200]{1,0:T(8,128)(2,1)S(1)}, u32[]{:S(2)}, u32[]{:S(2)}) collective-permute-start(bf16[160,200]{1,0:T(8,128)(2,1)S(1)} %get-tuple-element.110), channel_id=1, source_target_pairs={{0,16},{1,17},{2,18},{3,19},{4,20},{5,21},{6,22},{7,23},{8,24},{9,... | collective-permute-start | bytes 192008 | tf_op jit(solution)/shard_map/ppermute | solution.py:388
  44.2 2.0 %collective-permute-start.13 = (bf16[32,200]{1,0:T(8,128)(2,1)S(1)}, bf16[32,200]{1,0:T(8,128)(2,1)S(1)}, u32[]{:S(2)}, u32[]{:S(2)}) collective-permute-start(bf16[32,200]{1,0:T(8,128)(2,1)S(1)} %slice.67), channel_id=1, source_target_pairs={{0,20},{1,21},{2,22},{3,23},{4,16},{5,17},{6,18},{7,19},{8,28},{9,... | collective-permute-start | bytes 38408 | tf_op jit(solution)/shard_map/ppermute | solution.py:388
  46.3 1.6 %collective-permute-start.17 = (bf16[4,208,128]{2,1,0:T(8,128)(2,1)S(1)}, bf16[4,208,128]{2,1,0:T(8,128)(2,1)S(1)}, u32[]{:S(2)}, u32[]{:S(2)}) collective-permute-start(bf16[4,208,128]{2,1,0:T(8,128)(2,1)S(1)} %pad_maximum_fusion.refs_0_), channel_id=1, source_target_pairs={{0,16},{1,17},{2,18},{3,19},{4,20},{5,21},{6,22},{7,23},{8,24},{9,... | collective-permute-start | bytes 638984 | tf_op jit(solution)/shard_map/ppermute | solution.py:388
  47.8 2.0 %collective-permute-done.13 = bf16[32,200]{1,0:T(8,128)(2,1)S(1)} collective-permute-done((bf16[32,200]{1,0:T(8,128)(2,1)S(1)}, bf16[32,200]{1,0:T(8,128)(2,1)S(1)}, u32[]{:S(2)}, u32[]{:S(2)}) %collective-permute-start.13) | collective-permute-done | bytes 12832 | tf_op jit(solution)/shard_map/ppermute | solution.py:388
  51.2 2.7 %collective-permute-done.14 = bf16[64,200]{1,0:T(8,128)(2,1)S(1)} collective-permute-done((bf16[64,200]{1,0:T(8,128)(2,1)S(1)}, bf16[64,200]{1,0:T(8,128)(2,1)S(1)}, u32[]{:S(2)}, u32[]{:S(2)}) %collective-permute-start.14) | collective-permute-done | bytes 25632 | tf_op jit(solution)/shard_map/ppermute | solution.py:388
  54.2 2.3 %collective-permute-done.18.refs_3_.refs_0_ = bf16[4,208,128]{2,1,0:T(8,128)(2,1)S(1)} collective-permute-done((bf16[4,208,128]{2,1,0:T(8,128)(2,1)S(1)}, bf16[4,208,128]{2,1,0:T(8,128)(2,1)S(1)}, u32[]{:S(2)}, u32[]{:S(2)}) %collective-permute-start.18) | collective-permute-done | bytes 213024 | tf_op jit(solution)/shard_map/ppermute | solution.py:388
  59.4 2.9 %forward.1 = (f32[128,200]{1,0:T(8,128)S(1)}, f32[9,128,1152]{2,1,0:T(8,128)S(1)}, bf16[9,1152,200]{2,1,0:T(8,128)(2,1)S(1)}, f32[200,1024]{1,0:T(8,128)S(1)}) custom-call(bf16[9,1152,200]{2,1,0:T(8,128)(2,1)S(1)} %bitcast.28, s32[2,128]{1,0:T(2,128)S(1)} %copy-done.5, ...), custom_call_target="tpu_custom_call", output_to_operand_aliasing={{2}: (0, {}), {3}: (2, {})} | custom-call | flops 7500000256 | bytes 22500000 | tf_op jit(solution)/shard_map/forward/pallas_call | solution.py:50
  63.3 3.0 %backward.3 = (bf16[208,128]{1,0:T(8,128)(2,1)S(1)}, f32[200,128]{1,0:T(8,128)S(1)}, bf16[9,1152,200]{2,1,0:T(8,128)(2,1)S(1)}) custom-call(bf16[9,1152,200]{2,1,0:T(8,128)(2,1)S(1)} %get-tuple-element.122.fc_ref, s32[2,128]{1,0:T(2,128)S(1)} %copy-done.4, bf16[128,200]{1,0:T(8,128)(2,1)S(1)} %get-tuple-element.125.grad_ref, ...), custom_call_target="tpu_custom_call", output_to_operand_aliasing={{2}: (0, {})} | custom-call | flops 8999999488 | bytes 27000000 | tf_op jit(solution)/shard_map/backward/pallas_call | solution.py:50
  66.3 2.5 %collective-permute-start.22 = (bf16[1,208,128]{2,1,0:T(8,128)(2,1)S(1)}, bf16[1,208,128]{2,1,0:T(8,128)(2,1)S(1)}, u32[]{:S(2)}, u32[]{:S(2)}) collective-permute-start(bf16[1,208,128]{2,1,0:T(8,128)(2,1)S(1)} %bitcast.13), channel_id=1, source_target_pairs={{0,4},{1,5},{2,6},{3,7},{4,0},{5,1},{6,2},{7,3},{8,12},{9,13},{10,... | collective-permute-start | bytes 159752 | tf_op jit(solution)/shard_map/ppermute | solution.py:388
  69.9 2.6 %early_sums.2 = (f32[200,1408]{1,0:T(8,128)S(1)}, f32[200,1408]{1,0:T(8,128)S(1)}) custom-call(s32[4]{0:T(128)S(1)} %iota_xor_fusion.place_ref, bf16[4,208,128]{2,1,0:T(8,128)(2,1)S(1)} %pad_maximum_fusion.refs_0_, bf16[4,208,128]{2,1,0:T(8,128)(2,1)S(1)} %collective-permute-done.16.refs_1_, bf16[4,208,128]{2,1,0:T(8,128)(2,1)S(1)} %collective-permute-done.17.refs_2_), custom_call_target="tpu_custom_call" | custom-call | flops 8999999488 | bytes 27000000 | tf_op jit(solution)/shard_map/early_sums/pallas_call | solution.py:50
  75.0 2.6 %collective-permute-start.29 = (bf16[32,200]{1,0:T(8,128)(2,1)S(1)}, bf16[32,200]{1,0:T(8,128)(2,1)S(1)}, u32[]{:S(2)}, u32[]{:S(2)}) collective-permute-start(bf16[32,200]{1,0:T(8,128)(2,1)S(1)} %get-tuple-element.158), channel_id=1, source_target_pairs={{0,20},{1,21},{2,22},{3,23},{4,16},{5,17},{6,18},{7,19},{8,28},{9,... | collective-permute-start | bytes 38408 | tf_op jit(solution)/shard_map/ppermute | solution.py:388
  80.6 1.7 %entity_update.3 = (f32[200,1024]{1,0:T(8,128)}, f32[1,1024]{1,0:T(1,128)}) custom-call(s32[2,128]{1,0:T(2,128)S(1)} %copy-done.5, s32[2,128]{1,0:T(2,128)S(1)} %collective-permute-done.9.next_ref.asked_ref, s32[2,128]{1,0:T(2,128)S(1)} %collective-permute-done.9.next_ref.asked_ref, f32[200,1024]{1,0:T(8,128)S(1)} %get-tuple-element.140.ent_ref, ...), custom_call_target="tpu_custom_call" | custom-call | flops 4499999744 | bytes 13500000 | tf_op jit(solution)/shard_map/entity_update/pallas_call | solution.py:50
  82.3 2.8 %collective-permute-done.25.refs_1_ = bf16[4,208,128]{2,1,0:T(8,128)(2,1)S(1)} collective-permute-done((bf16[4,208,128]{2,1,0:T(8,128)(2,1)S(1)}, bf16[4,208,128]{2,1,0:T(8,128)(2,1)S(1)}, u32[]{:S(2)}, u32[]{:S(2)}) %collective-permute-start.25) | collective-permute-done | bytes 213024 | tf_op jit(solution)/shard_map/ppermute | solution.py:388
  86.2 2.6 %early_sums.3 = (f32[200,1408]{1,0:T(8,128)S(1)}, f32[200,1408]{1,0:T(8,128)S(1)}) custom-call(s32[4]{0:T(128)S(1)} %iota_xor_fusion.place_ref, bf16[4,208,128]{2,1,0:T(8,128)(2,1)S(1)} %pad_maximum_fusion.1.refs_0_, bf16[4,208,128]{2,1,0:T(8,128)(2,1)S(1)} %collective-permute-done.25.refs_1_, bf16[4,208,128]{2,1,0:T(8,128)(2,1)S(1)} %collective-permute-done.26.refs_2_), custom_call_target="tpu_custom_call" | custom-call | flops 8999999488 | bytes 27000000 | tf_op jit(solution)/shard_map/early_sums/pallas_call | solution.py:50
  88.8 2.6 %collective-permute-done.27.refs_0_ = bf16[4,208,128]{2,1,0:T(8,128)(2,1)S(1)} collective-permute-done((bf16[4,208,128]{2,1,0:T(8,128)(2,1)S(1)}, bf16[4,208,128]{2,1,0:T(8,128)(2,1)S(1)}, u32[]{:S(2)}, u32[]{:S(2)}) %collective-permute-start.27) | collective-permute-done | bytes 213024 | tf_op jit(solution)/shard_map/ppermute | solution.py:388
  94.1 1.6 %collective-permute-done.31.refs_3_ = f32[200,1408]{1,0:T(8,128)S(1)} collective-permute-done((f32[200,1408]{1,0:T(8,128)S(1)}, f32[200,1408]{1,0:T(8,128)S(1)}, u32[]{:S(2)}, u32[]{:S(2)}) %collective-permute-start.31) | collective-permute-done | bytes 1126432 | tf_op jit(solution)/shard_map/ppermute | solution.py:388
  95.8 1.7 %relation_update.1 = (f32[200,1387]{1,0:T(8,128)}, f32[1387]{0:T(1024)}) custom-call(f32[200,1387]{1,0:T(8,128)S(1)} %bitcast.20, f32[1,1387]{1,0:T(1,128)S(1)} %broadcast_in_dim.15.state_ref, f32[200,1408]{1,0:T(8,128)S(1)} %late_sums.2.refs_0_, f32[200,1408]{1,0:T(8,128)S(1)} %collective-permute-done.30.refs_1_, f32[200,1408]{1,0:T(8,128)S(1)} %late_sums.3.refs_2_, ...), custom_call_target="tpu_custom_call" | custom-call | flops 6000000000 | bytes 18000000 | tf_op jit(solution)/shard_map/relation_update/pallas_call | solution.py:50
  (119 shorter events, 22.2 us)
Async XLA Ops:
  1.5 4.6 %collective-permute-start = (s32[2,128]{1,0:T(2,128)S(1)}, s32[2,128]{1,0:T(2,128)S(1)}, u32[]{:S(2)}, u32[]{:S(2)}) collective-permute-start(s32[2,128]{1,0:T(2,128)S(1)} %get-tuple-element.81), channel_id=1, source_target_pairs={{0,8},{1,9},{2,10},{3,11},{4,12},{5,13},{6,14},{7,15},{8,0},{9,1},... | collective-permute-start | bytes 3080 | tf_op jit(solution)/shard_map/ppermute | solution.py:388
  6.5 11.4 %collective-permute-start.1 = (bf16[160,200]{1,0:T(8,128)(2,1)S(1)}, bf16[160,200]{1,0:T(8,128)(2,1)S(1)}, u32[]{:S(2)}, u32[]{:S(2)}) collective-permute-start(bf16[160,200]{1,0:T(8,128)(2,1)S(1)} %answer.1), channel_id=1, source_target_pairs={{0,8},{1,9},{2,10},{3,11},{4,12},{5,13},{6,14},{7,15},{8,0},{9,1},... | collective-permute-start | bytes 192008 | tf_op jit(solution)/shard_map/ppermute | solution.py:388
  8.5 9.3 %collective-permute-start.2 = (bf16[32,200]{1,0:T(8,128)(2,1)S(1)}, bf16[32,200]{1,0:T(8,128)(2,1)S(1)}, u32[]{:S(2)}, u32[]{:S(2)}) collective-permute-start(bf16[32,200]{1,0:T(8,128)(2,1)S(1)} %slice.76), channel_id=1, source_target_pairs={{0,12},{1,13},{2,14},{3,15},{4,8},{5,9},{6,10},{7,11},{8,4},{9,5},... | collective-permute-start | bytes 38408 | tf_op jit(solution)/shard_map/ppermute | solution.py:388
  17.9 4.0 %collective-permute-start.3 = (bf16[64,200]{1,0:T(8,128)(2,1)S(1)}, bf16[64,200]{1,0:T(8,128)(2,1)S(1)}, u32[]{:S(2)}, u32[]{:S(2)}) collective-permute-start(bf16[64,200]{1,0:T(8,128)(2,1)S(1)} %pad_maximum_fusion.10), channel_id=1, source_target_pairs={{0,2},{1,3},{2,0},{3,1},{4,6},{5,7},{6,4},{7,5},{8,10},{9,11},{10,... | collective-permute-start | bytes 76808 | tf_op jit(solution)/shard_map/ppermute | solution.py:388
  21.9 1.3 %collective-permute-start.4 = (bf16[128,200]{1,0:T(8,128)(2,1)S(1)}, bf16[128,200]{1,0:T(8,128)(2,1)S(1)}, u32[]{:S(2)}, u32[]{:S(2)}) collective-permute-start(bf16[128,200]{1,0:T(8,128)(2,1)S(1)} %pad_maximum_fusion.8), channel_id=1, source_target_pairs={{0,1},{1,0},{2,3},{3,2},{4,5},{5,4},{6,7},{7,6},{8,9},{9,8},{10,11... | collective-permute-start | bytes 153608 | tf_op jit(solution)/shard_map/ppermute | solution.py:388
  22.0 1.7 %collective-permute-start.5 = (s32[2,128]{1,0:T(2,128)S(1)}, s32[2,128]{1,0:T(2,128)S(1)}, u32[]{:S(2)}, u32[]{:S(2)}) collective-permute-start(s32[2,128]{1,0:T(2,128)S(1)} %copy-done.4), channel_id=1, source_target_pairs={{0,1},{1,0},{2,3},{3,2},{4,5},{5,4},{6,7},{7,6},{8,9},{9,8},{10,11... | collective-permute-start | bytes 3080 | tf_op jit(solution)/shard_map/ppermute | solution.py:388
  23.7 3.2 %collective-permute-start.6 = (f32[128,200]{1,0:T(8,128)S(1)}, f32[128,200]{1,0:T(8,128)S(1)}, u32[]{:S(2)}, u32[]{:S(2)}) collective-permute-start(f32[128,200]{1,0:T(8,128)S(1)} %slice.61), channel_id=1, source_target_pairs={{0,1},{1,0},{2,3},{3,2},{4,5},{5,4},{6,7},{7,6},{8,9},{9,8},{10,11... | collective-permute-start | bytes 307208 | tf_op jit(solution)/shard_map/ppermute | solution.py:388
  27.0 5.8 %collective-permute-start.7 = (bf16[1,208,128]{2,1,0:T(8,128)(2,1)S(1)}, bf16[1,208,128]{2,1,0:T(8,128)(2,1)S(1)}, u32[]{:S(2)}, u32[]{:S(2)}) collective-permute-start(bf16[1,208,128]{2,1,0:T(8,128)(2,1)S(1)} %bitcast.16), channel_id=1, source_target_pairs={{0,4},{1,5},{2,6},{3,7},{4,0},{5,1},{6,2},{7,3},{8,12},{9,13},{10,... | collective-permute-start | bytes 159752 | tf_op jit(solution)/shard_map/ppermute | solution.py:388
  27.1 5.5 %collective-permute-start.8 = (f32[64,200]{1,0:T(8,128)S(1)}, f32[64,200]{1,0:T(8,128)S(1)}, u32[]{:S(2)}, u32[]{:S(2)}) collective-permute-start(f32[64,200]{1,0:T(8,128)S(1)} %slice.77), channel_id=1, source_target_pairs={{0,2},{1,3},{2,0},{3,1},{4,6},{5,7},{6,4},{7,5},{8,10},{9,11},{10,... | collective-permute-start | bytes 153608 | tf_op jit(solution)/shard_map/ppermute | solution.py:388
  29.1 3.6 %collective-permute-start.9 = (s32[2,128]{1,0:T(2,128)S(1)}, s32[2,128]{1,0:T(2,128)S(1)}, u32[]{:S(2)}, u32[]{:S(2)}) collective-permute-start(s32[2,128]{1,0:T(2,128)S(1)} %get-tuple-element.104), channel_id=1, source_target_pairs={{0,16},{1,17},{2,18},{3,19},{4,20},{5,21},{6,22},{7,23},{8,24},{9,... | collective-permute-start | bytes 3080 | tf_op jit(solution)/shard_map/ppermute | solution.py:388
  32.9 5.1 %collective-permute-start.15 = (bf16[2,208,128]{2,1,0:T(8,128)(2,1)S(1)}, bf16[2,208,128]{2,1,0:T(8,128)(2,1)S(1)}, u32[]{:S(2)}, u32[]{:S(2)}) collective-permute-start(bf16[2,208,128]{2,1,0:T(8,128)(2,1)S(1)} %pad_maximum_fusion.4), channel_id=1, source_target_pairs={{0,2},{1,3},{2,0},{3,1},{4,6},{5,7},{6,4},{7,5},{8,10},{9,11},{10,... | collective-permute-start | bytes 319496 | tf_op jit(solution)/shard_map/ppermute | solution.py:388
  34.3 7.2 %collective-permute-start.10 = (bf16[160,200]{1,0:T(8,128)(2,1)S(1)}, bf16[160,200]{1,0:T(8,128)(2,1)S(1)}, u32[]{:S(2)}, u32[]{:S(2)}) collective-permute-start(bf16[160,200]{1,0:T(8,128)(2,1)S(1)} %pad_maximum_fusion.6), channel_id=1, source_target_pairs={{0,8},{1,9},{2,10},{3,11},{4,12},{5,13},{6,14},{7,15},{8,0},{9,1},... | collective-permute-start | bytes 192008 | tf_op jit(solution)/shard_map/ppermute | solution.py:388
  35.9 5.6 %collective-permute-start.11 = (bf16[32,200]{1,0:T(8,128)(2,1)S(1)}, bf16[32,200]{1,0:T(8,128)(2,1)S(1)}, u32[]{:S(2)}, u32[]{:S(2)}) collective-permute-start(bf16[32,200]{1,0:T(8,128)(2,1)S(1)} %get-tuple-element.160), channel_id=1, source_target_pairs={{0,12},{1,13},{2,14},{3,15},{4,8},{5,9},{6,10},{7,11},{8,4},{9,5},... | collective-permute-start | bytes 38408 | tf_op jit(solution)/shard_map/ppermute | solution.py:388
  38.0 12.6 %collective-permute-start.16 = (bf16[4,208,128]{2,1,0:T(8,128)(2,1)S(1)}, bf16[4,208,128]{2,1,0:T(8,128)(2,1)S(1)}, u32[]{:S(2)}, u32[]{:S(2)}) collective-permute-start(bf16[4,208,128]{2,1,0:T(8,128)(2,1)S(1)} %pad_maximum_fusion.refs_0_), channel_id=1, source_target_pairs={{0,8},{1,9},{2,10},{3,11},{4,12},{5,13},{6,14},{7,15},{8,0},{9,1},... | collective-permute-start | bytes 638984 | tf_op jit(solution)/shard_map/ppermute | solution.py:388
  42.7 7.2 %collective-permute-start.12 = (bf16[160,200]{1,0:T(8,128)(2,1)S(1)}, bf16[160,200]{1,0:T(8,128)(2,1)S(1)}, u32[]{:S(2)}, u32[]{:S(2)}) collective-permute-start(bf16[160,200]{1,0:T(8,128)(2,1)S(1)} %get-tuple-element.110), channel_id=1, source_target_pairs={{0,16},{1,17},{2,18},{3,19},{4,20},{5,21},{6,22},{7,23},{8,24},{9,... | collective-permute-start | bytes 192008 | tf_op jit(solution)/shard_map/ppermute | solution.py:388
  44.2 5.6 %collective-permute-start.13 = (bf16[32,200]{1,0:T(8,128)(2,1)S(1)}, bf16[32,200]{1,0:T(8,128)(2,1)S(1)}, u32[]{:S(2)}, u32[]{:S(2)}) collective-permute-start(bf16[32,200]{1,0:T(8,128)(2,1)S(1)} %slice.67), channel_id=1, source_target_pairs={{0,20},{1,21},{2,22},{3,23},{4,16},{5,17},{6,18},{7,19},{8,28},{9,... | collective-permute-start | bytes 38408 | tf_op jit(solution)/shard_map/ppermute | solution.py:388
  46.3 7.9 %collective-permute-start.17 = (bf16[4,208,128]{2,1,0:T(8,128)(2,1)S(1)}, bf16[4,208,128]{2,1,0:T(8,128)(2,1)S(1)}, u32[]{:S(2)}, u32[]{:S(2)}) collective-permute-start(bf16[4,208,128]{2,1,0:T(8,128)(2,1)S(1)} %pad_maximum_fusion.refs_0_), channel_id=1, source_target_pairs={{0,16},{1,17},{2,18},{3,19},{4,20},{5,21},{6,22},{7,23},{8,24},{9,... | collective-permute-start | bytes 638984 | tf_op jit(solution)/shard_map/ppermute | solution.py:388
  49.9 4.0 %collective-permute-start.14 = (bf16[64,200]{1,0:T(8,128)(2,1)S(1)}, bf16[64,200]{1,0:T(8,128)(2,1)S(1)}, u32[]{:S(2)}, u32[]{:S(2)}) collective-permute-start(bf16[64,200]{1,0:T(8,128)(2,1)S(1)} %pad_maximum_fusion.11), channel_id=1, source_target_pairs={{0,2},{1,3},{2,0},{3,1},{4,6},{5,7},{6,4},{7,5},{8,10},{9,11},{10,... | collective-permute-start | bytes 76808 | tf_op jit(solution)/shard_map/ppermute | solution.py:388
  50.7 5.8 %collective-permute-start.18 = (bf16[4,208,128]{2,1,0:T(8,128)(2,1)S(1)}, bf16[4,208,128]{2,1,0:T(8,128)(2,1)S(1)}, u32[]{:S(2)}, u32[]{:S(2)}) collective-permute-start(bf16[4,208,128]{2,1,0:T(8,128)(2,1)S(1)} %collective-permute-done.16.refs_1_), channel_id=1, source_target_pairs={{0,16},{1,17},{2,18},{3,19},{4,20},{5,21},{6,22},{7,23},{8,24},{9,... | collective-permute-start | bytes 638984 | tf_op jit(solution)/shard_map/ppermute | solution.py:388
  57.9 1.3 %collective-permute-start.20 = (bf16[128,200]{1,0:T(8,128)(2,1)S(1)}, bf16[128,200]{1,0:T(8,128)(2,1)S(1)}, u32[]{:S(2)}, u32[]{:S(2)}) collective-permute-start(bf16[128,200]{1,0:T(8,128)(2,1)S(1)} %pad_maximum_fusion.9), channel_id=1, source_target_pairs={{0,1},{1,0},{2,3},{3,2},{4,5},{5,4},{6,7},{7,6},{8,9},{9,8},{10,11... | collective-permute-start | bytes 153608 | tf_op jit(solution)/shard_map/ppermute | solution.py:388
  58.0 1.4 %collective-permute-start.19 = (f32[208,128]{1,0:T(8,128)S(1)}, f32[208,128]{1,0:T(8,128)S(1)}, u32[]{:S(2)}, u32[]{:S(2)}) collective-permute-start(f32[208,128]{1,0:T(8,128)S(1)} %get-tuple-element.118), channel_id=1, source_target_pairs={{0,1},{1,0},{2,3},{3,2},{4,5},{5,4},{6,7},{7,6},{8,9},{9,8},{10,11... | collective-permute-start | bytes 319496 | tf_op jit(solution)/shard_map/ppermute | solution.py:388
  62.8 3.5 %collective-permute-start.21 = (f32[128,200]{1,0:T(8,128)S(1)}, f32[128,200]{1,0:T(8,128)S(1)}, u32[]{:S(2)}, u32[]{:S(2)}) collective-permute-start(f32[128,200]{1,0:T(8,128)S(1)} %slice.70), channel_id=1, source_target_pairs={{0,1},{1,0},{2,3},{3,2},{4,5},{5,4},{6,7},{7,6},{8,9},{9,8},{10,11... | collective-permute-start | bytes 307208 | tf_op jit(solution)/shard_map/ppermute | solution.py:388
  66.3 7.0 %collective-permute-start.22 = (bf16[1,208,128]{2,1,0:T(8,128)(2,1)S(1)}, bf16[1,208,128]{2,1,0:T(8,128)(2,1)S(1)}, u32[]{:S(2)}, u32[]{:S(2)}) collective-permute-start(bf16[1,208,128]{2,1,0:T(8,128)(2,1)S(1)} %bitcast.13), channel_id=1, source_target_pairs={{0,4},{1,5},{2,6},{3,7},{4,0},{5,1},{6,2},{7,3},{8,12},{9,13},{10,... | collective-permute-start | bytes 159752 | tf_op jit(solution)/shard_map/ppermute | solution.py:388
  68.8 4.5 %collective-permute-start.23 = (f32[64,200]{1,0:T(8,128)S(1)}, f32[64,200]{1,0:T(8,128)S(1)}, u32[]{:S(2)}, u32[]{:S(2)}) collective-permute-start(f32[64,200]{1,0:T(8,128)S(1)} %slice.81), channel_id=1, source_target_pairs={{0,2},{1,3},{2,0},{3,1},{4,6},{5,7},{6,4},{7,5},{8,10},{9,11},{10,... | collective-permute-start | bytes 153608 | tf_op jit(solution)/shard_map/ppermute | solution.py:388
  73.3 5.7 %collective-permute-start.24 = (bf16[2,208,128]{2,1,0:T(8,128)(2,1)S(1)}, bf16[2,208,128]{2,1,0:T(8,128)(2,1)S(1)}, u32[]{:S(2)}, u32[]{:S(2)}) collective-permute-start(bf16[2,208,128]{2,1,0:T(8,128)(2,1)S(1)} %pad_maximum_fusion.5), channel_id=1, source_target_pairs={{0,2},{1,3},{2,0},{3,1},{4,6},{5,7},{6,4},{7,5},{8,10},{9,11},{10,... | collective-permute-start | bytes 319496 | tf_op jit(solution)/shard_map/ppermute | solution.py:388
  74.4 6.1 %collective-permute-start.28 = (bf16[160,200]{1,0:T(8,128)(2,1)S(1)}, bf16[160,200]{1,0:T(8,128)(2,1)S(1)}, u32[]{:S(2)}, u32[]{:S(2)}) collective-permute-start(bf16[160,200]{1,0:T(8,128)(2,1)S(1)} %pad_maximum_fusion.7), channel_id=1, source_target_pairs={{0,16},{1,17},{2,18},{3,19},{4,20},{5,21},{6,22},{7,23},{8,24},{9,... | collective-permute-start | bytes 192008 | tf_op jit(solution)/shard_map/ppermute | solution.py:388
  75.0 5.5 %collective-permute-start.29 = (bf16[32,200]{1,0:T(8,128)(2,1)S(1)}, bf16[32,200]{1,0:T(8,128)(2,1)S(1)}, u32[]{:S(2)}, u32[]{:S(2)}) collective-permute-start(bf16[32,200]{1,0:T(8,128)(2,1)S(1)} %get-tuple-element.158), channel_id=1, source_target_pairs={{0,20},{1,21},{2,22},{3,23},{4,16},{5,17},{6,18},{7,19},{8,28},{9,... | collective-permute-start | bytes 38408 | tf_op jit(solution)/shard_map/ppermute | solution.py:388
  79.0 6.1 %collective-permute-start.25 = (bf16[4,208,128]{2,1,0:T(8,128)(2,1)S(1)}, bf16[4,208,128]{2,1,0:T(8,128)(2,1)S(1)}, u32[]{:S(2)}, u32[]{:S(2)}) collective-permute-start(bf16[4,208,128]{2,1,0:T(8,128)(2,1)S(1)} %pad_maximum_fusion.1.refs_0_), channel_id=1, source_target_pairs={{0,8},{1,9},{2,10},{3,11},{4,12},{5,13},{6,14},{7,15},{8,0},{9,1},... | collective-permute-start | bytes 638984 | tf_op jit(solution)/shard_map/ppermute | solution.py:388
  79.7 5.8 %collective-permute-start.26 = (bf16[4,208,128]{2,1,0:T(8,128)(2,1)S(1)}, bf16[4,208,128]{2,1,0:T(8,128)(2,1)S(1)}, u32[]{:S(2)}, u32[]{:S(2)}) collective-permute-start(bf16[4,208,128]{2,1,0:T(8,128)(2,1)S(1)} %pad_maximum_fusion.1.refs_0_), channel_id=1, source_target_pairs={{0,16},{1,17},{2,18},{3,19},{4,20},{5,21},{6,22},{7,23},{8,24},{9,... | collective-permute-start | bytes 638984 | tf_op jit(solution)/shard_map/ppermute | solution.py:388
  85.5 5.8 %collective-permute-start.27 = (bf16[4,208,128]{2,1,0:T(8,128)(2,1)S(1)}, bf16[4,208,128]{2,1,0:T(8,128)(2,1)S(1)}, u32[]{:S(2)}, u32[]{:S(2)}) collective-permute-start(bf16[4,208,128]{2,1,0:T(8,128)(2,1)S(1)} %collective-permute-done.25.refs_1_), channel_id=1, source_target_pairs={{0,16},{1,17},{2,18},{3,19},{4,20},{5,21},{6,22},{7,23},{8,24},{9,... | collective-permute-start | bytes 638984 | tf_op jit(solution)/shard_map/ppermute | solution.py:388
  91.4 2.8 %collective-permute-start.30 = (f32[200,1408]{1,0:T(8,128)S(1)}, f32[200,1408]{1,0:T(8,128)S(1)}, u32[]{:S(2)}, u32[]{:S(2)}) collective-permute-start(f32[200,1408]{1,0:T(8,128)S(1)} %late_sums.2.refs_0_), channel_id=1, source_target_pairs={{0,1},{1,0},{2,3},{3,2},{4,5},{5,4},{6,7},{7,6},{8,9},{9,8},{10,11... | collective-permute-start | bytes 3379208 | tf_op jit(solution)/shard_map/ppermute | solution.py:388
  92.7 3.0 %collective-permute-start.31 = (f32[200,1408]{1,0:T(8,128)S(1)}, f32[200,1408]{1,0:T(8,128)S(1)}, u32[]{:S(2)}, u32[]{:S(2)}) collective-permute-start(f32[200,1408]{1,0:T(8,128)S(1)} %late_sums.3.refs_2_), channel_id=1, source_target_pairs={{0,1},{1,0},{2,3},{3,2},{4,5},{5,4},{6,7},{7,6},{8,9},{9,8},{10,11... | collective-permute-start | bytes 3379208 | tf_op jit(solution)/shard_map/ppermute | solution.py:388
  (16 other events, 85.1 us)
